TPU v7x, 32 devices: a whole 2x2x4 slice. The times are simulated.
32 devices in a mesh: dp: 8 (over z, x), tensor: 4 (over y, core).
Axes of the slice: x: 2, y: 2, z: 4, core: 2. Of those that a mesh axis runs over, the one named last changes fastest.
Arguments:
- inputs: bfloat16 [32768, 768], P(('dp', 'tensor')), may hold values from -5.6 to 5.6
- lengths: int32 [32], P('dp'), may hold values from 256 to 1024, as said below
- groups: int32 [32, 32], replicated, may hold values from 0 to 1, as said below
- qkv_weight: float32 [3, 768, 768], P(None, 'dp', 'tensor'), may hold values from -0.21875 to 0.21875
- out_weight: float32 [768, 768], P('tensor', 'dp'), may hold values from -0.21875 to 0.21875
- up_weight: float32 [768, 3072], P('dp', 'tensor'), may hold values from -0.21875 to 0.21875
- down_weight: float32 [3072, 768], P('tensor', 'dp'), may hold values from -0.109375 to 0.109375
- col_bias: float32 [4, 1152], P('tensor', 'dp'), may hold values from -0.4 to 0.4
- row_params: float32 [6, 768], P(None, 'dp'), may hold values from -0.4 to 1.4
- qkv_first: float32 [3, 768, 768], P(None, 'dp', 'tensor'), may hold values from -0.56568545 to 0.56568545
- out_first: float32 [768, 768], P('tensor', 'dp'), may hold values from -0.56568545 to 0.56568545
- up_first: float32 [768, 3072], P('dp', 'tensor'), may hold values from -0.56568545 to 0.56568545
- down_first: float32 [3072, 768], P('tensor', 'dp'), may hold values from -0.56568545 to 0.56568545
- col_first: float32 [4, 1152], P('tensor', 'dp'), may hold values from -0.56568545 to 0.56568545
- row_first: float32 [6, 768], P(None, 'dp'), may hold values from -3.6769552 to 3.6769552
- qkv_second: float32 [3, 768, 768], P(None, 'dp', 'tensor'), may hold values from 0.0128 to 0.0512
- out_second: float32 [768, 768], P('tensor', 'dp'), may hold values from 0.0128 to 0.0512
- up_second: float32 [768, 3072], P('dp', 'tensor'), may hold values from 0.0128 to 0.0512
- down_second: float32 [3072, 768], P('tensor', 'dp'), may hold values from 0.0128 to 0.0512
- col_second: float32 [4, 1152], P('tensor', 'dp'), may hold values from 0.0128 to 0.0512
- row_second: float32 [6, 768], P(None, 'dp'), may hold values from 0.64 to 2.56
- qkv_ema: float32 [3, 768, 768], P(None, 'dp', 'tensor'), may hold values from -0.21875 to 0.21875
- out_ema: float32 [768, 768], P('tensor', 'dp'), may hold values from -0.21875 to 0.21875
- up_ema: float32 [768, 3072], P('dp', 'tensor'), may hold values from -0.21875 to 0.21875
- down_ema: float32 [3072, 768], P('tensor', 'dp'), may hold values from -0.109375 to 0.109375
- col_ema: float32 [4, 1152], P('tensor', 'dp'), may hold values from -0.4 to 0.4
- row_ema: float32 [6, 768], P(None, 'dp'), may hold values from -0.4 to 1.4
Outputs:
- outputs: bfloat16 [32768, 768], P(('dp', 'tensor'))
- input_grad: float32 [32768, 768], P(('dp', 'tensor'))
- qkv_first_new: float32 [3, 768, 768], P(None, 'dp', 'tensor')
- qkv_second_new: float32 [3, 768, 768], P(None, 'dp', 'tensor')
- qkv_weight_new: float32 [3, 768, 768], P(None, 'dp', 'tensor')
- qkv_ema_new: float32 [3, 768, 768], P(None, 'dp', 'tensor')
- out_first_new: float32 [768, 768], P('tensor', 'dp')
- out_second_new: float32 [768, 768], P('tensor', 'dp')
- out_weight_new: float32 [768, 768], P('tensor', 'dp')
- out_ema_new: float32 [768, 768], P('tensor', 'dp')
- up_first_new: float32 [768, 3072], P('dp', 'tensor')
- up_second_new: float32 [768, 3072], P('dp', 'tensor')
- up_weight_new: float32 [768, 3072], P('dp', 'tensor')
- up_ema_new: float32 [768, 3072], P('dp', 'tensor')
- down_first_new: float32 [3072, 768], P('tensor', 'dp')
- down_second_new: float32 [3072, 768], P('tensor', 'dp')
- down_weight_new: float32 [3072, 768], P('tensor', 'dp')
- down_ema_new: float32 [3072, 768], P('tensor', 'dp')
- col_first_new: float32 [4, 1152], P('tensor', 'dp')
- col_second_new: float32 [4, 1152], P('tensor', 'dp')
- col_bias_new: float32 [4, 1152], P('tensor', 'dp')
- col_ema_new: float32 [4, 1152], P('tensor', 'dp')
- row_first_new: float32 [6, 768], P(None, 'dp')
- row_second_new: float32 [6, 768], P(None, 'dp')
- row_params_new: float32 [6, 768], P(None, 'dp')
- row_ema_new: float32 [6, 768], P(None, 'dp')
Inputs may be any that keep to these rules, and one draw needn't show every extreme that they name: The last 1024 - lengths[s] rows of sequence s are padding; some sequence has none. `groups`: each row has 1 to 6 ones, none on the diagonal; some row has 6.
All inputs are finite; a program needn't handle non-finite values.
Results may differ from a plain program's by a relative error of at most 0.0055.
The roundings to bfloat16 on the way count: a program that leaves them out, or rounds other values in their place, can miss the bound.
Values may be sent and summed in bfloat16 or wider, within the bound.
A program may use at most 192 MiB of HBM per device.

v0:
```python
import jax
import jax.numpy as jnp
from jax import lax
from jax.sharding import PartitionSpec as P

D = 768
HD = 64
FF = 3072
LEN = 1024
STEP = 5


highest = lax.Precision.HIGHEST
eps_norm = 1e-05
temper = 40.0
masked = -1000000000.0
beta_one = 0.5
beta_two = 0.5
adam_eps = 1e-08
decay_rate = 0.01
ema_keep = 0.9


def layer_norm(seq_rows, gain_row, shift_row):
    row_mean = jnp.mean(seq_rows, axis=-1, keepdims=True)
    centred = seq_rows - row_mean
    variance = jnp.mean(centred * centred, axis=-1, keepdims=True)
    return centred * lax.rsqrt(variance + eps_norm) * gain_row + shift_row


def gelu_exact(values):
    return jax.nn.gelu(values, approximate=False)


def contrast_loss(pooled, groups):
    inverse_norm = lax.rsqrt(jnp.sum(pooled * pooled, axis=1, keepdims=True) + eps_norm)
    unit_rows = pooled * inverse_norm
    similar = temper * jnp.dot(unit_rows, unit_rows.T, precision=highest)
    diagonal = jnp.eye(pooled.shape[0], dtype=bool)
    others = jnp.where(diagonal, masked, similar)
    spread = jax.nn.logsumexp(others, axis=1)
    members = groups.astype(jnp.float32)
    positive = jnp.sum(members * similar, axis=1) / jnp.sum(members, axis=1)
    return jnp.sum(spread - positive)


def block_size():
    return 512


def attend(queries, keys_all, values, key_bias):
    length = queries.shape[1]
    columns = queries.shape[2]
    local_heads = columns // HD
    block_rows = block_size()
    blocks = length // block_rows
    score_scale = HD ** (-0.5)

    def one_sequence(packed):
        q_seq, k_seq, v_seq, bias_row = packed
        q_blocks = q_seq.reshape(blocks, block_rows, local_heads, HD)
        k_heads = k_seq.reshape(length, local_heads, HD)
        v_heads = v_seq.reshape(length, local_heads, HD)

        def one_block(q_blk):
            scores = (
                jnp.einsum("qhd,khd->hqk", q_blk, k_heads, preferred_element_type=jnp.float32)
                * score_scale
                + bias_row
            )
            row_max = jnp.max(scores, axis=-1, keepdims=True)
            exp_terms = jnp.exp(scores - row_max)
            row_total = jnp.sum(exp_terms, axis=-1, keepdims=True)
            soft_weights = (exp_terms / row_total).astype(jnp.bfloat16)
            context = jnp.einsum(
                "hqk,khd->qhd", soft_weights, v_heads, preferred_element_type=jnp.float32
            )
            return (context.astype(jnp.bfloat16), (row_max + jnp.log(row_total))[:, :, 0])

        contexts, log_total = lax.map(one_block, q_blocks)
        return (contexts.reshape(length, columns), log_total)

    return lax.map(one_sequence, (queries, keys_all, values, key_bias))


def attend_back(queries, keys_all, values, key_bias, grad_ctx, log_total):
    length = queries.shape[1]
    columns = queries.shape[2]
    local_heads = columns // HD
    block_rows = block_size()
    blocks = length // block_rows
    score_scale = HD ** (-0.5)

    def one_sequence(packed):
        q_seq, k_seq, v_seq, bias_row, g_seq, total_seq = packed
        q_blocks = q_seq.reshape(blocks, block_rows, local_heads, HD)
        g_blocks = g_seq.reshape(blocks, block_rows, local_heads, HD)
        k_heads = k_seq.reshape(length, local_heads, HD)
        v_heads = v_seq.reshape(length, local_heads, HD)

        def one_block(running, block_in):
            key_acc, value_acc = running
            q_blk, g_blk, total_blk = block_in
            scores = (
                jnp.einsum("qhd,khd->hqk", q_blk, k_heads, preferred_element_type=jnp.float32)
                * score_scale
                + bias_row
            )
            soft_probs = jnp.exp(scores - total_blk[:, :, None])
            grad_soft = jnp.einsum(
                "qhd,khd->hqk", g_blk, v_heads, preferred_element_type=jnp.float32
            )
            inner_sum = jnp.sum(soft_probs * grad_soft, axis=-1, keepdims=True)
            grad_scores = (soft_probs * (grad_soft - inner_sum)).astype(jnp.bfloat16)
            grad_query = (
                jnp.einsum("hqk,khd->qhd", grad_scores, k_heads, preferred_element_type=jnp.float32)
                * score_scale
            )
            key_acc = (
                key_acc
                + jnp.einsum("hqk,qhd->khd", grad_scores, q_blk, preferred_element_type=jnp.float32)
                * score_scale
            )
            value_acc = value_acc + jnp.einsum(
                "hqk,qhd->khd",
                soft_probs.astype(jnp.bfloat16),
                g_blk,
                preferred_element_type=jnp.float32,
            )
            return ((key_acc, value_acc), grad_query)

        empty_acc = jnp.zeros((length, local_heads, HD), jnp.float32)
        (key_acc, value_acc), grad_query = lax.scan(
            one_block, (empty_acc, empty_acc), (q_blocks, g_blocks, total_seq)
        )
        return (
            grad_query.reshape(length, columns),
            key_acc.reshape(length, columns),
            value_acc.reshape(length, columns),
        )

    return lax.map(one_sequence, (queries, keys_all, values, key_bias, grad_ctx, log_total))


def adam_update(weight, first_old, second, ema_old, gradient, step_rate):
    first_new = beta_one * first_old + (1 - beta_one) * gradient
    second_new = beta_two * second + (1 - beta_two) * gradient * gradient
    first_hat = first_new / (1 - beta_one**STEP)
    second_hat = second_new / (1 - beta_two**STEP)
    weight_new = weight - step_rate * (
        first_hat / (jnp.sqrt(second_hat) + adam_eps) + decay_rate * weight
    )
    ema_new = ema_keep * ema_old + (1 - ema_keep) * weight_new
    return (first_new, second_new, weight_new, ema_new)


def on_device(
    inputs,
    lengths,
    groups,
    qkv_weight,
    out_weight,
    up_weight,
    down_weight,
    col_bias,
    row_params,
    qkv_first,
    out_first,
    up_first,
    down_first,
    col_first,
    row_first,
    qkv_second,
    out_second,
    up_second,
    down_second,
    col_second,
    row_second,
    qkv_ema,
    out_ema,
    up_ema,
    down_ema,
    col_ema,
    row_ema,
):
    own_rows = inputs.shape[0]
    own_seqs = own_rows // LEN
    head_cols = qkv_weight.shape[2]
    hidden_cols = up_weight.shape[1]
    wq_rows, wo_rows, up_rows, down_rows, col_rows, row_full = (
        lax.all_gather(qkv_weight.astype(jnp.bfloat16), "dp", axis=1, tiled=True),
        lax.all_gather(out_weight.astype(jnp.bfloat16), "dp", axis=1, tiled=True),
        lax.all_gather(up_weight.astype(jnp.bfloat16), "dp", axis=0, tiled=True),
        lax.all_gather(down_weight.astype(jnp.bfloat16), "dp", axis=1, tiled=True),
        lax.all_gather(col_bias.astype(jnp.bfloat16), "dp", axis=1, tiled=True),
        lax.all_gather(row_params.astype(jnp.bfloat16), "dp", axis=1, tiled=True),
    )
    first_seq = lax.axis_index("tensor") * own_seqs
    own_lengths = lax.dynamic_slice_in_dim(lengths, first_seq, own_seqs)
    wq_full, wo_full, up_full, down_full, col_full = (
        wq_rows,
        wo_rows,
        up_rows,
        down_rows,
        col_rows,
    )
    rows_in = lax.all_gather(inputs, "tensor", axis=0, tiled=True)
    col_values = col_full.astype(jnp.float32)
    query_bias = col_values[:, :head_cols].reshape(-1)
    value_bias = col_values[:, head_cols : 2 * head_cols].reshape(-1)
    hidden_bias = col_values[:, 2 * head_cols :].reshape(-1)
    row_vals = row_full.astype(jnp.float32)
    many_rows = rows_in.shape[0]
    many_seqs = many_rows // LEN
    local_cols = wq_full.shape[2]
    positions = jnp.arange(LEN)
    key_bias = jnp.where(positions[None, :] < lengths[:, None], 0.0, masked).astype(jnp.float32)
    projected = jnp.einsum("nd,kdc->knc", rows_in, wq_full, preferred_element_type=jnp.float32)
    queries = (projected[0] + query_bias).astype(jnp.bfloat16).reshape(many_seqs, LEN, local_cols)
    keys_all = projected[1].astype(jnp.bfloat16).reshape(many_seqs, LEN, local_cols)
    values = (projected[2] + value_bias).astype(jnp.bfloat16).reshape(many_seqs, LEN, local_cols)
    contexts, log_total = attend(queries, keys_all, values, key_bias)
    context = contexts.reshape(many_rows, local_cols)
    row_piece = context
    branch_sum = lax.psum_scatter(
        jnp.dot(row_piece, wo_full, preferred_element_type=jnp.float32),
        "tensor",
        scatter_dimension=0,
        tiled=True,
    )
    attn_resid = inputs.astype(jnp.float32) + (branch_sum + row_vals[0])
    first = layer_norm(attn_resid, row_vals[1], row_vals[2])
    mid_in = lax.all_gather(first.astype(jnp.bfloat16), "tensor", axis=0, tiled=True)
    hidden = jnp.dot(mid_in, up_full, preferred_element_type=jnp.float32) + hidden_bias
    active = gelu_exact(hidden).astype(jnp.bfloat16)
    row_piece = active
    second_sum = lax.psum_scatter(
        jnp.dot(row_piece, down_full, preferred_element_type=jnp.float32),
        "tensor",
        scatter_dimension=0,
        tiled=True,
    )
    ffn_resid = first + (second_sum + row_vals[3])
    outputs = layer_norm(ffn_resid, row_vals[4], row_vals[5])
    token_weights = (positions[None, :] < own_lengths[:, None]).astype(jnp.float32)
    length_float = own_lengths.astype(jnp.float32)
    pooled_own = (
        jnp.sum(outputs.reshape(own_seqs, LEN, -1) * token_weights[:, :, None], axis=1)
        / length_float[:, None]
    )
    all_pooled = lax.all_gather(pooled_own, ("dp", "tensor"), axis=0, tiled=True)
    loss_value, loss_pull = jax.vjp(lambda pooled: contrast_loss(pooled, groups), all_pooled)
    (grad_pooled,) = loss_pull(jnp.ones_like(loss_value))
    own_grad = lax.dynamic_slice_in_dim(
        grad_pooled, lax.axis_index(("dp", "tensor")) * own_seqs, own_seqs, 0
    )
    grad_outputs = (
        (own_grad / length_float[:, None])[:, None, :] * token_weights[:, :, None]
    ).reshape(own_rows, -1)
    _, norm_pull = jax.vjp(layer_norm, ffn_resid, row_vals[4], row_vals[5])
    grad_resid, grad_gain_two, grad_shift_two = norm_pull(grad_outputs)
    grad_branch_two = grad_resid.astype(jnp.bfloat16)
    grad_bias_two = jnp.sum(grad_branch_two.astype(jnp.float32), axis=0)
    mid_grads = lax.all_gather(grad_branch_two, "tensor", axis=0, tiled=True)
    grad_down = jnp.einsum("nf,nd->fd", active, mid_grads, preferred_element_type=jnp.float32)
    grad_active = jnp.einsum("nd,fd->nf", mid_grads, down_full, preferred_element_type=jnp.float32)
    _, gelu_pull = jax.vjp(gelu_exact, hidden)
    (grad_hidden,) = gelu_pull(grad_active)
    grad_hidden_low = grad_hidden.astype(jnp.bfloat16)
    grad_bias_one = jnp.sum(grad_hidden_low.astype(jnp.float32), axis=0)
    grad_up = jnp.einsum("nd,nf->df", mid_in, grad_hidden_low, preferred_element_type=jnp.float32)
    row_piece = grad_hidden_low
    grad_first = (
        lax.psum_scatter(
            jnp.einsum("nf,df->nd", row_piece, up_full, preferred_element_type=jnp.float32),
            "tensor",
            scatter_dimension=0,
            tiled=True,
        )
        + grad_resid
    )
    _, first_pull = jax.vjp(layer_norm, attn_resid, row_vals[1], row_vals[2])
    grad_attn_resid, grad_gain_one, grad_shift_one = first_pull(grad_first)
    grad_branch_one = grad_attn_resid.astype(jnp.bfloat16)
    grad_out_bias = jnp.sum(grad_branch_one.astype(jnp.float32), axis=0)
    branch_grads = lax.all_gather(grad_branch_one, "tensor", axis=0, tiled=True)
    grad_out_w = jnp.einsum("nc,nd->cd", context, branch_grads, preferred_element_type=jnp.float32)
    grad_ctx = jnp.einsum(
        "nd,cd->nc", branch_grads, wo_full, preferred_element_type=jnp.float32
    ).astype(jnp.bfloat16)
    grad_query, grad_key, grad_value = attend_back(
        queries, keys_all, values, key_bias, grad_ctx.reshape(many_seqs, LEN, local_cols), log_total
    )
    stacked = jnp.stack(
        [
            grad_query.reshape(many_rows, local_cols),
            grad_key.reshape(many_rows, local_cols),
            grad_value.reshape(many_rows, local_cols),
        ]
    ).astype(jnp.bfloat16)
    grad_query_bias = jnp.sum(stacked[0].astype(jnp.float32), axis=0)
    grad_value_bias = jnp.sum(stacked[2].astype(jnp.float32), axis=0)
    grad_qkv = jnp.einsum("nd,knc->kdc", rows_in, stacked, preferred_element_type=jnp.float32)
    row_piece = stacked
    input_grad = (
        lax.psum_scatter(
            jnp.einsum("knc,kdc->nd", row_piece, wq_full, preferred_element_type=jnp.float32),
            "tensor",
            scatter_dimension=0,
            tiled=True,
        )
        + grad_attn_resid
    )
    col_grad = jnp.concatenate(
        [
            grad_query_bias.reshape(-1, head_cols),
            grad_value_bias.reshape(-1, head_cols),
            grad_bias_one.reshape(-1, hidden_cols),
        ],
        axis=1,
    )
    row_grad = jnp.stack(
        [grad_out_bias, grad_gain_one, grad_shift_one, grad_bias_two, grad_gain_two, grad_shift_two]
    )
    grad_qkv, grad_out_w, grad_up, grad_down, col_grad, row_grad = (
        lax.psum_scatter(grad_qkv, "dp", scatter_dimension=1, tiled=True),
        lax.psum_scatter(grad_out_w, "dp", scatter_dimension=1, tiled=True),
        lax.psum_scatter(grad_up, "dp", scatter_dimension=0, tiled=True),
        lax.psum_scatter(grad_down, "dp", scatter_dimension=1, tiled=True),
        lax.psum_scatter(col_grad, "dp", scatter_dimension=1, tiled=True),
        lax.psum_scatter(row_grad, "dp", scatter_dimension=1, tiled=True),
    )
    row_grad = lax.psum(row_grad, "tensor")
    qkv_new = adam_update(qkv_weight, qkv_first, qkv_second, qkv_ema, grad_qkv, D ** (-0.5))
    out_new = adam_update(out_weight, out_first, out_second, out_ema, grad_out_w, D ** (-0.5))
    up_new = adam_update(up_weight, up_first, up_second, up_ema, grad_up, D ** (-0.5))
    down_new = adam_update(down_weight, down_first, down_second, down_ema, grad_down, FF ** (-0.5))
    col_new = adam_update(col_bias, col_first, col_second, col_ema, col_grad, 0.1)
    row_new = adam_update(row_params, row_first, row_second, row_ema, row_grad, 0.15)
    return (
        outputs.astype(jnp.bfloat16),
        input_grad,
        qkv_new[0],
        qkv_new[1],
        qkv_new[2],
        qkv_new[3],
        out_new[0],
        out_new[1],
        out_new[2],
        out_new[3],
        up_new[0],
        up_new[1],
        up_new[2],
        up_new[3],
        down_new[0],
        down_new[1],
        down_new[2],
        down_new[3],
        col_new[0],
        col_new[1],
        col_new[2],
        col_new[3],
        row_new[0],
        row_new[1],
        row_new[2],
        row_new[3],
    )


def solution(mesh):
    placed = (
        P(("dp", "tensor"), None),
        P("dp"),
        P(),
        P(None, "dp", "tensor"),
        P("tensor", "dp"),
        P("dp", "tensor"),
        P("tensor", "dp"),
        P("tensor", "dp"),
        P(None, "dp"),
        P(None, "dp", "tensor"),
        P("tensor", "dp"),
        P("dp", "tensor"),
        P("tensor", "dp"),
        P("tensor", "dp"),
        P(None, "dp"),
        P(None, "dp", "tensor"),
        P("tensor", "dp"),
        P("dp", "tensor"),
        P("tensor", "dp"),
        P("tensor", "dp"),
        P(None, "dp"),
        P(None, "dp", "tensor"),
        P("tensor", "dp"),
        P("dp", "tensor"),
        P("tensor", "dp"),
        P("tensor", "dp"),
        P(None, "dp"),
    )
    return jax.shard_map(
        on_device,
        mesh=mesh,
        in_specs=placed,
        out_specs=(
            P(("dp", "tensor"), None),
            P(("dp", "tensor"), None),
            P(None, "dp", "tensor"),
            P(None, "dp", "tensor"),
            P(None, "dp", "tensor"),
            P(None, "dp", "tensor"),
            P("tensor", "dp"),
            P("tensor", "dp"),
            P("tensor", "dp"),
            P("tensor", "dp"),
            P("dp", "tensor"),
            P("dp", "tensor"),
            P("dp", "tensor"),
            P("dp", "tensor"),
            P("tensor", "dp"),
            P("tensor", "dp"),
            P("tensor", "dp"),
            P("tensor", "dp"),
            P("tensor", "dp"),
            P("tensor", "dp"),
            P("tensor", "dp"),
            P("tensor", "dp"),
            P(None, "dp"),
            P(None, "dp"),
            P(None, "dp"),
            P(None, "dp"),
        ),
        check_vma=False,
    )
```

profile of v0, /device:TPU:0, one launch (start us, length us, event | category | flops | bytes accessed | tf_op | source)
XLA Modules:
  0.0 1335.7 jit_solution(827697696152611194)
XLA Ops:
  12.8 23.1 %all-reduce = bf16[1152]{0:T(1024)(128)(2,1)S(1)} all-reduce(bf16[1152]{0:T(1024)(128)(2,1)S(1)} %dynamic-update-slice), channel_id=1, replica_groups=mesh['dp'=8,'tensor'=4] {'dp'}, use_global_device_ids=true, to_apply=%add | all-reduce | flops 1152 | bytes 4608
  36.9 33.4 %all_gather.36 = bf16[192,768]{0,1:T(8,128)(2,1)} all-gather(bf16[192,96]{0,1:T(8,128)(2,1)S(1)} %copy.170), channel_id=1, replica_groups=mesh['dp'=8,'tensor'=4] {'dp'}, dimensions={1}, use_global_device_ids=true | all-gather | bytes 331776 | tf_op jit(solution)/shard_map/all_gather | solution.py:192
  71.2 35.4 %all_gather.33 = bf16[3,768,192]{2,0,1:T(4,128)(2,1)S(1)} all-gather(bf16[3,96,192]{2,0,1:T(4,128)(2,1)S(1)} %copy.164), channel_id=1, replica_groups=mesh['dp'=8,'tensor'=4] {'dp'}, dimensions={1}, use_global_device_ids=true | all-gather | bytes 995328 | tf_op jit(solution)/shard_map/all_gather | solution.py:191
  139.2 56.1 %while.54 = (s32[]{:T(128)}, bf16[4,1024,192]{1,2,0:T(8,128)(2,1)}, f32[4,2,3,512]{3,2,1,0:T(4,128)}, bf16[4,1024,192]{1,2,0:T(8,128)(2,1)}, bf16[4,1024,192]{1,...) while((s32[]{:T(128)}, bf16[4,1024,192]{1,2,0:T(8,128)(2,1)}, ...), condition=%wide.region_5.6_spmd, body=%wide.region_0.5_spmd.sunk | while | flops 421624320 | bytes 26455320 | solution.py:83
  206.8 26.0 %all-gather.1 = bf16[8,96,6]{1,2,0:T(8,128)(2,1)S(1)} all-gather(bf16[1,96,6]{1,2,0:T(8,128)(2,1)S(1)} %convert_bitcast_fusion), channel_id=1, replica_groups=mesh['dp'=8,'tensor'=4] {'dp'}, dimensions={0}, use_global_device_ids=true | all-gather | bytes 10368 | tf_op jit(solution)/shard_map/all_gather | solution.py:196
  233.0 70.5 %reduce-scatter.19.cloned.1.call-done = f32[1024,768]{1,0:T(8,128)} async-done(((f32[4096,768]{1,0:T(8,128)}), f32[1024,768]{1,0:T(8,128)}) %reduce-scatter.19.cloned.1.call-update) | async-done | bytes 3145744 | tf_op jit(solution)/shard_map/reduce_scatter | solution.py:225
  310.1 45.5 %all-gather.12.cloned.1.call-done = bf16[4096,768]{1,0:T(8,128)(2,1)} async-done(((bf16[1024,768]{1,0:T(8,128)(2,1)}), bf16[4096,768]{1,0:T(8,128)(2,1)}) %all-gather.12.cloned.1.call-update) | async-done | bytes 6291472 | tf_op jit(solution)/shard_map/all_gather | solution.py:233
  355.5 35.3 %multiply_convert_fusion.1 = (bf16[4096,768]{1,0:T(8,128)(2,1)}, f32[4096,768]{1,0:T(8,128)}, f32[4096,768]{1,0:T(8,128)}) fusion(f32[768]{0:T(1024)S(1)} %slice_reduce_fusion.3, bf16[4096,768]{1,0:T(8,128)(2,1)} %all-gather.12.cloned.1.call-done, bf16[768,768]{1,0:T(8,128)(2,1)} %all-gather.14.cloned.1.call-done), kind=kOutput, calls=%fused_computation.62 | convolution fusion | flops 5039456256 | bytes 38931456 | tf_op jit(solution)/shard_map/dot_general | solution.py:234
  412.6 94.9 %reduce-scatter.21.cloned.1.call-done = f32[1024,768]{1,0:T(8,128)} async-done(((f32[4096,768]{1,0:T(8,128)}), f32[1024,768]{1,0:T(8,128)}) %reduce-scatter.21.cloned.1.call-update) | async-done | bytes 3145744 | tf_op jit(solution)/shard_map/reduce_scatter | solution.py:237
  512.7 40.8 %all-gather.2 = f32[32,1,768]{2,1,0:T(1,128)S(1)} all-gather(f32[1,1,768]{2,1,0:T(1,128)S(1)} %reshape.301), channel_id=2, replica_groups=mesh['dp'=8,'tensor'=4] {'dp','tensor'}, dimensions={0}, use_global_device_ids=true | all-gather | bytes 101376 | tf_op jit(solution)/shard_map/all_gather | solution.py:251
  563.6 42.6 %all-gather.18.cloned.1.call-done = bf16[4096,768]{1,0:T(8,128)(2,1)} async-done(((bf16[1024,768]{1,0:T(8,128)(2,1)}), bf16[4096,768]{1,0:T(8,128)(2,1)}) %all-gather.18.cloned.1.call-update) | async-done | bytes 6291472 | tf_op jit(solution)/shard_map/all_gather | solution.py:264
  606.2 18.7 %convert_reduce_fusion = (f32[768]{0:T(1024)S(1)}, bf16[4096,768]{1,0:T(8,128)(2,1)}) fusion(f32[4096,768]{1,0:T(8,128)} %get-tuple-element.649, f32[4096,768]{1,0:T(8,128)} %get-tuple-element.666, f32[768]{0:T(1024)S(1)} %slice_reduce_fusion.3, bf16[4096,768]{1,0:T(8,128)(2,1)} %all-gather.18.cloned.1.call-done, ...), kind=kOutput, calls=%fused_computation.60 | convolution fusion | flops 4885314560 | bytes 38934528 | tf_op jit(solution)/shard_map/nd,fd->nf/dot_general | solution.py:266
  625.0 10.6 fusion.97
  635.6 99.0 %reduce-scatter.23.cloned.1.call-done = f32[1024,768]{1,0:T(8,128)} async-done(((f32[4096,768]{1,0:T(8,128)}), f32[1024,768]{1,0:T(8,128)}) %reduce-scatter.23.cloned.1.call-update) | async-done | bytes 3145744 | tf_op jit(solution)/shard_map/reduce_scatter | solution.py:274
  765.3 24.2 %all-gather.20.cloned.1.call-done = bf16[4096,768]{1,0:T(8,128)(2,1)} async-done(((bf16[1024,768]{1,0:T(8,128)(2,1)}), bf16[4096,768]{1,0:T(8,128)(2,1)}) %all-gather.20.cloned.1.call-update) | async-done | bytes 6291472 | tf_op jit(solution)/shard_map/all_gather | solution.py:286
  794.7 214.3 %while.56 = (s32[]{:T(128)}, bf16[4,1024,192]{1,2,0:T(8,128)(2,1)}, bf16[4,1024,192]{1,2,0:T(8,128)(2,1)}, bf16[4,1024,192]{1,2,0:T(8,128)(2,1)}, bf16[4,1024,19...) while((s32[]{:T(128)}, bf16[4,1024,192]{1,2,0:T(8,128)(2,1)}, ...), condition=%wide.region_27.28_spmd, body=%wide.region_23.27_spmd.sunk | while | flops 1031404032 | bytes 138406688 | solution.py:142
  800.5 44.4 %while.58 = (s32[]{:T(128)}, f32[1024,3,64]{0,2,1:T(8,128)}, f32[1024,3,64]{0,2,1:T(8,128)}, bf16[2,512,3,64]{1,0,3,2:T(2,128)(2,1)}, bf16[2,512,3,64]{1,3,2,0:T...) while((s32[]{:T(128)}, f32[1024,3,64]{0,2,1:T(8,128)}, ...), condition=%wide.region_26.26_spmd.clone, body=%wide.region_24.25_spmd.clone.sunk | while | flops 1031404032 | bytes 113206720 | solution.py:133
  854.1 44.4 %while.58 = (s32[]{:T(128)}, f32[1024,3,64]{0,2,1:T(8,128)}, f32[1024,3,64]{0,2,1:T(8,128)}, bf16[2,512,3,64]{1,0,3,2:T(2,128)(2,1)}, bf16[2,512,3,64]{1,3,2,0:T...) while((s32[]{:T(128)}, f32[1024,3,64]{0,2,1:T(8,128)}, ...), condition=%wide.region_26.26_spmd.clone, body=%wide.region_24.25_spmd.clone.sunk | while | flops 1031404032 | bytes 113206720 | solution.py:133
  907.7 44.3 %while.58 = (s32[]{:T(128)}, f32[1024,3,64]{0,2,1:T(8,128)}, f32[1024,3,64]{0,2,1:T(8,128)}, bf16[2,512,3,64]{1,0,3,2:T(2,128)(2,1)}, bf16[2,512,3,64]{1,3,2,0:T...) while((s32[]{:T(128)}, f32[1024,3,64]{0,2,1:T(8,128)}, ...), condition=%wide.region_26.26_spmd.clone, body=%wide.region_24.25_spmd.clone.sunk | while | flops 1031404032 | bytes 113206720 | solution.py:133
  961.1 44.2 %while.58 = (s32[]{:T(128)}, f32[1024,3,64]{0,2,1:T(8,128)}, f32[1024,3,64]{0,2,1:T(8,128)}, bf16[2,512,3,64]{1,0,3,2:T(2,128)(2,1)}, bf16[2,512,3,64]{1,3,2,0:T...) while((s32[]{:T(128)}, f32[1024,3,64]{0,2,1:T(8,128)}, ...), condition=%wide.region_26.26_spmd.clone, body=%wide.region_24.25_spmd.clone.sunk | while | flops 1031404032 | bytes 113206720 | solution.py:133
  1052.1 10.5 convolution_bitcast_fusion
  1090.5 63.7 %reduce-scatter.33.cloned.1.call-done = f32[96,192]{1,0:T(8,128)} async-done(((f32[768,192]{1,0:T(8,128)}), f32[96,192]{1,0:T(8,128)}) %reduce-scatter.33.cloned.1.call-update) | async-done | bytes 73744
  1156.0 67.6 %reduce-scatter.31.cloned.1.call-done = f32[96,576]{1,0:T(8,128)} async-done(((f32[768,576]{1,0:T(8,128)}), f32[96,576]{1,0:T(8,128)}) %reduce-scatter.31.cloned.1.call-update) | async-done | bytes 221200
  1234.5 90.0 %reduce-scatter.25.cloned.1.call-done = f32[1024,768]{1,0:T(8,128)} async-done(((f32[4096,768]{1,0:T(8,128)}), f32[1024,768]{1,0:T(8,128)}) %reduce-scatter.25.cloned.1.call-update) | async-done | bytes 3145744 | tf_op jit(solution)/shard_map/reduce_scatter | solution.py:306
  (661 shorter events, 521.6 us)
Async XLA Ops:
  8.0 98.5 %all-gather.10.cloned.1.call-start = ((), (), s32[]{:S(2)}) async-start(), calls=%async_computation.10 | async-start | bytes 7864320 | tf_op jit(solution)/shard_map/all_gather | solution.py:207
  8.8 294.8 %reduce-scatter.19.cloned.1.call-start = ((), (), s32[]{:S(2)}) async-start(), calls=%async_computation.11 | async-start | bytes 15728640 | tf_op jit(solution)/shard_map/reduce_scatter | solution.py:225
  35.9 34.5 %copy-start.47 = (f32[1,1152]{1,0:T(1,128)}, f32[1,1152]{1,0:T(1,128)S(1)}, u32[]{:S(2)}) copy-start(f32[1,1152]{1,0:T(1,128)S(1)} %reshape.303) | copy-start | bytes 13828
  205.1 104.9 %all-gather.14.cloned.1.call-start = ((), (), s32[]{:S(2)}) async-start(), calls=%async_computation.13 | async-start | bytes 1327104 | tf_op jit(solution)/shard_map/all_gather | solution.py:193
  206.7 148.8 %all-gather.12.cloned.1.call-start = ((), (), s32[]{:S(2)}) async-start(), calls=%async_computation.12 | async-start | bytes 7864320 | tf_op jit(solution)/shard_map/all_gather | solution.py:233
  309.2 90.5 %all-gather.16.cloned.1.call-start = ((), (), s32[]{:S(2)}) async-start(), calls=%async_computation.14 | async-start | bytes 1327104 | tf_op jit(solution)/shard_map/all_gather | solution.py:194
  309.9 197.6 %reduce-scatter.21.cloned.1.call-start = ((), (), s32[]{:S(2)}) async-start(), calls=%async_computation.15 | async-start | bytes 15728640 | tf_op jit(solution)/shard_map/reduce_scatter | solution.py:237
  410.0 196.3 %all-gather.18.cloned.1.call-start = ((), (), s32[]{:S(2)}) async-start(), calls=%async_computation.16 | async-start | bytes 7864320 | tf_op jit(solution)/shard_map/all_gather | solution.py:264
  563.6 171.0 %reduce-scatter.23.cloned.1.call-start = ((), (), s32[]{:S(2)}) async-start(), calls=%async_computation.17 | async-start | bytes 15728640 | tf_op jit(solution)/shard_map/reduce_scatter | solution.py:274
  635.6 102.7 %copy-start.46 = (f32[1024]{0:T(1024)S(1)}, f32[1024]{0:T(1024)}, u32[]{:S(2)}) copy-start(f32[1024]{0:T(1024)} %copy-done.45) | copy-start | bytes 12292
  635.6 154.0 %all-gather.20.cloned.1.call-start = ((), (), s32[]{:S(2)}) async-start(), calls=%async_computation.18 | async-start | bytes 7864320 | tf_op jit(solution)/shard_map/all_gather | solution.py:286
  743.0 324.1 %reduce-scatter.29.cloned.1.call-start = ((), (), s32[]{:S(2)}) async-start(), calls=%async_computation.21 | async-start | bytes 2654208 | tf_op jit(solution)/shard_map/reduce_scatter | solution.py:329
  753.2 316.1 %reduce-scatter.27.cloned.1.call-start = ((), (), s32[]{:S(2)}) async-start(), calls=%async_computation.20 | async-start | bytes 2654208 | tf_op jit(solution)/shard_map/reduce_scatter | solution.py:328
  763.6 307.9 %reduce-scatter.37.cloned.1.call-start = ((), (), s32[]{:S(2)}) async-start(), calls=%async_computation.25 | async-start | bytes 442368
  765.3 323.6 %reduce-scatter.35.cloned.1.call-start = ((), (), s32[]{:S(2)}) async-start(), calls=%async_computation.24 | async-start | bytes 663552
  1026.6 127.6 %reduce-scatter.33.cloned.1.call-start = ((), (), s32[]{:S(2)}) async-start(), calls=%async_computation.23 | async-start | bytes 884736
  1035.7 188.0 %reduce-scatter.31.cloned.1.call-start = ((), (), s32[]{:S(2)}) async-start(), calls=%async_computation.22 | async-start | bytes 2211840
  1052.1 272.4 %reduce-scatter.25.cloned.1.call-start = ((), (), s32[]{:S(2)}) async-start(), calls=%async_computation.19 | async-start | bytes 15728640 | tf_op jit(solution)/shard_map/reduce_scatter | solution.py:306
  1066.2 89.0 %copy-start.29 = (f32[192,96]{1,0:T(8,128)S(1)}, f32[192,96]{1,0:T(8,128)}, u32[]{:S(2)}) copy-start(f32[192,96]{1,0:T(8,128)} %param.39) | copy-start | bytes 221188
  1066.2 89.0 %copy-start.40 = (f32[192,96]{1,0:T(8,128)S(1)}, f32[192,96]{1,0:T(8,128)}, u32[]{:S(2)}) copy-start(f32[192,96]{1,0:T(8,128)} %param.57) | copy-start | bytes 221188
  1066.2 89.0 %copy-start.41 = (f32[192,96]{1,0:T(8,128)S(1)}, f32[192,96]{1,0:T(8,128)}, u32[]{:S(2)}) copy-start(f32[192,96]{1,0:T(8,128)} %param.51) | copy-start | bytes 221188
  1066.3 89.0 %copy-start.42 = (f32[192,96]{1,0:T(8,128)S(1)}, f32[192,96]{1,0:T(8,128)}, u32[]{:S(2)}) copy-start(f32[192,96]{1,0:T(8,128)} %param.45) | copy-start | bytes 221188
  1156.0 168.5 %copy-start.9 = (f32[1024,768]{1,0:T(8,128)S(1)}, f32[1024,768]{1,0:T(8,128)}, u32[]{:S(2)}) copy-start(f32[1024,768]{1,0:T(8,128)} %copy-done.8) | copy-start | bytes 9437188
  1156.0 168.5 %copy-start.44 = (f32[1024]{0:T(1024)S(1)}, f32[1024]{0:T(1024)}, u32[]{:S(2)}) copy-start(f32[1024]{0:T(1024)} %copy-done.43) | copy-start | bytes 12292
  (133 other events, 525.3 us)
Sparse Core Ops, SparseCore 0:
  10.4 49.0 all-gather.9
  205.2 98.2 reduce-scatter.18
  563.7 42.4 all-gather.17
  743.1 46.3 all-gather.19
Sparse Core Ops, SparseCore 1:
  208.3 40.7 all-gather.13
  309.3 46.2 all-gather.11
  358.2 41.5 all-gather.15
  410.1 97.4 reduce-scatter.20
  635.6 98.9 reduce-scatter.22
  753.3 69.1 reduce-scatter.28
  825.8 67.8 reduce-scatter.26
  896.8 60.7 reduce-scatter.36
  1026.7 62.2 reduce-scatter.34
  1092.6 61.5 reduce-scatter.32
  1157.5 66.0 reduce-scatter.30
  1226.4 98.0 reduce-scatter.24
where the time goes:
time: 1350 us; the launch traced here: 1340 us
  waiting for transfers between devices  618 us (46%)
  matrix products  250 us (19%)
  local copies, waits for them, and re-layouts  209 us (15%)
  blocking collectives  165 us (12%)
  other arithmetic  73.8 us (5%)
  between operations  17.7 us (1%)
    unnamed x20, waiting for transfers between devices  142 us
    reduce_scatter x1, waiting for transfers between devices, on_device(): lax.psum_scatter(jnp.einsum('nf,df->nd', row_piece, up_full, preferred_el...  99 us
    reduce_scatter x1, waiting for transfers between devices, on_device(): lax.psum_scatter(jnp.dot(row_piece, down_full, preferred_element_type=jnp...  94.9 us
    reduce_scatter x1, waiting for transfers between devices, on_device(): lax.psum_scatter(jnp.einsum('knc,kdc->nd', row_piece, wq_full, preferred_...  90 us
    reduce_scatter x1, waiting for transfers between devices, on_device(): lax.psum_scatter(jnp.dot(row_piece, wo_full, preferred_element_type=jnp.f...  70.5 us
    dynamic_update_slice x16, local copies, waits for them, and re-layouts, one_sequence(): lax.scan(one_block, (empty_acc, empty_acc), (q_blocks, g_blocks, total_seq))  69.8 us
    all_gather x1, waiting for transfers between devices, on_device(): lax.all_gather(first.astype(jnp.bfloat16), 'tensor', axis=0, tiled=True)  45.5 us
    all_gather x1, waiting for transfers between devices, on_device(): mid_grads = lax.all_gather(grad_branch_two, 'tensor', axis=0, tiled=True)  42.6 us
  transfers between devices with their start and end apart: 16, of which 11 were waited for; matrix products, arithmetic and copies ran while one was open for 27% of the time, Pallas kernels for 0%

commit v1 on v0

v1 whole, which is shorter than its diff:
```python
import functools

import jax
import jax.numpy as jnp
from jax import lax
from jax.experimental import pallas as pl
from jax.experimental.pallas import tpu as pltpu
from jax.sharding import PartitionSpec as P

D = 768
H = 12
HD = 64
FF = 3072
LEN = 1024
STEP = 5
NT = 4
HC = D // NT
AUG = 80

MESH = pl.DeviceIdType.MESH
f32 = jnp.float32
bf16 = jnp.bfloat16
highest = lax.Precision.HIGHEST
eps_norm = 1e-05
temper = 40.0
masked = -1000000000.0
beta_one = 0.5
beta_two = 0.5
adam_eps = 1e-08
decay_rate = 0.01
ema_keep = 0.9
VMEM_CAP = 60 << 20


def nn(a, b):
    return jnp.dot(a, b, preferred_element_type=f32)


def nt(a, b):
    return lax.dot_general(a, b, (((1,), (1,)), ((), ())), preferred_element_type=f32)


def tn(a, b):
    return lax.dot_general(a, b, (((0,), (0,)), ((), ())), preferred_element_type=f32)


def contrast_loss(pooled, groups):
    inverse_norm = lax.rsqrt(jnp.sum(pooled * pooled, axis=1, keepdims=True) + eps_norm)
    unit_rows = pooled * inverse_norm
    similar = temper * jnp.dot(unit_rows, unit_rows.T, precision=highest)
    diagonal = jnp.eye(pooled.shape[0], dtype=bool)
    others = jnp.where(diagonal, masked, similar)
    spread = jax.nn.logsumexp(others, axis=1)
    members = groups.astype(jnp.float32)
    positive = jnp.sum(members * similar, axis=1) / jnp.sum(members, axis=1)
    return jnp.sum(spread - positive)


def adam_update(weight, first_old, second, ema_old, gradient, step_rate):
    first_new = beta_one * first_old + (1 - beta_one) * gradient
    second_new = beta_two * second + (1 - beta_two) * gradient * gradient
    first_hat = first_new / (1 - beta_one**STEP)
    second_hat = second_new / (1 - beta_two**STEP)
    weight_new = weight - step_rate * (
        first_hat / (jnp.sqrt(second_hat) + adam_eps) + decay_rate * weight
    )
    ema_new = ema_keep * ema_old + (1 - ema_keep) * weight_new
    return (first_new, second_new, weight_new, ema_new)


class Place:
    def __init__(self, depth):
        dp = lax.axis_index("dp")
        t = lax.axis_index("tensor")
        self.depth = depth
        self.z, self.x, self.y, self.c = dp // 2, dp % 2, t // 2, t % 2
        self.me = (self.z, self.x, self.y, self.c)
        self.over_x = (self.z, 1 - self.x, self.y, self.c)
        self.over_y = (self.z, self.x, 1 - self.y, self.c)
        self.over_xy = (self.z, 1 - self.x, 1 - self.y, self.c)
        self.over_c = (self.z, self.x, self.y, 1 - self.c)

    def along_z(self, k):
        return ((self.z + k) % self.depth, self.x, self.y, self.c)


def device(place):
    z, x, y, c = place
    return (z * 2 + x, y * 2 + c)


def enter(p):
    bar = pltpu.get_barrier_semaphore()
    to = [p.over_x, p.over_y, p.over_c] + [p.along_z(k) for k in range(1, p.depth)]
    for place in to:
        pl.semaphore_signal(bar, inc=1, device_id=device(place), device_id_type=MESH)
    pl.semaphore_wait(bar, len(to))


def remote(src, dst, send, recv, to):
    return pltpu.make_async_remote_copy(
        src_ref=src, dst_ref=dst, send_sem=send, recv_sem=recv, device_id=device(to), device_id_type=MESH
    )


class Gather:
    def __init__(self, p, part, own, full, sems):
        self.p, self.part, self.rows, self.own, self.full = p, part, own.shape[0], own, full
        self.recv, self.sz, self.sx, self.sy, self.sc = sems
        self.sent = []

    def spot(self, place, half=None):
        z, x, y, c = place
        r = self.rows
        step = 32 // self.full.dtype.itemsize
        start = (z * 2 + x) * r
        if half is not None:
            start, r = start + half * (r // 2), r // 2
        return self.full.at[y * 2 + c, pl.ds(pl.multiple_of(start, step), r), :]

    def copy(self, src, place, half, to, send):
        z, x, y, c = place
        dst = self.spot(place, half)
        recv = self.recv.at[self.part, (z * 2 + x) * 4 + y * 2 + c, half or 0]
        return remote(dst if src is None else src, dst, send, recv, to)

    def send(self, src, place, half, to, send):
        def make():
            return self.copy(src, place(), half, to(), send())

        make().start()
        self.sent.append(make)

    def arrived(self, place, half=None):
        self.copy(None, place, half, self.p.over_c, self.sc.at[self.part, 0]).wait_recv()

    def line_place(self, k, base=None):
        z, x, y, c = base or self.p.me
        return ((self.p.z + k) % self.p.depth, x, y, c)

    def start(self):
        p, q = self.p, self.part
        for k in range(1, p.depth):
            self.send(self.own, lambda: p.me, None, lambda k=k: p.along_z(k), lambda k=k: self.sz.at[q, k])
        self.send(self.own, lambda: p.me, None, lambda: p.over_x, lambda: self.sx.at[q, 0, 0])
        self.send(self.own, lambda: p.me, None, lambda: p.over_y, lambda: self.sy.at[q, 0, 0])
        self.send(self.own, lambda: p.me, None, lambda: p.over_c, lambda: self.sc.at[q, 0])

    def local(self, sem):
        return pltpu.make_async_copy(self.own, self.spot(self.p.me), sem.at[self.part])

    def line(self, k):
        p, q = self.p, self.part
        place = functools.partial(self.line_place, k)
        self.arrived(place())
        self.send(None, place, None, lambda: p.over_x, lambda: self.sx.at[q, 0, k])
        self.send(None, place, None, lambda: p.over_y, lambda: self.sy.at[q, 0, k])
        self.send(None, place, None, lambda: p.over_c, lambda: self.sc.at[q, k])

    def cross(self, k):
        p, q, n = self.p, self.part, self.p.depth
        for way, (base, to, sem) in enumerate(((p.over_x, p.over_y, self.sy), (p.over_y, p.over_x, self.sx))):
            place = functools.partial(self.line_place, k, base)
            self.arrived(place())
            self.send(None, place, way, lambda to=to: to, lambda sem=sem: sem.at[q, 1, k])
            self.send(None, place, None, lambda: p.over_c, lambda way=way: self.sc.at[q, (1 + way) * n + k])

    def corner(self, k):
        p, q, n = self.p, self.part, self.p.depth
        place = functools.partial(self.line_place, k, p.over_xy)
        self.arrived(place(), 0)
        self.arrived(place(), 1)
        self.send(None, place, None, lambda: p.over_c, lambda: self.sc.at[q, 3 * n + k])

    def other_core(self):
        p = self.p
        for k in range(p.depth):
            for x in range(2):
                for y in range(2):
                    self.arrived(((p.z + k) % p.depth, x, y, 1 - p.c))

    def flow(self):
        n = self.p.depth
        steps = [functools.partial(self.cross, 0)]
        for k in ([1, n - 1] + list(range(2, n - 1))) if n > 2 else range(1, n):
            steps.append(functools.partial(self.line, k))
            steps.append(functools.partial(self.cross, k))
        steps += [functools.partial(self.corner, k) for k in range(n)]
        steps.append(self.other_core)
        return steps

    def finish(self):
        for make in self.sent:
            make().wait_send()


def gather_sems(parts, n):
    dma = pltpu.SemaphoreType.DMA
    return [dma((parts, 8 * n, 2)), dma((parts, n)), dma((parts, 2, n)), dma((parts, 2, n)), dma((parts, 4 * n))]


def gather_kernel(n, *refs):
    own, full = refs[0], refs[1]
    sems, local = refs[2:7], refs[7]
    p = Place(n)
    enter(p)
    g = Gather(p, 0, own, full, sems)
    g.start()
    g.local(local).start()
    for step in g.flow():
        step()
    g.finish()
    g.local(local).wait()


def gather_one(own, n, ident):
    return pl.pallas_call(
        functools.partial(gather_kernel, n),
        out_shape=jax.ShapeDtypeStruct((4, 2 * n * own.shape[0], own.shape[1]), own.dtype),
        in_specs=[pl.BlockSpec(memory_space=pl.ANY)],
        out_specs=pl.BlockSpec(memory_space=pl.ANY),
        scratch_shapes=gather_sems(1, n) + [pltpu.SemaphoreType.DMA((1,))],
        compiler_params=pltpu.CompilerParams(collective_id=ident, has_side_effects=True),
    )(own)


class Scatter:
    def __init__(self, p, part, rows, source, slab, out, bufs, sems):
        self.p, self.part, self.rows, self.source, self.slab, self.out = p, part, rows, source, slab, out
        self.b_core, self.b_corner, self.b_cross, self.b_line = bufs
        self.ss, self.rs, self.sc, self.rc, self.sx, self.rx, self.sl, self.rl = sems
        self.sent = []

    def span(self, z, x, half=None):
        r = self.rows
        start = (z * 2 + x) * r
        if half is not None:
            start, r = start + half * (r // 2), r // 2
        return pl.ds(pl.multiple_of(start, 16), r)

    def go(self, make, *args):
        make(*args).start()
        self.sent.append(functools.partial(make, *args))

    def core_copy(self, y):
        p, q = self.p, self.part
        return remote(self.source(y * 2 + 1 - p.c), self.b_core.at[y], self.ss.at[q, y], self.rs.at[q, y], p.over_c)

    def core(self):
        for y in range(2):
            self.go(self.core_copy, y)

    def corner_copy(self, z, half):
        p, q = self.p, self.part
        src = self.slab(1 - p.y).at[self.span(z, 1 - p.x, half), :]
        to = p.over_x if half else p.over_y
        return remote(src, self.b_corner.at[half, z], self.sc.at[q, half, z], self.rc.at[q, half, z], to)

    def corner(self):
        r = self.rows
        for y in range(2):
            self.core_copy(y).wait_recv()
            slab = self.slab(y)

            def add(i, _, y=y, slab=slab):
                s = pl.ds(pl.multiple_of(i * r, 16), r)
                slab[s, :] = (slab[s, :].astype(f32) + self.b_core[y, s, :].astype(f32)).astype(bf16)
                return 0

            lax.fori_loop(0, 2 * self.p.depth, add, 0)
        for z in range(self.p.depth):
            for half in range(2):
                self.go(self.corner_copy, z, half)

    def cross_copy(self, z, way):
        p, q = self.p, self.part
        src = self.slab(1 - p.y).at[self.span(z, p.x), :] if way else self.slab(p.y).at[self.span(z, 1 - p.x), :]
        to = p.over_y if way else p.over_x
        return remote(src, self.b_cross.at[way, z], self.sx.at[q, way, z], self.rx.at[q, way, z], to)

    def cross(self):
        p = self.p
        for z in range(p.depth):
            for way in range(2):
                self.corner_copy(z, way).wait_recv()
                slab, s = (self.slab(1 - p.y), self.span(z, p.x, 1)) if way else (self.slab(p.y), self.span(z, 1 - p.x, 0))
                slab[s, :] = (slab[s, :].astype(f32) + self.b_corner[way, z].astype(f32)).astype(bf16)
                self.go(self.cross_copy, z, way)

    def line_copy(self, k):
        p, q = self.p, self.part
        z = (p.z + k) % p.depth
        return remote(self.slab(p.y).at[self.span(z, p.x), :], self.b_line.at[k], self.sl.at[q, k], self.rl.at[q, k], p.along_z(k))

    def column(self, z):
        p = self.p
        for way in range(2):
            self.cross_copy(z, way).wait_recv()
        return self.slab(p.y)[self.span(z, p.x), :].astype(f32) + self.b_cross[0, z].astype(f32) + self.b_cross[1, z].astype(f32)

    def line(self):
        p = self.p
        for k in range(1, p.depth):
            z = (p.z + k) % p.depth
            self.slab(p.y)[self.span(z, p.x), :] = self.column(z).astype(bf16)
            self.go(self.line_copy, k)

    def last(self):
        p = self.p
        total = self.column(p.z)
        for k in range(1, p.depth):
            self.line_copy(k).wait_recv()
            total = total + self.b_line[k].astype(f32)
        self.out[...] = total

    def finish(self):
        for make in self.sent:
            make().wait_send()


def scatter_bufs(n, rows, width):
    return [
        pltpu.VMEM((2, 2 * n * rows, width), bf16), pltpu.VMEM((2, n, rows // 2, width), bf16),
        pltpu.VMEM((2, n, rows, width), bf16), pltpu.VMEM((n, rows, width), bf16),
    ]


def scatter_sems(parts, n):
    dma = pltpu.SemaphoreType.DMA
    return [dma((parts, 2))] * 2 + [dma((parts, 2, n))] * 4 + [dma((parts, n))] * 2


def split3(row):
    hi = row.astype(bf16).astype(f32)
    mid = (row - hi).astype(bf16).astype(f32)
    return hi, mid, row - hi - mid


def aug_rows(*rows):
    width = rows[0].shape[1]
    at = lax.broadcasted_iota(jnp.int32, (16, width), 0)
    out = jnp.zeros((16, width), f32)
    for i, row in enumerate(rows):
        out = jnp.where(at == i, row, out)
    return out.astype(bf16)


def norm(r):
    cent = r - jnp.mean(r, axis=1, keepdims=True)
    rstd = lax.rsqrt(jnp.mean(cent * cent, axis=1, keepdims=True) + eps_norm)
    return cent * rstd, rstd


def any_spec(n):
    return [pl.BlockSpec(memory_space=pl.ANY)] * n


def vmem_spec(n):
    return [pl.BlockSpec(memory_space=pltpu.VMEM)] * n


def run(steps):
    for step in steps:
        step()


def at_step(index, hooks):
    for k, steps in hooks.items():
        pl.when(index == k)(functools.partial(run, steps))


NJ = HC // HD
ROWS = 256
CHUNKS = LEN // ROWS
PARTS = 7


def forward_kernel(n, cb, comm, *refs):
    dp = 2 * n
    r = D // dp
    (len_ref, x_ref, own_a, own_b, own_1, own_2,
     out_ref, h1_ref, xhat1_ref, rstd1_ref, g_ref, xhat2_ref, rstd2_ref, gain_ref, row_ref, hb_ref, ct_ref, every_ref, xt,
     gp_out, q_out, k_out, v_out, wa_out, w1_out, w2_out,
     wa, w1, w2, table, bcol, col, qt, kt, vt, c_nat, wo, r2, stage, pool_own, every,
     local, q_sem, stage_sem, w_sem, *sems) = refs
    length = len_ref[0]
    gathers = {}
    if comm:
        p = Place(n)
        enter(p)
        pairs = [(own_a.at[j], wa.at[j]) for j in range(NJ)] + [(own_b, table), (own_1, w1), (own_2, w2), (pool_own, every)]
        a0, a1, a2, bias, up, down, pools = [Gather(p, i, own, full, sems) for i, (own, full) in enumerate(pairs)]

        def begin(g):
            g.start()
            g.local(local).start()

        def end(g):
            g.flow()[-1]()
            g.local(local).wait()

        def piece(g, first, last):
            return [functools.partial(run, g.flow()[first:last])]

        begin(a0)
        begin(bias)
        for one, two in zip(a0.flow()[:-1], bias.flow()[:-1]):
            one()
            two()
            if one is None:
                break
        begin(a1)
        begin(a2)
        xt[...] = x_ref[...].T
        end(a0)
        end(bias)
        begin(up)
        begin(down)
        hooks = {
            0: piece(a1, 0, 3), 1: piece(a1, 3, 7), 2: piece(a1, 7, 11) + piece(a2, 0, 3),
            3: [functools.partial(end, a1)] + piece(a2, 3, 7), 4: piece(a2, 7, 11) + piece(up, 0, 1),
            5: piece(up, 1, 3), 6: piece(up, 3, 5) + piece(down, 0, 1), 7: [functools.partial(end, a2)] + piece(up, 5, 7),
            8: piece(down, 1, 3), 9: piece(down, 3, 5), 10: piece(up, 7, 11), 11: piece(down, 5, 7),
        }
    else:
        loads = [
            pltpu.make_async_copy(src, dst, local.at[i])
            for i, (src, dst) in enumerate(((own_a, wa), (own_b, table), (own_1, w1), (own_2, w2)))
        ]
        for cp in loads:
            cp.start()
        xt[...] = x_ref[...].T
        for cp in loads:
            cp.wait()
        hooks = {}

    col_rows = -(-cb // r)
    for i in range(dp):
        rows = slice(i * 32, i * 32 + 16)
        row_ref[:, i * r : i * r + r] = table[0, rows, 0:r].astype(f32)
        for t in range(NT):
            tile = table[t, rows, :].astype(f32)
            for k in range(col_rows):
                wide = min(r, cb - k * r)
                col[t, :, i * cb + k * r : i * cb + k * r + wide] = jnp.broadcast_to(tile[6 + k : 7 + k, 0:wide], (8, wide))
    for t in range(NT):
        bcol[t] = jnp.transpose(col[t, :, 0 : 2 * HC])[:, 0:1]
        hb_ref[t] = col[t, 0:1, 2 * HC : 2 * HC + D]

    ones = jnp.ones((1, LEN), f32)
    where = lax.broadcasted_iota(jnp.int32, (1, LEN), 1)
    key_bias = jnp.where(where < length, 0.0, masked).astype(f32)
    kept = ((qt, q_out), (kt, k_out), (vt, v_out))

    def head(h, _):
        j, t = h // NT, h % NT
        qkv = tn(wa[j, t, :, 0 : 3 * HD], xt[...])
        qt[h, 0:HD, :] = ((qkv[0:HD] + bcol[t, pl.ds(pl.multiple_of(j * HD, HD), HD), :]) * HD**-0.5).astype(bf16)
        kt[h, 0:HD, :] = qkv[HD : 2 * HD].astype(bf16)
        vt[h] = (qkv[2 * HD : 3 * HD] + bcol[t, pl.ds(pl.multiple_of(HC + j * HD, HD), HD), :]).astype(bf16)
        qt[h, HD:AUG, :] = aug_rows(ones)
        kt[h, HD:AUG, :] = aug_rows(key_bias, ones, ones, ones)
        s = tn(kt[h], qt[h])
        top = jnp.max(s, axis=0, keepdims=True)
        e = jnp.exp(s - top)
        total = jnp.sum(e, axis=0, keepdims=True)
        prob = (e * (1.0 / total)).astype(bf16)
        ct_ref[pl.ds(pl.multiple_of(h * HD, HD), HD), :] = nn(vt[h], prob).astype(bf16)
        hi, mid, lo = split3(-(top + jnp.log(total)))
        qt[h, HD:AUG, :] = aug_rows(ones, hi, mid, lo)
        for i, (src, dst) in enumerate(kept):
            pltpu.make_async_copy(src.at[h], dst.at[h], q_sem.at[i, h]).start()
        at_step(h, hooks)
        return 0

    lax.fori_loop(0, H, head, 0)

    if comm:
        run(piece(down, 7, 9))
    c_nat[...] = ct_ref[...].T
    for j in range(NJ):
        for t in range(NT):
            h = j * NT + t
            wo[:, h * HD : h * HD + HD] = wa[j, t, :, 3 * HD : 4 * HD]
    weights = ((wa, wa_out), (w1, w1_out), (w2, w2_out))

    def first(i, _):
        s = pl.ds(pl.multiple_of(i * ROWS, ROWS), ROWS)
        r1 = x_ref[s, :].astype(f32) + (nt(c_nat[s, :], wo[...]) + row_ref[0:1])
        xhat, rstd = norm(r1)
        xhat1_ref[s, :] = xhat
        rstd1_ref[s, :] = rstd
        h1_ref[s, :] = (xhat * row_ref[1:2] + row_ref[2:3]).astype(bf16)
        return 0

    lax.fori_loop(0, CHUNKS, first, 0)
    if comm:
        end(up)

    def staged(step):
        t, i = step // CHUNKS, step % CHUNKS
        s = pl.ds(pl.multiple_of(i * ROWS, ROWS), ROWS)
        return pltpu.make_async_copy(stage.at[step % 2], gp_out.at[t, s, :], stage_sem.at[step % 2])

    def hidden(step, _):
        t, i = step // CHUNKS, step % CHUNKS
        s = pl.ds(pl.multiple_of(i * ROWS, ROWS), ROWS)
        z = nn(h1_ref[s, :], w1[t]) + hb_ref[t]
        cdf = 0.5 + 0.5 * lax.erf(z * 0.5**0.5)
        g_ref[t, s, :] = (z * cdf).astype(bf16)

        @pl.when(step >= 2)
        def _():
            staged(step - 2).wait()

        stage[step % 2] = cdf + z * (jnp.exp(-0.5 * z * z) * 0.3989422804014327)
        staged(step).start()
        if comm:
            at_step(step, {8: piece(down, 9, 11)})
        return 0

    lax.fori_loop(0, NT * CHUNKS, hidden, 0)
    staged(NT * CHUNKS - 2).wait()
    staged(NT * CHUNKS - 1).wait()
    if comm:
        end(down)
    for i, (src, dst) in enumerate(weights):
        pltpu.make_async_copy(src, dst, w_sem.at[i]).start()
    pool = jnp.zeros((1, D), f32)
    gain_ref[...] = jnp.zeros_like(gain_ref)
    r2[0:1, :] = pool

    def second(i, _):
        s = pl.ds(pl.multiple_of(i * ROWS, ROWS), ROWS)
        res = xhat1_ref[s, :] * row_ref[1:2] + row_ref[2:3] + row_ref[3:4]
        for t in range(NT):
            res = res + nt(g_ref[t, s, :], w2[t])
        xhat, rstd = norm(res)
        xhat2_ref[s, :] = xhat
        rstd2_ref[s, :] = rstd
        y = xhat * row_ref[4:5] + row_ref[5:6]
        out_ref[s, :] = y.astype(bf16)
        here = i * ROWS + lax.broadcasted_iota(jnp.int32, (ROWS, 1), 0) < length
        r2[0:1, :] += jnp.sum(jnp.where(here, y, 0.0), axis=0, keepdims=True)
        gain_ref[...] += jnp.sum(jnp.where(here, xhat, 0.0), axis=0, keepdims=True)
        return 0

    lax.fori_loop(0, CHUNKS, second, 0)
    mean = r2[0:1, :] * (1.0 / jnp.full((1, 1), length).astype(f32))
    pool_own[...] = jnp.zeros_like(pool_own)
    for i in range(D // 128):
        pool_own[i : i + 1, :] = mean[:, i * 128 : i * 128 + 128]
    if comm:
        begin(pools)
        run(pools.flow()[:-1])
        end(pools)
        every_ref[...] = every[...]
        for g in (a0, a1, a2, bias, up, down, pools):
            g.finish()
    else:
        every_ref[...] = pool_own[...]
    for h in range(H):
        for i, (src, dst) in enumerate(kept):
            pltpu.make_async_copy(src.at[h], dst.at[h], q_sem.at[i, h]).wait()
    for i, (src, dst) in enumerate(weights):
        pltpu.make_async_copy(src, dst, w_sem.at[i]).wait()


def forward(length, x, own_a, own_b, own_1, own_2, n, cb, comm):
    s = jax.ShapeDtypeStruct
    dp = 2 * n
    dma = pltpu.SemaphoreType.DMA
    shapes = [
        s((LEN, D), bf16), s((LEN, D), bf16), s((LEN, D), f32), s((LEN, 1), f32), s((NT, LEN, D), bf16), s((LEN, D), f32),
        s((LEN, 1), f32), s((1, D), f32), s((16, D), f32), s((NT, 1, D), f32), s((D, LEN), bf16),
        s((NT, dp * 16, 128) if comm else (16, 128), f32), s((D, LEN), bf16),
    ]
    kept = [
        s((NT, LEN, D), f32), s((H, AUG, LEN), bf16), s((H, AUG, LEN), bf16), s((H, HD, LEN), bf16),
        s((NJ, NT, D, 4 * HD), bf16), s((NT, D, D), bf16), s((NT, D, D), bf16),
    ]
    scratch = [
        pltpu.VMEM((NJ, NT, D, 4 * HD), bf16), pltpu.VMEM((NT, D, D), bf16), pltpu.VMEM((NT, D, D), bf16),
        pltpu.VMEM((NT, dp * 32, 128), bf16), pltpu.VMEM((NT, 2 * HC, 1), f32), pltpu.VMEM((NT, 8, dp * cb), f32),
        pltpu.VMEM((H, AUG, LEN), bf16), pltpu.VMEM((H, AUG, LEN), bf16), pltpu.VMEM((H, HD, LEN), bf16),
        pltpu.VMEM((LEN, D), bf16), pltpu.VMEM((D, D), bf16), pltpu.VMEM((8, D), f32), pltpu.VMEM((2, ROWS, D), f32),
        pltpu.VMEM((16, 128), f32), pltpu.VMEM((NT, dp * 16, 128), f32),
        dma((PARTS,)), dma((3, H)), dma((2,)), dma((3,)),
    ]
    if comm:
        scratch += gather_sems(PARTS, n)
        params = pltpu.CompilerParams(collective_id=0, has_side_effects=True, vmem_limit_bytes=VMEM_CAP)
    else:
        params = pltpu.CompilerParams(vmem_limit_bytes=VMEM_CAP)
    return pl.pallas_call(
        functools.partial(forward_kernel, n, cb, comm),
        out_shape=shapes + kept,
        in_specs=[pl.BlockSpec(memory_space=pltpu.SMEM)] + vmem_spec(1) + any_spec(4),
        out_specs=vmem_spec(len(shapes)) + any_spec(len(kept)),
        scratch_shapes=scratch,
        compiler_params=params,
    )(length, x, own_a, own_b, own_1, own_2)


def feed_back_kernel(
    len_ref, u_ref, gain_ref, xhat2_ref, rstd2_ref, row_ref, w1_ref, w2_ref, g_ref, gp_ref, h1_ref,
    gw1_ref, gw2_ref, dh_ref, ghb_ref, grow_ref,
    df_ref, dft_ref, h1t_ref, dz_ref,
):
    @pl.when(pl.program_id(0) == 0)
    def _():
        length = len_ref[0]
        u = u_ref[...]
        du = u * row_ref[4:5]
        mean_du = jnp.mean(du, axis=1, keepdims=True)
        h1t_ref[...] = h1_ref[...].T
        grow_ref[...] = jnp.zeros_like(grow_ref)

        def rows(i, _):
            s = pl.ds(pl.multiple_of(i * ROWS, ROWS), ROWS)
            here = i * ROWS + lax.broadcasted_iota(jnp.int32, (ROWS, 1), 0) < length
            xhat = xhat2_ref[s, :]
            dot = jnp.mean(xhat * du, axis=1, keepdims=True)
            dr = jnp.where(here, rstd2_ref[s, :] * (du - mean_du - xhat * dot), 0.0)
            dh_ref[s, :] = dr
            low = dr.astype(bf16)
            df_ref[s, :] = low
            grow_ref[3:4] += jnp.sum(low.astype(f32), axis=0, keepdims=True)
            return 0

        lax.fori_loop(0, CHUNKS, rows, 0)
        grow_ref[4:5] = u * gain_ref[...]
        grow_ref[5:6] = u * jnp.full((1, 1), length).astype(f32)
        dft_ref[...] = df_ref[...].T

    hb = jnp.zeros((1, D), f32)
    for i in range(CHUNKS):
        s = pl.ds(i * ROWS, ROWS)
        dz = (nn(df_ref[s, :], w2_ref[0]) * gp_ref[0, s, :]).astype(bf16)
        dz_ref[s, :] = dz
        hb = hb + jnp.sum(dz.astype(f32), axis=0, keepdims=True)
        dh_ref[s, :] += nt(dz, w1_ref[0])
    ghb_ref[0] = hb
    gw1_ref[0] = nn(h1t_ref[...], dz_ref[...]).astype(bf16)
    gw2_ref[0] = nn(dft_ref[...], g_ref[0]).astype(bf16)


def feed_back(length, u, gain, xhat2, rstd2, row, w1, w2, g, gp, h1):
    s = jax.ShapeDtypeStruct

    def part(rows):
        return pl.BlockSpec((1, rows, D), lambda t: (t, 0, 0))

    def all_of(*shape):
        return pl.BlockSpec(shape, lambda t: (0,) * len(shape))

    return pl.pallas_call(
        feed_back_kernel,
        grid=(NT,),
        out_shape=[s((NT, D, D), bf16), s((NT, D, D), bf16), s((LEN, D), f32), s((NT, 1, D), f32), s((16, D), f32)],
        in_specs=[pl.BlockSpec(memory_space=pltpu.SMEM), all_of(1, D), all_of(1, D), all_of(LEN, D), all_of(LEN, 1), all_of(16, D),
                  part(D), part(D), part(LEN), part(LEN), all_of(LEN, D)],
        out_specs=[part(D), part(D), all_of(LEN, D), part(1), all_of(16, D)],
        scratch_shapes=[pltpu.VMEM((LEN, D), bf16), pltpu.VMEM((D, LEN), bf16), pltpu.VMEM((D, LEN), bf16), pltpu.VMEM((LEN, D), bf16)],
        compiler_params=pltpu.CompilerParams(vmem_limit_bytes=VMEM_CAP),
    )(length, u, gain, xhat2, rstd2, row, w1, w2, g, gp, h1)


def backward_kernel(n, cb, comm, *refs):
    dp = 2 * n
    r = D // dp
    (row_ref, rstd_ref, ghb_ref, grow_in, ct_ref, xt, dh_in, xhat_in, wa_in, q_in, k_in, v_in, gw1_in, gw2_in,
     dx_ref, *rest) = refs
    outs, rest = rest[: NJ + 3], rest[NJ + 3 :]
    (wa, qkv, dat, dct, dqkv, wcat, dxt, s_ref, d_ref, p_ref, ds_ref, grow, gcol, gbias, load, q_sem, *rest) = rest
    hooks = {}
    grads = [wa.at[j] for j in range(NJ)]
    if comm:
        own1, own2, *rest = rest
        bufs, sems = rest[:-8], rest[-8:]
        p = Place(n)
        enter(p)
        parts = []
        for i, (rows, src, slab) in enumerate(
            [(r, lambda t: gw1_in.at[t], lambda y: own1.at[y]), (r, lambda t: gw2_in.at[t], lambda y: own2.at[y])]
            + [(r, lambda t, g=g: g.at[t], lambda y, g=g: g.at[y * 2 + p.c]) for g in grads]
            + [(32, lambda t: gbias.at[t], lambda y: gbias.at[y * 2 + p.c])]
        ):
            parts.append(Scatter(p, i, rows, src, slab, outs[i], bufs[4 * i : 4 * i + 4], sems))
        up, down, a0, a1, a2, bias = parts
        up.core()
        down.core()
        owns = [
            pltpu.make_async_copy(src.at[y * 2 + p.c], dst.at[y], load.at[3 + 2 * i + y])
            for i, (src, dst) in enumerate(((gw1_in, own1), (gw2_in, own2))) for y in range(2)
        ]
        hooks = {
            0: [down.corner], 2: [up.cross], 3: [a0.core], 4: [down.cross], 5: [a0.corner], 6: [up.line], 7: [a1.core],
            8: [a0.cross], 9: [down.line, up.last, a1.corner], 10: [a0.line], 11: [a1.cross, a2.core],
        }
    else:
        owns = []
    loads = [
        pltpu.make_async_copy(dh_in, s_ref.at[:, 0:D], load.at[0]), pltpu.make_async_copy(xhat_in, d_ref.at[:, 0:D], load.at[1]),
        pltpu.make_async_copy(wa_in, wa, load.at[2]),
    ]
    for cp in loads + owns:
        cp.start()

    def fetch(h, slot):
        return [
            pltpu.make_async_copy(src.at[h], qkv.at[slot, i, 0 : src.shape[1], :], q_sem.at[slot, i])
            for i, src in enumerate((q_in, k_in, v_in))
        ]

    for cp in fetch(0, 0):
        cp.start()
    dxt[...] = jnp.zeros_like(dxt)
    grow[...] = grow_in[...]
    loads[0].wait()
    loads[1].wait()

    def first(i, _):
        s = pl.ds(pl.multiple_of(i * ROWS, ROWS), ROWS)
        dh = s_ref[s, 0:D]
        xhat = d_ref[s, 0:D]
        grow[1:2] += jnp.sum(dh * xhat, axis=0, keepdims=True)
        grow[2:3] += jnp.sum(dh, axis=0, keepdims=True)
        dn = dh * row_ref[1:2]
        dr = rstd_ref[s, :] * (dn - jnp.mean(dn, axis=1, keepdims=True) - xhat * jnp.mean(dn * xhat, axis=1, keepdims=True))
        dx_ref[s, :] = dr
        low = dr.astype(bf16)
        grow[0:1] += jnp.sum(low.astype(f32), axis=0, keepdims=True)
        dat[:, s] = low.T
        return 0

    for i in range(CHUNKS):
        first(i, 0)
    loads[2].wait()
    for cp in owns:
        cp.wait()
    for j in range(NJ):
        for t in range(NT):
            h = j * NT + t
            wcat[:, h * HD : h * HD + HD] = wa[j, t, :, 3 * HD : 4 * HD]
    for i in range(D // ROWS):
        s = slice(i * ROWS, (i + 1) * ROWS)
        dct[s, :] = tn(wcat[:, s], dat[...]).astype(bf16)
        gwo = nt(dat[s, :], ct_ref[...]).astype(bf16)
        for j in range(NJ):
            for t in range(NT):
                h = j * NT + t
                wa[j, t, s, 3 * HD : 4 * HD] = gwo[:, h * HD : h * HD + HD]
    if comm:
        up.corner()

    def head(h, _):
        j, t = h // NT, h % NT
        slot = h % 2
        for cp in fetch(h, slot):
            cp.wait()

        @pl.when(h + 1 < H)
        def _():
            for cp in fetch(h + 1, 1 - slot):
                cp.start()

        own = pl.ds(pl.multiple_of(h * HD, HD), HD)
        prob = jnp.exp(tn(qkv[slot, 1], qkv[slot, 0]))
        s_ref[...] = prob
        d_ref[...] = tn(qkv[slot, 2, 0:HD, :], dct[own, :])
        p_ref[...] = prob.astype(bf16)
        inner = jnp.sum(s_ref[...] * d_ref[...], axis=0, keepdims=True)
        ds_ref[...] = (s_ref[...] * (d_ref[...] - inner)).astype(bf16)
        at = pl.multiple_of(t * 3 * HD, HD)
        dqkv[pl.ds(at, HD), :] = (nn(qkv[slot, 1, 0:HD, :], ds_ref[...]) * HD**-0.5).astype(bf16)
        dqkv[pl.ds(at + HD, HD), :] = nt(qkv[slot, 0, 0:HD, :], ds_ref[...]).astype(bf16)
        dqkv[pl.ds(at + 2 * HD, HD), :] = nt(dct[own, :], p_ref[...]).astype(bf16)

        @pl.when(t == NT - 1)
        def _():
            for k in range(NT):
                wcat[:, k * 3 * HD : (k + 1) * 3 * HD] = wa[j, k, :, 0 : 3 * HD]
            sums = nt(jnp.ones((16, LEN), bf16), dqkv[...])
            for k in range(NT):
                gcol[j, k] = sums[0:8, k * 3 * HD : (k + 1) * 3 * HD]
            for i in range(D // ROWS):
                s = slice(i * ROWS, (i + 1) * ROWS)
                dxt[s, :] += nn(wcat[s, :], dqkv[...])
                g = nt(xt[s, :], dqkv[...]).astype(bf16)
                for k in range(NT):
                    wa[j, k, s, 0 : 3 * HD] = g[:, k * 3 * HD : (k + 1) * 3 * HD]

        at_step(h, hooks)
        return 0

    lax.fori_loop(0, H, head, 0)

    col_rows = -(-cb // r)
    cols = []
    for t in range(NT):
        pieces = [gcol[j, t, 0:1, 0:HD] for j in range(NJ)] + [gcol[j, t, 0:1, 2 * HD : 3 * HD] for j in range(NJ)]
        cols.append(jnp.concatenate(pieces + [ghb_ref[t]], axis=1))
    at = lax.broadcasted_iota(jnp.int32, (32, 128), 0)
    for i in range(dp):
        rows = jnp.pad(grow[0:8, i * r : i * r + r], ((0, 24), (0, 128 - r)))
        for t in range(NT):
            block = jnp.where(at < 6, rows, 0.0)
            for k in range(col_rows):
                wide = min(r, cb - k * r)
                piece = cols[t][:, i * cb + k * r : i * cb + k * r + wide]
                block = jnp.where(at == 6 + k, jnp.pad(piece, ((0, 0), (0, 128 - wide))), block)
            gbias[t, i * 32 : i * 32 + 32, :] = block.astype(bf16)
    if comm:
        bias.core()
    for i in range(CHUNKS):
        s = pl.ds(i * ROWS, ROWS)
        dx_ref[s, :] += dxt[:, s].T
    if comm:
        a2.corner()
        bias.corner()
        down.last()
        a0.last()
        a1.line()
        a2.cross()
        bias.cross()
        a1.last()
        a2.line()
        bias.line()
        a2.last()
        bias.last()
        for part in parts:
            part.finish()
    else:
        copies = [pltpu.make_async_copy(src, dst, load.at[i]) for i, (src, dst) in enumerate(zip(grads + [gbias], outs))]
        for cp in copies:
            cp.start()
        for cp in copies:
            cp.wait()


def backward(row, rstd1, ghb, grow, ct, xt, dh, xhat1, wa, qt, kt, vt, gw1, gw2, n, cb, comm):
    s = jax.ShapeDtypeStruct
    dp = 2 * n
    r = D // dp
    dma = pltpu.SemaphoreType.DMA
    if comm:
        widths = [(r, D), (r, D)] + [(r, 4 * HD)] * NJ + [(32, 128)]
        sums = [s(shape, f32) for shape in widths]
        sum_specs = vmem_spec(len(sums))
    else:
        widths = []
        sums = [s((NT, D, 4 * HD), bf16)] * NJ + [s((NT, dp * 32, 128), bf16)] + [s((8, 128), f32)] * 2
        sum_specs = any_spec(len(sums))
    scratch = [
        pltpu.VMEM((NJ, NT, D, 4 * HD), bf16), pltpu.VMEM((2, 3, AUG, LEN), bf16), pltpu.VMEM((D, LEN), bf16), pltpu.VMEM((D, LEN), bf16),
        pltpu.VMEM((D, LEN), bf16), pltpu.VMEM((D, D), bf16), pltpu.VMEM((D, LEN), f32),
        pltpu.VMEM((LEN, LEN), f32), pltpu.VMEM((LEN, LEN), f32), pltpu.VMEM((LEN, LEN), bf16), pltpu.VMEM((LEN, LEN), bf16),
        pltpu.VMEM((16, D), f32), pltpu.VMEM((NJ, NT, 8, 3 * HD), f32), pltpu.VMEM((NT, dp * 32, 128), bf16),
        dma((7,)), dma((2, 3)),
    ]
    if comm:
        scratch += [pltpu.VMEM((2, D, D), bf16)] * 2
        for rows, wide in widths:
            scratch += scatter_bufs(n, rows, wide)
        scratch += scatter_sems(len(widths), n)
        params = pltpu.CompilerParams(collective_id=1, has_side_effects=True, vmem_limit_bytes=VMEM_CAP)
    else:
        params = pltpu.CompilerParams(vmem_limit_bytes=VMEM_CAP)
    return pl.pallas_call(
        functools.partial(backward_kernel, n, cb, comm),
        out_shape=[s((LEN, D), f32)] + sums,
        in_specs=vmem_spec(6) + any_spec(8),
        out_specs=vmem_spec(1) + sum_specs,
        scratch_shapes=scratch,
        compiler_params=params,
    )(row, rstd1, ghb, grow, ct, xt, dh, xhat1, wa, qt, kt, vt, gw1, gw2)


def gather_plain(own):
    return lax.all_gather(lax.all_gather(own, "dp", axis=0, tiled=True), "tensor", axis=0)


def scatter_plain(full):
    own = lax.psum_scatter(full.astype(f32), "tensor", scatter_dimension=0, tiled=False)
    return lax.psum_scatter(own, "dp", scatter_dimension=0, tiled=True)


def by_head(wide):
    return jnp.moveaxis(wide.reshape(*wide.shape[:-1], NJ, HD), -2, 0)


def on_device(
    inputs, lengths, groups, qkv_weight, out_weight, up_weight, down_weight, col_bias, row_params,
    qkv_first, out_first, up_first, down_first, col_first, row_first,
    qkv_second, out_second, up_second, down_second, col_second, row_second,
    qkv_ema, out_ema, up_ema, down_ema, col_ema, row_ema,
):
    dp = lax.axis_size("dp")
    n = dp // 2
    r = D // dp
    cb = col_bias.shape[1]
    index = lax.axis_index(("dp", "tensor"))
    length = lax.dynamic_slice_in_dim(lengths, lax.axis_index("tensor"), 1)
    comm = r % 32 == 0

    own_a = jnp.concatenate([by_head(qkv_weight[i]) for i in range(3)] + [by_head(out_weight.T)], axis=-1).astype(bf16)
    own_1 = up_weight.astype(bf16)
    own_2 = down_weight.T.astype(bf16)
    col_rows = -(-cb // r)
    col_pad = jnp.pad(col_bias[0], (0, col_rows * r - cb)).reshape(col_rows, r)
    own_b = jnp.pad(jnp.concatenate([row_params, col_pad], axis=0), ((0, 26 - col_rows), (0, 128 - r))).astype(bf16)
    if not comm:
        own_a = jnp.stack([gather_plain(own_a[j]) for j in range(NJ)])
        own_b, own_1, own_2 = gather_plain(own_b), gather_plain(own_1), gather_plain(own_2)
    (outputs, h1, xhat1, rstd1, g, xhat2, rstd2, gain, row, hb, ct, every, xt, gp, qt, kt, vt, wa, w1, w2) = forward(
        length, inputs, own_a, own_b, own_1, own_2, n, cb, comm
    )
    if not comm:
        every = gather_plain(every)
    every = every.reshape(NT, dp, 16, 128)[:, :, : D // 128].transpose(1, 0, 2, 3).reshape(dp * NT, D)
    grad_pooled = jax.grad(lambda v: contrast_loss(v, groups))(every)
    u = lax.dynamic_slice_in_dim(grad_pooled, index, 1, 0) / length[0].astype(f32)

    gw1, gw2, dh, ghb, grow = feed_back(length, u, gain, xhat2, rstd2, row, w1, w2, g, gp, h1)
    input_grad, *sums = backward(row, rstd1, ghb, grow, ct, xt, dh, xhat1, wa, qt, kt, vt, gw1, gw2, n, cb, comm)
    if comm:
        gw1, gw2, *ga, gbias = sums
    else:
        *ga, gbias = [scatter_plain(v) for v in sums[: NJ + 1]]
        gw1, gw2 = scatter_plain(gw1), scatter_plain(gw2)

    ga = jnp.stack(ga, axis=1).reshape(r, NJ, 4, HD).transpose(2, 0, 1, 3).reshape(4, r, HC)
    grad_row = gbias[0:6, :r]
    grad_col = gbias[6 : 6 + col_rows, :r].reshape(1, col_rows * r)[:, :cb]
    qkv_new = adam_update(qkv_weight, qkv_first, qkv_second, qkv_ema, ga[0:3], D ** (-0.5))
    out_new = adam_update(out_weight, out_first, out_second, out_ema, ga[3].T, D ** (-0.5))
    up_new = adam_update(up_weight, up_first, up_second, up_ema, gw1, D ** (-0.5))
    down_new = adam_update(down_weight, down_first, down_second, down_ema, gw2.T, FF ** (-0.5))
    col_new = adam_update(col_bias, col_first, col_second, col_ema, grad_col, 0.1)
    row_new = adam_update(row_params, row_first, row_second, row_ema, grad_row, 0.15)
    return (outputs, input_grad, *qkv_new, *out_new, *up_new, *down_new, *col_new, *row_new)


def solution(mesh):
    tokens = P(("dp", "tensor"), None)
    placed = (P(None, "dp", "tensor"), P("tensor", "dp"), P("dp", "tensor"), P("tensor", "dp"), P("tensor", "dp"), P(None, "dp"))
    new = tuple(spec for spec in placed for _ in range(4))
    return jax.shard_map(
        on_device,
        mesh=mesh,
        in_specs=(tokens, P("dp"), P()) + placed * 4,
        out_specs=(tokens, tokens) + new,
        check_vma=False,
    )
```

time: 1350 us -> 326 us (0.24)
  waiting for transfers between devices: 618 us -> 0 us
  Pallas kernels: 0 us -> 288 us
  matrix products: 250 us -> 0.95 us
  local copies, waits for them, and re-layouts: 209 us -> 17.4 us
  blocking collectives: 165 us -> 0 us
  other arithmetic: 73.8 us -> 17.3 us
  between operations: 17.7 us -> 1.76 us
    reduce_scatter x6 -> x0, waiting for transfers between devices: 354 us -> none  [the longest x1 99 us: on_device(): lax.psum_scatter(jnp.einsum('nf,df->nd', row_piece, up_full, preferred_el...]
    pallas_call x0 -> x3, Pallas kernels: none -> 288 us  [the longest x1 162 us: forward(): pl.pallas_call(functools.partial(forward_kernel, n, cb, comm), out_shape=...]
    dot_general x67 -> x0, matrix products: 242 us -> none  [the longest x1 35.3 us: on_device(): jnp.dot(mid_in, up_full, preferred_element_type=jnp.float32) + hidden_bias]
    unnamed x20 -> x0, waiting for transfers between devices: 142 us -> none
    all_gather x4 -> x0, blocking collectives: 136 us -> none  [the longest x1 40.8 us: on_device(): lax.all_gather(pooled_own, ('dp', 'tensor'), axis=0, tiled=True)]
    all_gather x6 -> x0, waiting for transfers between devices: 121 us -> none  [the longest x1 45.5 us: on_device(): lax.all_gather(first.astype(jnp.bfloat16), 'tensor', axis=0, tiled=True)]
    dynamic_update_slice x32 -> x0, local copies, waits for them, and re-layouts: 88.7 us -> none  [the longest x16 69.8 us: one_sequence(): lax.scan(one_block, (empty_acc, empty_acc), (q_blocks, g_blocks, total_seq))]
    reduce_sum x21 -> x0, other arithmetic: 33.2 us -> none  [the longest x8 12.8 us: one_block(): row_total = jnp.sum(exp_terms, axis=-1, keepdims=True)]
  transfers between devices with their start and end apart: 16 -> 0, of which waited for: 11 -> 0; matrix products, arithmetic and copies ran while one was open for 27% -> 0% of each run, Pallas kernels for 0% -> 0%
where the time goes in v1:
time: 326 us; the launch traced here: 325 us
  Pallas kernels  288 us (88%)
  local copies, waits for them, and re-layouts  17.4 us (5%)
  other arithmetic  17.3 us (5%)
    pallas_call x1, Pallas kernels, forward(): pl.pallas_call(functools.partial(forward_kernel, n, cb, comm), out_shape=...  162 us
    pallas_call x1, Pallas kernels, backward(): pl.pallas_call(functools.partial(backward_kernel, n, cb, comm), out_shape...  94.3 us
    pallas_call x1, Pallas kernels, feed_back(): pl.pallas_call(feed_back_kernel, grid=(NT,), out_shape=[s((NT, D, D), bf1...  31 us
    unnamed x55, local copies, waits for them, and re-layouts  9.58 us
    add x6, other arithmetic, adam_update(): ema_new = ema_keep * ema_old + (1 - ema_keep) * weight_new  7.64 us

profile of v1, /device:TPU:0, one launch (start us, length us, event | category | flops | bytes accessed | tf_op | source)
XLA Modules:
  0.0 325.2 jit_solution(13725610408196406366)
XLA Ops:
  0.7 1.3 dynamic_slice.6.refs_0_.len_ref
  2.0 1.1 copy.57
  3.5 0.9 convert.33
  5.3 1.6 convert_bitcast_fusion.refs_5_
  6.9 1.6 convert_element_type.23.refs_4_
  9.3 162.4 %shard_map.458 = (bf16[1024,768]{1,0:T(8,128)(2,1)}, bf16[1024,768]{1,0:T(8,128)(2,1)}, f32[1024,768]{1,0:T(8,128)}, f32[1024,1]{1,0:T(8,128)}, bf16[4,1024,768]...) custom-call(s32[1]{0:T(128)} %dynamic_slice.6.refs_0_.len_ref, ...), custom_call_target="tpu_custom_call" | custom-call | tf_op jit(solution)/shard_map/pallas_call | solution.py:595
  171.7 1.0 fusion.4
  172.8 1.0 bitcast_multiply_fusion
  174.3 0.9 slice.47
  177.8 1.9 fusion.21.u_ref
  179.7 31.0 %shard_map.459 = (bf16[4,768,768]{2,1,0:T(8,128)(2,1)}, bf16[4,768,768]{2,1,0:T(8,128)(2,1)}, f32[1024,768]{1,0:T(8,128)}, f32[4,1,768]{2,1,0:T(1,128)}, f32[16,768]{1,0:T(8,128)}) custom-call(s32[1]{0:T(128)} %dynamic_slice.6.refs_0_.len_ref, f32[1,768]{1,0:T(1,128)} %fusion.21.u_ref, f32[1,768]{1,0:T(1,128)} %get-tuple-element.61.gain_ref, ...), custom_call_target="tpu_custom_call" | custom-call | tf_op jit(solution)/shard_map/pallas_call | solution.py:657
  210.7 94.3 %shard_map.460 = (f32[1024,768]{1,0:T(8,128)}, f32[96,768]{1,0:T(8,128)}, f32[96,768]{1,0:T(8,128)}, f32[96,256]{1,0:T(8,128)}, f32[96,256]{1,0:T(8,128)}, /*index=5*/f32[96,256]{1,0:T(8,128)}, f32[32,128]{1,0:T(8,128)}) custom-call(f32[16,768]{1,0:T(8,128)} %get-tuple-element.58.row_ref.refs_0_, f32[1024,1]{1,0:T(8,128)} %get-tuple-element.59.refs_1_, ...), custom_call_target="tpu_custom_call" | custom-call | tf_op jit(solution)/shard_map/pallas_call | solution.py:870
  305.1 1.0 copy.65
  306.1 1.0 copy.66
  307.1 1.0 copy.67
  309.0 0.9 copy.73
  309.9 0.9 copy.74
  311.7 0.9 copy.76
  312.6 1.7 multiply_add_fusion.7
  314.4 1.2 multiply_add_fusion.4
  315.6 2.6 multiply_add_fusion.3
  318.2 1.3 multiply_add_fusion.9
  320.8 2.7 copy.92
  323.5 1.7 copy.93
  (82 shorter events, 7.5 us)
Async XLA Ops:
  0.7 7.9 %copy-start.12 = (f32[6,96]{1,0:T(8,128)S(1)}, f32[6,96]{1,0:T(8,128)}, u32[]{:S(2)}) copy-start(f32[6,96]{1,0:T(8,128)} %param.35) | copy-start | bytes 6916
  0.7 7.9 %copy-start.17 = (f32[1,144]{1,0:T(1,128)S(1)}, f32[1,144]{1,0:T(1,128)}, u32[]{:S(2)}) copy-start(f32[1,144]{1,0:T(1,128)} %param.34) | copy-start | bytes 1732
  0.7 173.3 %copy-start.13 = (s32[32,32]{1,0:T(8,128)S(1)}, s32[32,32]{1,0:T(8,128)}, u32[]{:S(2)}) copy-start(s32[32,32]{1,0:T(8,128)} %param.29) | copy-start | bytes 12292
  210.7 97.5 %copy-start.4 = (f32[3,96,192]{2,1,0:T(8,128)S(1)}, f32[3,96,192]{2,1,0:T(8,128)}, u32[]{:S(2)}) copy-start(f32[3,96,192]{2,1,0:T(8,128)} %param.36) | copy-start | bytes 663556
  305.0 3.3 %copy-start.5 = (f32[3,96,192]{2,1,0:T(8,128)S(1)}, f32[3,96,192]{2,1,0:T(8,128)}, u32[]{:S(2)}) copy-start(f32[3,96,192]{2,1,0:T(8,128)} %param.42) | copy-start | bytes 663556
  305.1 3.5 %copy-start.6 = (f32[3,96,192]{2,1,0:T(8,128)S(1)}, f32[3,96,192]{2,1,0:T(8,128)}, u32[]{:S(2)}) copy-start(f32[3,96,192]{2,1,0:T(8,128)} %param.48) | copy-start | bytes 663556
  308.4 4.2 %copy-start.3 = (f32[192,96]{1,0:T(8,128)S(1)}, f32[192,96]{1,0:T(8,128)}, u32[]{:S(2)}) copy-start(f32[192,96]{1,0:T(8,128)} %param.31) | copy-start | bytes 221188
  308.4 4.2 %copy-start.11 = (f32[192,96]{1,0:T(8,128)S(1)}, f32[192,96]{1,0:T(8,128)}, u32[]{:S(2)}) copy-start(f32[192,96]{1,0:T(8,128)} %param.49) | copy-start | bytes 221188
  308.7 5.7 %copy-start.1 = (f32[96,768]{1,0:T(8,128)S(1)}, f32[96,768]{1,0:T(8,128)}, u32[]{:S(2)}) copy-start(f32[96,768]{1,0:T(8,128)} %param.32) | copy-start | bytes 884740
  309.0 5.4 %copy-start.7 = (f32[96,768]{1,0:T(8,128)S(1)}, f32[96,768]{1,0:T(8,128)}, u32[]{:S(2)}) copy-start(f32[96,768]{1,0:T(8,128)} %param.50) | copy-start | bytes 884740
  309.0 5.4 %copy-start.8 = (f32[96,768]{1,0:T(8,128)S(1)}, f32[96,768]{1,0:T(8,128)}, u32[]{:S(2)}) copy-start(f32[96,768]{1,0:T(8,128)} %param.44) | copy-start | bytes 884740
  309.0 5.4 %copy-start.9 = (f32[96,768]{1,0:T(8,128)S(1)}, f32[96,768]{1,0:T(8,128)}, u32[]{:S(2)}) copy-start(f32[96,768]{1,0:T(8,128)} %param.38) | copy-start | bytes 884740
  309.0 5.4 %copy-start.10 = (f32[96,768]{1,0:T(8,128)S(1)}, f32[96,768]{1,0:T(8,128)}, u32[]{:S(2)}) copy-start(f32[96,768]{1,0:T(8,128)} %get-tuple-element.85) | copy-start | bytes 884740
  309.0 6.6 %copy-start.2 = (f32[768,96]{0,1:T(8,128)S(1)}, f32[768,96]{0,1:T(8,128)}, u32[]{:S(2)}) copy-start(f32[768,96]{0,1:T(8,128)} %param.33) | copy-start | bytes 884740
  312.6 5.6 %copy-start.14 = (f32[6,96]{1,0:T(8,128)S(1)}, f32[6,96]{1,0:T(8,128)}, u32[]{:S(2)}) copy-start(f32[6,96]{1,0:T(8,128)} %param.53) | copy-start | bytes 6916
  312.6 5.6 %copy-start.15 = (f32[6,96]{1,0:T(8,128)S(1)}, f32[6,96]{1,0:T(8,128)}, u32[]{:S(2)}) copy-start(f32[6,96]{1,0:T(8,128)} %param.47) | copy-start | bytes 6916
  312.6 5.6 %copy-start.16 = (f32[6,96]{1,0:T(8,128)S(1)}, f32[6,96]{1,0:T(8,128)}, u32[]{:S(2)}) copy-start(f32[6,96]{1,0:T(8,128)} %param.41) | copy-start | bytes 6916
  312.6 7.6 %copy-start.18 = (f32[1,144]{1,0:T(1,128)S(1)}, f32[1,144]{1,0:T(1,128)}, u32[]{:S(2)}) copy-start(f32[1,144]{1,0:T(1,128)} %param.52) | copy-start | bytes 1732
  312.6 7.6 %copy-start.19 = (f32[1,144]{1,0:T(1,128)S(1)}, f32[1,144]{1,0:T(1,128)}, u32[]{:S(2)}) copy-start(f32[1,144]{1,0:T(1,128)} %param.46) | copy-start | bytes 1732
  314.4 5.9 %copy-start.20 = (f32[1,144]{1,0:T(1,128)S(1)}, f32[1,144]{1,0:T(1,128)}, u32[]{:S(2)}) copy-start(f32[1,144]{1,0:T(1,128)} %param.40) | copy-start | bytes 1732
  315.6 7.9 %copy-start = (f32[1024,768]{1,0:T(8,128)S(1)}, f32[1024,768]{1,0:T(8,128)}, u32[]{:S(2)}) copy-start(f32[1024,768]{1,0:T(8,128)} %get-tuple-element.176) | copy-start | bytes 9437188

commit v2 on v1

--- a/solution.py
+++ b/solution.py
@@ -44,18 +44,6 @@
     return lax.dot_general(a, b, (((0,), (0,)), ((), ())), preferred_element_type=f32)
 
 
-def contrast_loss(pooled, groups):
-    inverse_norm = lax.rsqrt(jnp.sum(pooled * pooled, axis=1, keepdims=True) + eps_norm)
-    unit_rows = pooled * inverse_norm
-    similar = temper * jnp.dot(unit_rows, unit_rows.T, precision=highest)
-    diagonal = jnp.eye(pooled.shape[0], dtype=bool)
-    others = jnp.where(diagonal, masked, similar)
-    spread = jax.nn.logsumexp(others, axis=1)
-    members = groups.astype(jnp.float32)
-    positive = jnp.sum(members * similar, axis=1) / jnp.sum(members, axis=1)
-    return jnp.sum(spread - positive)
-
-
 def adam_update(weight, first_old, second, ema_old, gradient, step_rate):
     first_new = beta_one * first_old + (1 - beta_one) * gradient
     second_new = beta_two * second + (1 - beta_two) * gradient * gradient
@@ -104,8 +92,8 @@
 
 
 class Gather:
-    def __init__(self, p, part, own, full, sems):
-        self.p, self.part, self.rows, self.own, self.full = p, part, own.shape[0], own, full
+    def __init__(self, p, part, own, full, sems, straight=False):
+        self.p, self.part, self.rows, self.own, self.full, self.straight = p, part, own.shape[0], own, full, straight
         self.recv, self.sz, self.sx, self.sy, self.sc = sems
         self.sent = []
 
@@ -124,104 +112,115 @@
         recv = self.recv.at[self.part, (z * 2 + x) * 4 + y * 2 + c, half or 0]
         return remote(dst if src is None else src, dst, send, recv, to)
 
-    def send(self, src, place, half, to, send):
+    def send(self, place, half, to, send, when=None, src=None):
         def make():
             return self.copy(src, place(), half, to(), send())
 
-        make().start()
-        self.sent.append(make)
+        if when is not None:
+            pl.when(when())(lambda: make().start())
+        else:
+            make().start()
+        self.sent.append((make, when))
 
     def arrived(self, place, half=None):
         self.copy(None, place, half, self.p.over_c, self.sc.at[self.part, 0]).wait_recv()
 
-    def line_place(self, k, base=None):
-        z, x, y, c = base or self.p.me
-        return ((self.p.z + k) % self.p.depth, x, y, c)
-
-    def start(self):
-        p, q = self.p, self.part
-        for k in range(1, p.depth):
-            self.send(self.own, lambda: p.me, None, lambda k=k: p.along_z(k), lambda k=k: self.sz.at[q, k])
-        self.send(self.own, lambda: p.me, None, lambda: p.over_x, lambda: self.sx.at[q, 0, 0])
-        self.send(self.own, lambda: p.me, None, lambda: p.over_y, lambda: self.sy.at[q, 0, 0])
-        self.send(self.own, lambda: p.me, None, lambda: p.over_c, lambda: self.sc.at[q, 0])
-
     def local(self, sem):
         return pltpu.make_async_copy(self.own, self.spot(self.p.me), sem.at[self.part])
 
+    def spread(self, place, slot, when=None, src=None):
+        p, q = self.p, self.part
+        self.send(place, None, lambda: p.over_x, lambda: self.sx.at[q, 0, slot], when, src)
+        self.send(place, None, lambda: p.over_y, lambda: self.sy.at[q, 0, slot], when, src)
+        self.send(place, None, lambda: p.over_c, lambda: self.sc.at[q, slot], when, src)
+
+    def start(self):
+        p, q, n = self.p, self.part, self.p.depth
+        if self.straight:
+            for k in range(1, n):
+                self.send(lambda: p.me, None, lambda k=k: p.along_z(k), lambda k=k: self.sz.at[q, k], None, self.own)
+        else:
+            self.send(lambda: p.me, None, lambda: p.along_z(1), lambda: self.sz.at[q, 0], lambda: p.z + 1 < n, self.own)
+            self.send(lambda: p.me, None, lambda: p.along_z(-1), lambda: self.sz.at[q, n], lambda: p.z > 0, self.own)
+        self.spread(lambda: p.me, 0, None, self.own)
+
+    def sides(self, k):
+        p, n = self.p, self.p.depth
+        if k == 0:
+            return [(0, 0, None)]
+        if self.straight:
+            return [(1, k, None)]
+        return [(-1, k, lambda: p.z >= k), (1, n + k, lambda: p.z + k < n)]
+
+    def line_place(self, k, base):
+        z, x, y, c = base
+        return ((self.p.z + k) % self.p.depth, x, y, c)
+
+    def wait_for(self, places, when):
+        def wait():
+            for place, half in places:
+                self.arrived(place(), half)
+
+        if when is not None:
+            pl.when(when())(wait)
+        else:
+            wait()
+
     def line(self, k):
-        p, q = self.p, self.part
-        place = functools.partial(self.line_place, k)
-        self.arrived(place())
-        self.send(None, place, None, lambda: p.over_x, lambda: self.sx.at[q, 0, k])
-        self.send(None, place, None, lambda: p.over_y, lambda: self.sy.at[q, 0, k])
-        self.send(None, place, None, lambda: p.over_c, lambda: self.sc.at[q, k])
+        p, q, n = self.p, self.part, self.p.depth
+        for sign, slot, when in self.sides(k):
+            place = functools.partial(self.line_place, sign * k, p.me)
+            self.wait_for([(place, None)], when)
+            if not self.straight:
+                more = (lambda: jnp.logical_and(p.z >= k, p.z + 1 < n)) if sign < 0 else (lambda: jnp.logical_and(p.z + k < n, p.z > 0))
+                self.send(place, None, lambda sign=sign: p.along_z(-sign), lambda slot=slot: self.sz.at[q, slot], more)
+            self.spread(place, slot, when)
 
     def cross(self, k):
         p, q, n = self.p, self.part, self.p.depth
-        for way, (base, to, sem) in enumerate(((p.over_x, p.over_y, self.sy), (p.over_y, p.over_x, self.sx))):
-            place = functools.partial(self.line_place, k, base)
-            self.arrived(place())
-            self.send(None, place, way, lambda to=to: to, lambda sem=sem: sem.at[q, 1, k])
-            self.send(None, place, None, lambda: p.over_c, lambda way=way: self.sc.at[q, (1 + way) * n + k])
+        for sign, slot, when in self.sides(k):
+            for way, (base, to, sem) in enumerate(((p.over_x, p.over_y, self.sy), (p.over_y, p.over_x, self.sx))):
+                place = functools.partial(self.line_place, sign * k, base)
+                self.wait_for([(place, None)], when)
+                self.send(place, way, lambda to=to: to, lambda sem=sem, slot=slot: sem.at[q, 1, slot], when)
+                at = (1 + way) * 2 * n + slot
+                self.send(place, None, lambda: p.over_c, lambda at=at: self.sc.at[q, at], when)
 
     def corner(self, k):
         p, q, n = self.p, self.part, self.p.depth
-        place = functools.partial(self.line_place, k, p.over_xy)
-        self.arrived(place(), 0)
-        self.arrived(place(), 1)
-        self.send(None, place, None, lambda: p.over_c, lambda: self.sc.at[q, 3 * n + k])
+        for sign, slot, when in self.sides(k):
+            place = functools.partial(self.line_place, sign * k, p.over_xy)
+            self.wait_for([(place, 0), (place, 1)], when)
+            self.send(place, None, lambda: p.over_c, lambda slot=slot: self.sc.at[q, 6 * n + slot], when)
 
     def other_core(self):
         p = self.p
-        for k in range(p.depth):
+        for z in range(p.depth):
             for x in range(2):
                 for y in range(2):
-                    self.arrived(((p.z + k) % p.depth, x, y, 1 - p.c))
+                    self.arrived((z, x, y, 1 - p.c))
 
     def flow(self):
         n = self.p.depth
         steps = [functools.partial(self.cross, 0)]
-        for k in ([1, n - 1] + list(range(2, n - 1))) if n > 2 else range(1, n):
-            steps.append(functools.partial(self.line, k))
-            steps.append(functools.partial(self.cross, k))
+        order = [1, n - 1] + list(range(2, n - 1)) if self.straight and n > 2 else list(range(1, n))
+        for k in order:
+            steps += [functools.partial(self.line, k), functools.partial(self.cross, k)]
         steps += [functools.partial(self.corner, k) for k in range(n)]
         steps.append(self.other_core)
         return steps
 
     def finish(self):
-        for make in self.sent:
-            make().wait_send()
+        for make, when in self.sent:
+            if when is not None:
+                pl.when(when())(lambda make=make: make().wait_send())
+            else:
+                make().wait_send()
 
 
 def gather_sems(parts, n):
     dma = pltpu.SemaphoreType.DMA
-    return [dma((parts, 8 * n, 2)), dma((parts, n)), dma((parts, 2, n)), dma((parts, 2, n)), dma((parts, 4 * n))]
-
-
-def gather_kernel(n, *refs):
-    own, full = refs[0], refs[1]
-    sems, local = refs[2:7], refs[7]
-    p = Place(n)
-    enter(p)
-    g = Gather(p, 0, own, full, sems)
-    g.start()
-    g.local(local).start()
-    for step in g.flow():
-        step()
-    g.finish()
-    g.local(local).wait()
-
-
-def gather_one(own, n, ident):
-    return pl.pallas_call(
-        functools.partial(gather_kernel, n),
-        out_shape=jax.ShapeDtypeStruct((4, 2 * n * own.shape[0], own.shape[1]), own.dtype),
-        in_specs=[pl.BlockSpec(memory_space=pl.ANY)],
-        out_specs=pl.BlockSpec(memory_space=pl.ANY),
-        scratch_shapes=gather_sems(1, n) + [pltpu.SemaphoreType.DMA((1,))],
-        compiler_params=pltpu.CompilerParams(collective_id=ident, has_side_effects=True),
-    )(own)
+    return [dma((parts, 8 * n, 2)), dma((parts, 2 * n)), dma((parts, 2, 2 * n)), dma((parts, 2, 2 * n)), dma((parts, 8 * n))]
 
 
 class Scatter:
@@ -374,22 +373,85 @@
 CHUNKS = LEN // ROWS
 PARTS = 7
 
+PRE = ((0, 0), (3, 0), (1, 0), (0, 1), (2, 0), (3, 1), (3, 2), (0, 2), (1, 1), (3, 3), (3, 4), (1, 2), (2, 1), (0, 3), (3, 5), (3, 6), (0, 4), (1, 3), (1, 4), (3, 7), (3, 8), (3, 9), (0, 5), (0, 6), (2, 2), (1, 5), (3, 10), (3, 11), (0, 7), (0, 8), (0, 9), (4, 0), (3, 12), (0, 10), (0, 11), (1, 6), (2, 3), (0, 12), (2, 4))
+HEAD = {0: ((1, 7), (1, 8), (1, 9), (1, 10), (2, 5), (2, 6), (1, 11), (4, 1), (4, 2), (5, 0), (1, 12), (2, 7), (2, 8), (2, 9), (2, 10)), 3: ((4, 3), (2, 11), (4, 4), (2, 12), (5, 1), (5, 2)), 5: ((4, 5), (4, 6)), 9: ((4, 7), (4, 8), (4, 9), (4, 10), (5, 3), (5, 4)), 10: ((4, 11),), 11: ((4, 12),)}
+MID = ((5, 5), (5, 6))
+LATE = {6: ((5, 7), (5, 8), (5, 9), (5, 10)), 9: ((5, 11),), 10: ((5, 12),)}
+
+
+def pack(refs, own_a, own_b, own_1, own_2, r, cb):
+    qkv, out, up, down, col, row = refs
+    high = -(-r // 128) * 128
+    out_t = jnp.concatenate([out[...], jnp.zeros((HC, high - r), f32)], axis=1)
+    out_t = jnp.concatenate([out_t, jnp.zeros((256 - HC, high), f32)], axis=0).T[0:r]
+    for j in range(NJ):
+        s = slice(j * HD, j * HD + HD)
+        own_a[j] = jnp.concatenate([qkv[0, :, s], qkv[1, :, s], qkv[2, :, s], out_t[:, s]], axis=1).astype(bf16)
+    own_b[...] = jnp.zeros_like(own_b)
+    tile = jnp.concatenate([row[...], jnp.zeros((10, r), f32)], axis=0)
+    at = lax.broadcasted_iota(jnp.int32, (16, r), 0)
+    for k in range(-(-cb // r)):
+        wide = min(r, cb - k * r)
+        piece = col[:, k * r : k * r + wide]
+        if wide < r:
+            piece = jnp.concatenate([piece, jnp.zeros((1, r - wide), f32)], axis=1)
+        tile = jnp.where(at == 6 + k, piece, tile)
+    own_b[0:16, 0:r] = tile.astype(bf16)
+    own_1[...] = up[...].astype(bf16)
+    own_2[...] = down[...].astype(bf16)
+
+
+def loss_pull(pooled, groups, index):
+    count = pooled.shape[0]
+    inv = lax.rsqrt(jnp.sum(pooled * pooled, axis=1, keepdims=True) + eps_norm)
+    unit = pooled * inv
+    similar = temper * lax.dot_general(unit, unit, (((1,), (1,)), ((), ())), precision=highest, preferred_element_type=f32)
+    rows = lax.broadcasted_iota(jnp.int32, (count, count), 0)
+    cols = lax.broadcasted_iota(jnp.int32, (count, count), 1)
+    others = jnp.where(rows == cols, masked, similar)
+    members = groups.astype(f32)
+    eye = jnp.where(rows == cols, 1.0, 0.0).astype(bf16)
+    turned = nt(eye, members.astype(bf16))
+
+    def pull(table, axis):
+        top = jnp.max(others, axis=axis, keepdims=True)
+        e = jnp.exp(others - top)
+        return e / jnp.sum(e, axis=axis, keepdims=True) - table / jnp.sum(table, axis=axis, keepdims=True)
+
+    both = temper * (pull(members, 1) + pull(turned, 0))
+    grad = lax.dot_general(both, unit, (((1,), (0,)), ((), ())), precision=highest, preferred_element_type=f32)
+    own = lax.broadcasted_iota(jnp.int32, (count, 1), 0) == index
+
+    def pick(v):
+        return jnp.sum(jnp.where(own, v, 0.0), axis=0, keepdims=True)
+
+    unit, grad = pick(unit), pick(grad)
+    return pick(inv) * (grad - unit * jnp.sum(unit * grad, axis=1, keepdims=True))
+
 
 def forward_kernel(n, cb, comm, *refs):
     dp = 2 * n
     r = D // dp
-    (len_ref, x_ref, own_a, own_b, own_1, own_2,
-     out_ref, h1_ref, xhat1_ref, rstd1_ref, g_ref, xhat2_ref, rstd2_ref, gain_ref, row_ref, hb_ref, ct_ref, every_ref, xt,
-     gp_out, q_out, k_out, v_out, wa_out, w1_out, w2_out,
-     wa, w1, w2, table, bcol, col, qt, kt, vt, c_nat, wo, r2, stage, pool_own, every,
-     local, q_sem, stage_sem, w_sem, *sems) = refs
+    given, refs = (6, refs[:2] + refs[2:]) if comm else (4, refs)
+    len_ref, groups_ref, x_ref = refs[:3]
+    weights_in, refs = refs[3 : 3 + given], refs[3 + given :]
+    (rstd1_ref, rstd2_ref, gain_ref, row_ref, hb_ref, u_ref,
+     out_out, h1_out, xhat1_out, g_out, xhat2_out, ct_out, xt_out, gp_out, q_out, k_out, v_out, wa_out, w1_out, w2_out,
+     out_ref, h1_ref, xhat1_ref, g_ref, xhat2_ref, ct_ref, xt,
+     wa, w1, w2, table, bcol, col, qt, kt, vt, kn, sb, wo, pool, stage, pool_own, every, pooled,
+     local, q_sem, stage_sem, o_sem, *sems) = refs
     length = len_ref[0]
-    gathers = {}
+    hooks, middle, late = {}, [], {}
     if comm:
+        own_a, own_b, own_1, own_2, *sems = sems
         p = Place(n)
+        pack(weights_in, own_a, own_b, own_1, own_2, r, cb)
         enter(p)
         pairs = [(own_a.at[j], wa.at[j]) for j in range(NJ)] + [(own_b, table), (own_1, w1), (own_2, w2), (pool_own, every)]
-        a0, a1, a2, bias, up, down, pools = [Gather(p, i, own, full, sems) for i, (own, full) in enumerate(pairs)]
+        straight = (False,) * NJ + (True, False, False, True)
+        a0, a1, a2, bias, up, down, pools = [
+            Gather(p, i, own, full, sems, way) for i, ((own, full), way) in enumerate(zip(pairs, straight))
+        ]
 
         def begin(g):
             g.start()
@@ -399,40 +461,37 @@
             g.flow()[-1]()
             g.local(local).wait()
 
-        def piece(g, first, last):
-            return [functools.partial(run, g.flow()[first:last])]
-
-        begin(a0)
-        begin(bias)
-        for one, two in zip(a0.flow()[:-1], bias.flow()[:-1]):
-            one()
-            two()
-            if one is None:
-                break
-        begin(a1)
-        begin(a2)
-        xt[...] = x_ref[...].T
-        end(a0)
-        end(bias)
-        begin(up)
-        begin(down)
-        hooks = {
-            0: piece(a1, 0, 3), 1: piece(a1, 3, 7), 2: piece(a1, 7, 11) + piece(a2, 0, 3),
-            3: [functools.partial(end, a1)] + piece(a2, 3, 7), 4: piece(a2, 7, 11) + piece(up, 0, 1),
-            5: piece(up, 1, 3), 6: piece(up, 3, 5) + piece(down, 0, 1), 7: [functools.partial(end, a2)] + piece(up, 5, 7),
-            8: piece(down, 1, 3), 9: piece(down, 3, 5), 10: piece(up, 7, 11), 11: piece(down, 5, 7),
-        }
+        parts = (a0, a1, a2, bias, up, down)
+        flows = [[functools.partial(begin, g)] + g.flow()[:-1] + [functools.partial(end, g)] for g in parts]
+
+        def steps(pairs):
+            return [flows[g][k] for g, k in pairs]
+
+        if n == 4:
+            run(steps(PRE[:5]))
+            xt[...] = x_ref[...].T
+            run(steps(PRE[5:]))
+            hooks = {h: steps(pairs) for h, pairs in HEAD.items()}
+            middle = steps(MID)
+            late = {h: steps(pairs) for h, pairs in LATE.items()}
+        else:
+            xt[...] = x_ref[...].T
+            for group in zip(*flows):
+                run(group)
     else:
-        loads = [
-            pltpu.make_async_copy(src, dst, local.at[i])
-            for i, (src, dst) in enumerate(((own_a, wa), (own_b, table), (own_1, w1), (own_2, w2)))
-        ]
+        loads = [pltpu.make_async_copy(src, dst, local.at[i]) for i, (src, dst) in enumerate(zip(weights_in, (wa, table, w1, w2)))]
         for cp in loads:
             cp.start()
         xt[...] = x_ref[...].T
         for cp in loads:
             cp.wait()
-        hooks = {}
+    saved = ((out_ref, out_out), (h1_ref, h1_out), (xhat1_ref, xhat1_out), (g_ref, g_out), (xhat2_ref, xhat2_out), (ct_ref, ct_out),
+             (xt, xt_out), (wa, wa_out), (w1, w1_out), (w2, w2_out))
+
+    def save(i):
+        return pltpu.make_async_copy(*saved[i], o_sem.at[i])
+
+    save(6).start()
 
     col_rows = -(-cb // r)
     for i in range(dp):
@@ -451,38 +510,60 @@
     where = lax.broadcasted_iota(jnp.int32, (1, LEN), 1)
     key_bias = jnp.where(where < length, 0.0, masked).astype(f32)
     kept = ((qt, q_out), (kt, k_out), (vt, v_out))
-
-    def head(h, _):
+    key_rows = aug_rows(key_bias, ones, ones, ones)
+    one_row = aug_rows(ones)
+    half = LEN // 2
+
+    def project(h):
         j, t = h // NT, h % NT
         qkv = tn(wa[j, t, :, 0 : 3 * HD], xt[...])
         qt[h, 0:HD, :] = ((qkv[0:HD] + bcol[t, pl.ds(pl.multiple_of(j * HD, HD), HD), :]) * HD**-0.5).astype(bf16)
         kt[h, 0:HD, :] = qkv[HD : 2 * HD].astype(bf16)
         vt[h] = (qkv[2 * HD : 3 * HD] + bcol[t, pl.ds(pl.multiple_of(HC + j * HD, HD), HD), :]).astype(bf16)
-        qt[h, HD:AUG, :] = aug_rows(ones)
-        kt[h, HD:AUG, :] = aug_rows(key_bias, ones, ones, ones)
-        s = tn(kt[h], qt[h])
+        qt[h, HD:AUG, :] = one_row
+        kt[h, HD:AUG, :] = key_rows
+        kn[h % 2] = kt[h].T
+
+    def attend(h, i, s):
+        where = slice(i * half, i * half + half)
         top = jnp.max(s, axis=0, keepdims=True)
         e = jnp.exp(s - top)
         total = jnp.sum(e, axis=0, keepdims=True)
-        prob = (e * (1.0 / total)).astype(bf16)
-        ct_ref[pl.ds(pl.multiple_of(h * HD, HD), HD), :] = nn(vt[h], prob).astype(bf16)
+        ct_ref[pl.ds(pl.multiple_of(h * HD, HD), HD), where] = (nn(vt[h], e.astype(bf16)) * (1.0 / total)).astype(bf16)
         hi, mid, lo = split3(-(top + jnp.log(total)))
-        qt[h, HD:AUG, :] = aug_rows(ones, hi, mid, lo)
+        qt[h, HD:AUG, where] = aug_rows(ones[:, where], hi, mid, lo)
+
+    project(0)
+    sb[0] = nn(kn[0], qt[0, :, 0:half])
+
+    def head(h, _):
+        after = nn(kn[h % 2], qt[h, :, half:LEN])
+        attend(h, 0, sb[0])
+        sb[1] = after
+        nxt = jnp.minimum(h + 1, H - 1)
+
+        @pl.when(h + 1 < H)
+        def _():
+            project(nxt)
+
+        after = nn(kn[nxt % 2], qt[nxt, :, 0:half])
+        attend(h, 1, sb[1])
+        sb[0] = after
         for i, (src, dst) in enumerate(kept):
             pltpu.make_async_copy(src.at[h], dst.at[h], q_sem.at[i, h]).start()
         at_step(h, hooks)
         return 0
 
     lax.fori_loop(0, H, head, 0)
-
-    if comm:
-        run(piece(down, 7, 9))
+    save(5).start()
+
+    c_nat = out_ref
     c_nat[...] = ct_ref[...].T
     for j in range(NJ):
         for t in range(NT):
             h = j * NT + t
             wo[:, h * HD : h * HD + HD] = wa[j, t, :, 3 * HD : 4 * HD]
-    weights = ((wa, wa_out), (w1, w1_out), (w2, w2_out))
+    save(7).start()
 
     def first(i, _):
         s = pl.ds(pl.multiple_of(i * ROWS, ROWS), ROWS)
@@ -494,8 +575,9 @@
         return 0
 
     lax.fori_loop(0, CHUNKS, first, 0)
-    if comm:
-        end(up)
+    save(1).start()
+    save(2).start()
+    run(middle)
 
     def staged(step):
         t, i = step // CHUNKS, step % CHUNKS
@@ -515,20 +597,16 @@
 
         stage[step % 2] = cdf + z * (jnp.exp(-0.5 * z * z) * 0.3989422804014327)
         staged(step).start()
-        if comm:
-            at_step(step, {8: piece(down, 9, 11)})
+        at_step(step, late)
         return 0
 
     lax.fori_loop(0, NT * CHUNKS, hidden, 0)
     staged(NT * CHUNKS - 2).wait()
     staged(NT * CHUNKS - 1).wait()
-    if comm:
-        end(down)
-    for i, (src, dst) in enumerate(weights):
-        pltpu.make_async_copy(src, dst, w_sem.at[i]).start()
-    pool = jnp.zeros((1, D), f32)
+    for i in (3, 8, 9):
+        save(i).start()
     gain_ref[...] = jnp.zeros_like(gain_ref)
-    r2[0:1, :] = pool
+    pool[...] = jnp.zeros_like(pool)
 
     def second(i, _):
         s = pl.ds(pl.multiple_of(i * ROWS, ROWS), ROWS)
@@ -541,65 +619,73 @@
         y = xhat * row_ref[4:5] + row_ref[5:6]
         out_ref[s, :] = y.astype(bf16)
         here = i * ROWS + lax.broadcasted_iota(jnp.int32, (ROWS, 1), 0) < length
-        r2[0:1, :] += jnp.sum(jnp.where(here, y, 0.0), axis=0, keepdims=True)
+        pool[0:1] += jnp.sum(jnp.where(here, y, 0.0), axis=0, keepdims=True)
         gain_ref[...] += jnp.sum(jnp.where(here, xhat, 0.0), axis=0, keepdims=True)
         return 0
 
     lax.fori_loop(0, CHUNKS, second, 0)
-    mean = r2[0:1, :] * (1.0 / jnp.full((1, 1), length).astype(f32))
+    size = jnp.full((1, 1), length).astype(f32)
+    mean = pool[0:1] / size
     pool_own[...] = jnp.zeros_like(pool_own)
     for i in range(D // 128):
         pool_own[i : i + 1, :] = mean[:, i * 128 : i * 128 + 128]
     if comm:
         begin(pools)
+    save(0).start()
+    save(4).start()
+    if comm:
         run(pools.flow()[:-1])
         end(pools)
-        every_ref[...] = every[...]
-        for g in (a0, a1, a2, bias, up, down, pools):
+        for i in range(dp):
+            for t in range(NT):
+                for k in range(D // 128):
+                    pooled[i * NT + t : i * NT + t + 1, k * 128 : k * 128 + 128] = every[t, i * 16 + k : i * 16 + k + 1, :]
+        u_ref[...] = loss_pull(pooled[...], groups_ref[...], lax.axis_index("dp") * NT + lax.axis_index("tensor")) / size
+        for g in parts + (pools,):
             g.finish()
     else:
-        every_ref[...] = pool_own[...]
+        u_ref[...] = mean
     for h in range(H):
         for i, (src, dst) in enumerate(kept):
             pltpu.make_async_copy(src.at[h], dst.at[h], q_sem.at[i, h]).wait()
-    for i, (src, dst) in enumerate(weights):
-        pltpu.make_async_copy(src, dst, w_sem.at[i]).wait()
-
-
-def forward(length, x, own_a, own_b, own_1, own_2, n, cb, comm):
+    for i in range(len(saved)):
+        save(i).wait()
+
+
+def forward(length, groups, x, weights, n, cb, comm):
     s = jax.ShapeDtypeStruct
     dp = 2 * n
+    r = D // dp
     dma = pltpu.SemaphoreType.DMA
-    shapes = [
-        s((LEN, D), bf16), s((LEN, D), bf16), s((LEN, D), f32), s((LEN, 1), f32), s((NT, LEN, D), bf16), s((LEN, D), f32),
-        s((LEN, 1), f32), s((1, D), f32), s((16, D), f32), s((NT, 1, D), f32), s((D, LEN), bf16),
-        s((NT, dp * 16, 128) if comm else (16, 128), f32), s((D, LEN), bf16),
-    ]
+    shapes = [s((LEN, 1), f32), s((LEN, 1), f32), s((1, D), f32), s((16, D), f32), s((NT, 1, D), f32), s((1, D), f32)]
+    big = [s((LEN, D), bf16), s((LEN, D), bf16), s((LEN, D), f32), s((NT, LEN, D), bf16), s((LEN, D), f32), s((D, LEN), bf16), s((D, LEN), bf16)]
     kept = [
         s((NT, LEN, D), f32), s((H, AUG, LEN), bf16), s((H, AUG, LEN), bf16), s((H, HD, LEN), bf16),
         s((NJ, NT, D, 4 * HD), bf16), s((NT, D, D), bf16), s((NT, D, D), bf16),
     ]
-    scratch = [
+    scratch = [pltpu.VMEM(v.shape, v.dtype) for v in big] + [
         pltpu.VMEM((NJ, NT, D, 4 * HD), bf16), pltpu.VMEM((NT, D, D), bf16), pltpu.VMEM((NT, D, D), bf16),
         pltpu.VMEM((NT, dp * 32, 128), bf16), pltpu.VMEM((NT, 2 * HC, 1), f32), pltpu.VMEM((NT, 8, dp * cb), f32),
         pltpu.VMEM((H, AUG, LEN), bf16), pltpu.VMEM((H, AUG, LEN), bf16), pltpu.VMEM((H, HD, LEN), bf16),
-        pltpu.VMEM((LEN, D), bf16), pltpu.VMEM((D, D), bf16), pltpu.VMEM((8, D), f32), pltpu.VMEM((2, ROWS, D), f32),
-        pltpu.VMEM((16, 128), f32), pltpu.VMEM((NT, dp * 16, 128), f32),
-        dma((PARTS,)), dma((3, H)), dma((2,)), dma((3,)),
+        pltpu.VMEM((2, LEN, AUG), bf16), pltpu.VMEM((2, LEN, LEN // 2), f32),
+        pltpu.VMEM((D, D), bf16), pltpu.VMEM((8, D), f32), pltpu.VMEM((2, ROWS, D), f32),
+        pltpu.VMEM((16, 128), f32), pltpu.VMEM((NT, dp * 16, 128), f32), pltpu.VMEM((dp * NT, D), f32),
+        dma((PARTS,)), dma((3, H)), dma((2,)), dma((len(big) + 3,)),
     ]
     if comm:
+        scratch += [pltpu.VMEM((NJ, r, 4 * HD), bf16), pltpu.VMEM((32, 128), bf16), pltpu.VMEM((r, D), bf16), pltpu.VMEM((r, D), bf16)]
         scratch += gather_sems(PARTS, n)
         params = pltpu.CompilerParams(collective_id=0, has_side_effects=True, vmem_limit_bytes=VMEM_CAP)
     else:
         params = pltpu.CompilerParams(vmem_limit_bytes=VMEM_CAP)
     return pl.pallas_call(
         functools.partial(forward_kernel, n, cb, comm),
-        out_shape=shapes + kept,
-        in_specs=[pl.BlockSpec(memory_space=pltpu.SMEM)] + vmem_spec(1) + any_spec(4),
-        out_specs=vmem_spec(len(shapes)) + any_spec(len(kept)),
+        out_shape=shapes + big + kept,
+        in_specs=[pl.BlockSpec(memory_space=pltpu.SMEM)] + vmem_spec(2) + (vmem_spec(6) if comm else any_spec(4)),
+        out_specs=vmem_spec(len(shapes)) + any_spec(len(big) + len(kept)),
         scratch_shapes=scratch,
         compiler_params=params,
-    )(length, x, own_a, own_b, own_1, own_2)
+    )(length, groups, x, *weights)
 
 
 def feed_back_kernel(
@@ -877,6 +963,49 @@
     )(row, rstd1, ghb, grow, ct, xt, dh, xhat1, wa, qt, kt, vt, gw1, gw2)
 
 
+def adam_kernel(cb, *refs):
+    sums, refs = refs[:6], refs[6:]
+    old, new = refs[:24], refs[24:]
+    gw1, gw2, ga, gbias = sums[0], sums[1], sums[2:5], sums[5]
+    r = gw1.shape[0]
+
+    def wide(k):
+        return jnp.concatenate([ga[j][:, k * HD : k * HD + HD] for j in range(NJ)], axis=1)
+
+    def update(i, grad, rate, at=()):
+        where = at + (Ellipsis,)
+        out = adam_update(*[old[4 * i + k][where] for k in range(4)], grad, rate)
+        for k, v in enumerate(out):
+            new[4 * i + k][where] = v
+
+    for k in range(3):
+        update(0, wide(k), D ** (-0.5), (k,))
+    high = -(-r // 128) * 128
+    turned = jnp.concatenate([wide(3), jnp.zeros((r, 256 - HC), f32)], axis=1)
+    if high > r:
+        turned = jnp.concatenate([turned, jnp.zeros((high - r, 256), f32)], axis=0)
+    update(1, turned.T[0:HC, 0:r], D ** (-0.5))
+    update(2, gw1[...], D ** (-0.5))
+    update(3, gw2[...], FF ** (-0.5))
+    rows = gbias[...]
+    pieces = [rows[6 + k : 7 + k, 0 : min(r, cb - k * r)] for k in range(-(-cb // r))]
+    update(4, jnp.concatenate(pieces, axis=1), 0.1)
+    update(5, rows[0:6, 0:r], 0.15)
+
+
+def adam(sums, olds, cb):
+    flat = [v for group in olds for v in group]
+    s = jax.ShapeDtypeStruct
+    shapes = [s(group[0].shape, f32) for group in olds for _ in range(4)]
+    return pl.pallas_call(
+        functools.partial(adam_kernel, cb),
+        out_shape=shapes,
+        in_specs=vmem_spec(6 + 24),
+        out_specs=vmem_spec(24),
+        compiler_params=pltpu.CompilerParams(vmem_limit_bytes=VMEM_CAP),
+    )(*sums, *flat)
+
+
 def gather_plain(own):
     return lax.all_gather(lax.all_gather(own, "dp", axis=0, tiled=True), "tensor", axis=0)
 
@@ -888,6 +1017,14 @@
 
 def by_head(wide):
     return jnp.moveaxis(wide.reshape(*wide.shape[:-1], NJ, HD), -2, 0)
+
+
+def packed(qkv_weight, out_weight, up_weight, down_weight, col_bias, row_params, r, cb):
+    own_a = jnp.concatenate([by_head(qkv_weight[i]) for i in range(3)] + [by_head(out_weight.T)], axis=-1).astype(bf16)
+    col_rows = -(-cb // r)
+    col_pad = jnp.pad(col_bias[0], (0, col_rows * r - cb)).reshape(col_rows, r)
+    own_b = jnp.pad(jnp.concatenate([row_params, col_pad], axis=0), ((0, 26 - col_rows), (0, 128 - r))).astype(bf16)
+    return own_a, own_b, up_weight.astype(bf16), down_weight.T.astype(bf16)
 
 
 def on_device(
@@ -900,46 +1037,36 @@
     n = dp // 2
     r = D // dp
     cb = col_bias.shape[1]
-    index = lax.axis_index(("dp", "tensor"))
     length = lax.dynamic_slice_in_dim(lengths, lax.axis_index("tensor"), 1)
     comm = r % 32 == 0
-
-    own_a = jnp.concatenate([by_head(qkv_weight[i]) for i in range(3)] + [by_head(out_weight.T)], axis=-1).astype(bf16)
-    own_1 = up_weight.astype(bf16)
-    own_2 = down_weight.T.astype(bf16)
-    col_rows = -(-cb // r)
-    col_pad = jnp.pad(col_bias[0], (0, col_rows * r - cb)).reshape(col_rows, r)
-    own_b = jnp.pad(jnp.concatenate([row_params, col_pad], axis=0), ((0, 26 - col_rows), (0, 128 - r))).astype(bf16)
-    if not comm:
-        own_a = jnp.stack([gather_plain(own_a[j]) for j in range(NJ)])
-        own_b, own_1, own_2 = gather_plain(own_b), gather_plain(own_1), gather_plain(own_2)
-    (outputs, h1, xhat1, rstd1, g, xhat2, rstd2, gain, row, hb, ct, every, xt, gp, qt, kt, vt, wa, w1, w2) = forward(
-        length, inputs, own_a, own_b, own_1, own_2, n, cb, comm
+    if comm:
+        weights = (qkv_weight, out_weight, up_weight, down_weight.T, col_bias, row_params)
+    else:
+        own_a, *others = packed(qkv_weight, out_weight, up_weight, down_weight, col_bias, row_params, r, cb)
+        own_b, own_1, own_2 = [gather_plain(v) for v in others]
+        weights = (jnp.stack([gather_plain(own_a[j]) for j in range(NJ)]), own_b, own_1, own_2)
+    (rstd1, rstd2, gain, row, hb, u, outputs, h1, xhat1, g, xhat2, ct, xt, gp, qt, kt, vt, wa, w1, w2) = forward(
+        length, groups, inputs, weights, n, cb, comm
     )
     if not comm:
-        every = gather_plain(every)
-    every = every.reshape(NT, dp, 16, 128)[:, :, : D // 128].transpose(1, 0, 2, 3).reshape(dp * NT, D)
-    grad_pooled = jax.grad(lambda v: contrast_loss(v, groups))(every)
-    u = lax.dynamic_slice_in_dim(grad_pooled, index, 1, 0) / length[0].astype(f32)
+        every = lax.all_gather(u, ("dp", "tensor"), axis=0, tiled=True)
+        u = loss_pull(every, groups, lax.axis_index(("dp", "tensor"))) / length[0].astype(f32)
 
     gw1, gw2, dh, ghb, grow = feed_back(length, u, gain, xhat2, rstd2, row, w1, w2, g, gp, h1)
     input_grad, *sums = backward(row, rstd1, ghb, grow, ct, xt, dh, xhat1, wa, qt, kt, vt, gw1, gw2, n, cb, comm)
-    if comm:
-        gw1, gw2, *ga, gbias = sums
-    else:
-        *ga, gbias = [scatter_plain(v) for v in sums[: NJ + 1]]
-        gw1, gw2 = scatter_plain(gw1), scatter_plain(gw2)
-
-    ga = jnp.stack(ga, axis=1).reshape(r, NJ, 4, HD).transpose(2, 0, 1, 3).reshape(4, r, HC)
-    grad_row = gbias[0:6, :r]
-    grad_col = gbias[6 : 6 + col_rows, :r].reshape(1, col_rows * r)[:, :cb]
-    qkv_new = adam_update(qkv_weight, qkv_first, qkv_second, qkv_ema, ga[0:3], D ** (-0.5))
-    out_new = adam_update(out_weight, out_first, out_second, out_ema, ga[3].T, D ** (-0.5))
-    up_new = adam_update(up_weight, up_first, up_second, up_ema, gw1, D ** (-0.5))
-    down_new = adam_update(down_weight, down_first, down_second, down_ema, gw2.T, FF ** (-0.5))
-    col_new = adam_update(col_bias, col_first, col_second, col_ema, grad_col, 0.1)
-    row_new = adam_update(row_params, row_first, row_second, row_ema, grad_row, 0.15)
-    return (outputs, input_grad, *qkv_new, *out_new, *up_new, *down_new, *col_new, *row_new)
+    if not comm:
+        sums = [scatter_plain(v) for v in (gw1, gw2, *sums[: NJ + 1])]
+    olds = (
+        (qkv_weight, qkv_first, qkv_second, qkv_ema),
+        (out_weight, out_first, out_second, out_ema),
+        (up_weight, up_first, up_second, up_ema),
+        (down_weight.T, down_first.T, down_second.T, down_ema.T),
+        (col_bias, col_first, col_second, col_ema),
+        (row_params, row_first, row_second, row_ema),
+    )
+    new = list(adam(sums, olds, cb))
+    new[12:16] = [v.T for v in new[12:16]]
+    return (outputs, input_grad, *new)
 
 
 def solution(mesh):

time: 326 us -> 255 us (0.78)
  Pallas kernels: 288 us -> 248 us
  other arithmetic: 17.3 us -> 0 us
  local copies, waits for them, and re-layouts: 17.4 us -> 5.56 us
    pallas_call x1, Pallas kernels: 162 us -> 118 us  [forward(): pl.pallas_call(functools.partial(forward_kernel, n, cb, comm), out_shape=...]
    add x6 -> x0, other arithmetic: 7.64 us -> none  [adam_update(): ema_new = ema_keep * ema_old + (1 - ema_keep) * weight_new]
    unnamed x55 -> x4, local copies, waits for them, and re-layouts: 9.58 us -> 4.32 us
    pallas_call x0 -> x1, Pallas kernels: none -> 4.92 us  [adam(): pl.pallas_call(functools.partial(adam_kernel, cb), out_shape=shapes, in_s...]
    convert_element_type x2 -> x0, other arithmetic: 3.28 us -> none  [the longest x1 1.64 us: on_device(): own_2 = down_weight.T.astype(bf16)]
where the time goes in v2:
time: 255 us
  Pallas kernels  248 us (97%)
  local copies, waits for them, and re-layouts  5.56 us (2%)
    pallas_call x1, Pallas kernels, forward(): pl.pallas_call(functools.partial(forward_kernel, n, cb, comm), out_shape=...  118 us
    pallas_call x1, Pallas kernels, backward(): pl.pallas_call(functools.partial(backward_kernel, n, cb, comm), out_shape...  95.1 us
    pallas_call x1, Pallas kernels, feed_back(): pl.pallas_call(feed_back_kernel, grid=(NT,), out_shape=[s((NT, D, D), bf1...  30.8 us

profile of v2, /device:TPU:0, one launch (start us, length us, event | category | flops | bytes accessed | tf_op | source)
XLA Modules:
  0.0 254.7 jit_solution(12264662759619814856)
XLA Ops:
  0.7 1.2 dynamic_slice.3.refs_0_.len_ref
  1.9 117.5 %shard_map.458 = (f32[1024,1]{1,0:T(8,128)}, f32[1024,1]{1,0:T(8,128)}, f32[1,768]{1,0:T(1,128)}, f32[16,768]{1,0:T(8,128)}, f32[4,1,768]{2,1,0:T(1,128)}, /*ind...) custom-call(s32[1]{0:T(128)} %dynamic_slice.3.refs_0_.len_ref, ...), custom_call_target="tpu_custom_call" | custom-call | tf_op jit(solution)/shard_map/pallas_call | solution.py:681
  119.5 30.8 %shard_map.459 = (bf16[4,768,768]{2,1,0:T(8,128)(2,1)}, bf16[4,768,768]{2,1,0:T(8,128)(2,1)}, f32[1024,768]{1,0:T(8,128)}, f32[4,1,768]{2,1,0:T(1,128)}, f32[16,768]{1,0:T(8,128)}) custom-call(s32[1]{0:T(128)} %dynamic_slice.3.refs_0_.len_ref, f32[1,768]{1,0:T(1,128)} %get-tuple-element.84.u_ref, f32[1,768]{1,0:T(1,128)} %get-tuple-element.85.gain_ref, ...), custom_call_target="tpu_custom_call" | custom-call | tf_op jit(solution)/shard_map/pallas_call | solution.py:743
  150.3 95.1 %shard_map.460 = (f32[1024,768]{1,0:T(8,128)}, f32[96,768]{1,0:T(8,128)}, f32[96,768]{1,0:T(8,128)}, f32[96,256]{1,0:T(8,128)}, f32[96,256]{1,0:T(8,128)}, /*index=5*/f32[96,256]{1,0:T(8,128)}, f32[32,128]{1,0:T(8,128)}) custom-call(f32[16,768]{1,0:T(8,128)} %get-tuple-element.82.row_ref.refs_0_, f32[1024,1]{1,0:T(8,128)} %get-tuple-element.83.refs_1_, ...), custom_call_target="tpu_custom_call" | custom-call | tf_op jit(solution)/shard_map/pallas_call | solution.py:956
  245.4 0.0 copy-start
  245.4 4.9 %shard_map.461 = (f32[3,96,192]{2,1,0:T(8,128)}, f32[3,96,192]{2,1,0:T(8,128)}, f32[3,96,192]{2,1,0:T(8,128)}, f32[3,96,192]{2,1,0:T(8,128)}, f32[192,96]{1,0:T(...) custom-call(f32[96,768]{1,0:T(8,128)} %get-tuple-element.106.refs_0_, ...), custom_call_target="tpu_custom_call" | custom-call | tf_op jit(solution)/shard_map/pallas_call | solution.py:1000
  250.4 2.7 %copy.55 = bf16[1024,768]{1,0:T(8,128)(2,1)} copy(bf16[1024,768]{1,0:T(8,128)(2,1)} %get-tuple-element.162) | data formatting | bytes 3145728
  253.0 0.0 copy-done
  253.0 1.7 copy.56
Async XLA Ops:
  245.4 7.6 %copy-start = (f32[1024,768]{1,0:T(8,128)S(1)}, f32[1024,768]{1,0:T(8,128)}, u32[]{:S(2)}) copy-start(f32[1024,768]{1,0:T(8,128)} %get-tuple-element.163) | copy-start | bytes 9437188

commit v3 on v2

v3 whole, which is shorter than its diff:
```python
import functools

import jax
import jax.numpy as jnp
from jax import lax
from jax.experimental import pallas as pl
from jax.experimental.pallas import tpu as pltpu
from jax.sharding import PartitionSpec as P

D = 768
H = 12
HD = 64
FF = 3072
LEN = 1024
STEP = 5
NT = 4
HC = D // NT
AUG = 80

MESH = pl.DeviceIdType.MESH
f32 = jnp.float32
bf16 = jnp.bfloat16
highest = lax.Precision.HIGHEST
eps_norm = 1e-05
temper = 40.0
masked = -1000000000.0
beta_one = 0.5
beta_two = 0.5
adam_eps = 1e-08
decay_rate = 0.01
ema_keep = 0.9
VMEM_CAP = 60 << 20


def nn(a, b):
    return jnp.dot(a, b, preferred_element_type=f32)


def nt(a, b):
    return lax.dot_general(a, b, (((1,), (1,)), ((), ())), preferred_element_type=f32)


def tn(a, b):
    return lax.dot_general(a, b, (((0,), (0,)), ((), ())), preferred_element_type=f32)


def adam_update(weight, first_old, second, ema_old, gradient, step_rate):
    first_new = beta_one * first_old + (1 - beta_one) * gradient
    second_new = beta_two * second + (1 - beta_two) * gradient * gradient
    first_hat = first_new / (1 - beta_one**STEP)
    second_hat = second_new / (1 - beta_two**STEP)
    weight_new = weight - step_rate * (
        first_hat / (jnp.sqrt(second_hat) + adam_eps) + decay_rate * weight
    )
    ema_new = ema_keep * ema_old + (1 - ema_keep) * weight_new
    return (first_new, second_new, weight_new, ema_new)


class Place:
    def __init__(self, depth):
        dp = lax.axis_index("dp")
        t = lax.axis_index("tensor")
        self.depth = depth
        self.z, self.x, self.y, self.c = dp // 2, dp % 2, t // 2, t % 2
        self.me = (self.z, self.x, self.y, self.c)
        self.over_x = (self.z, 1 - self.x, self.y, self.c)
        self.over_y = (self.z, self.x, 1 - self.y, self.c)
        self.over_xy = (self.z, 1 - self.x, 1 - self.y, self.c)
        self.over_c = (self.z, self.x, self.y, 1 - self.c)

    def along_z(self, k):
        return ((self.z + k) % self.depth, self.x, self.y, self.c)


def device(place):
    z, x, y, c = place
    return (z * 2 + x, y * 2 + c)


def enter(p):
    bar = pltpu.get_barrier_semaphore()
    to = [p.over_x, p.over_y, p.over_c] + [p.along_z(k) for k in range(1, p.depth)]
    for place in to:
        pl.semaphore_signal(bar, inc=1, device_id=device(place), device_id_type=MESH)
    pl.semaphore_wait(bar, len(to))


def remote(src, dst, send, recv, to):
    return pltpu.make_async_remote_copy(
        src_ref=src, dst_ref=dst, send_sem=send, recv_sem=recv, device_id=device(to), device_id_type=MESH
    )


class Gather:
    def __init__(self, p, part, full, sems, straight=False):
        self.p, self.part, self.full, self.straight = p, part, full, straight
        self.rows = full.shape[1] // (2 * p.depth)
        self.recv, self.pair_recv, self.sz, self.sx, self.sy, self.sk, self.sc = sems

    def spot(self, place, wide=1):
        z, x, y, c = place
        r = self.rows
        step = 32 // self.full.dtype.itemsize
        return self.full.at[y * 2 + c, pl.ds(pl.multiple_of((z * 2 + x) * r, step), wide * r), :]

    def copy(self, place, to, send):
        z, x, y, c = place
        ref = self.spot(place)
        return remote(ref, ref, send.at[self.part], self.recv.at[self.part, (z * 2 + x) * 4 + y * 2 + c], to)

    def pair_copy(self, z, y, c):
        ref = self.spot((z, 0, y, c), 2)
        return remote(ref, ref, self.sc.at[self.part], self.pair_recv.at[self.part, z * 2 + y], self.p.over_c)

    def send(self, place, to, send, when=None):
        def start():
            self.copy(place(), to, send).start()

        if when is not None:
            pl.when(when())(start)
        else:
            start()

    def start(self):
        p, n = self.p, self.p.depth

        def me():
            return p.me

        if self.straight:
            for k in range(1, n):
                self.send(me, p.along_z(k), self.sz)
        else:
            self.send(me, p.along_z(1), self.sz, lambda: p.z + 1 < n)
            self.send(me, p.along_z(-1), self.sz, lambda: p.z > 0)
        self.send(me, p.over_x, self.sx)
        self.send(me, p.over_y, self.sy)

    def sides(self, k):
        p, n = self.p, self.p.depth
        if k == 0:
            return [(0, None)]
        if self.straight:
            return [(1, None)]
        return [(-1, lambda: p.z >= k), (1, lambda: p.z + k < n)]

    def each(self, k, step):
        for sign, when in self.sides(k):
            go = functools.partial(step, sign, sign * k)
            if when is not None:
                pl.when(when())(go)
            else:
                go()

    def arrived(self, place):
        self.copy(place, self.p.over_c, self.sx).wait_recv()

    def at(self, k, x, y):
        return ((self.p.z + k) % self.p.depth, x, y, self.p.c)

    def line(self, k):
        p, n = self.p, self.p.depth

        def step(sign, far):
            place = functools.partial(self.at, far, p.x, p.y)
            self.arrived(place())
            if not self.straight:
                self.send(place, p.along_z(-sign), self.sz, (lambda: p.z + 1 < n) if sign < 0 else (lambda: p.z > 0))
            self.send(place, p.over_x, self.sx)
            self.send(place, p.over_y, self.sy)

        self.each(k, step)

    def cross(self, k):
        p = self.p

        def step(sign, far):
            self.arrived(self.at(far, 1 - p.x, p.y))
            self.arrived(self.at(far, p.x, 1 - p.y))
            z = (p.z + far) % p.depth
            odd = (z + self.part) % 2
            x, y = jnp.where(odd == 1, p.x, 1 - p.x), jnp.where(odd == 1, 1 - p.y, p.y)
            to = (p.z, jnp.where(odd == 1, 1 - p.x, p.x), jnp.where(odd == 1, p.y, 1 - p.y), p.c)
            self.copy((z, x, y, p.c), to, self.sk).start()
            self.pair_copy(z, p.y, p.c).start()

        self.each(k, step)

    def corner(self, k):
        p = self.p

        def step(sign, far):
            self.arrived(self.at(far, 1 - p.x, 1 - p.y))
            self.pair_copy((p.z + far) % p.depth, 1 - p.y, p.c).start()

        self.each(k, step)

    def other_core(self):
        for z in range(self.p.depth):
            for y in range(2):
                self.pair_copy(z, y, 1 - self.p.c).wait_recv()

    def flow(self):
        n = self.p.depth
        steps = [functools.partial(self.cross, 0)]
        order = [1, n - 1] + list(range(2, n - 1)) if self.straight and n > 2 else list(range(1, n))
        for k in order:
            steps += [functools.partial(self.line, k), functools.partial(self.cross, k)]
        steps += [functools.partial(self.corner, k) for k in range(n)]
        steps.append(self.other_core)
        return steps

    def finish(self):
        n, r = self.p.depth, self.rows

        def left(ref, sem):
            pltpu.make_async_copy(ref, ref, sem.at[self.part]).wait()

        for sem in (self.sx, self.sy, self.sk):
            left(self.full.at[0, 0 : n * r, :], sem)
        left(self.full.at[0:2], self.sc)
        if self.straight:
            left(self.full.at[0, 0 : (n - 1) * r, :], self.sz)
        else:
            for z in range(n):
                count = (z + 1 if z + 1 < n else 0) + (n - z if z > 0 else 0)
                if count:
                    pl.when(self.p.z == z)(functools.partial(left, self.full.at[0, 0 : count * r, :], self.sz))


def gather_sems(parts, n):
    dma = pltpu.SemaphoreType.DMA
    return [dma((parts, 8 * n)), dma((parts, 2 * n))] + [dma((parts,))] * 5


class Scatter:
    def __init__(self, p, part, rows, grads, out, bufs, temp, load, sems):
        self.p, self.part, self.rows, self.grads, self.out, self.temp, self.load = p, part, rows, grads, out, temp, load
        self.b_core, self.b_corner, self.b_cross, self.b_line = bufs
        self.ss, self.rs, self.sc, self.rc, self.sx, self.rx, self.sl, self.rl = sems

    def slab(self, y):
        return self.grads(y * 2 + self.p.c)

    def span(self, z, x):
        return pl.ds(pl.multiple_of((z * 2 + x) * self.rows, 16), self.rows)

    def which(self, k):
        return self.p.y if k else 1 - self.p.y

    def core_copy(self, k):
        p, q = self.p, self.part
        return remote(self.grads(self.which(k) * 2 + 1 - p.c), self.b_core.at[k], self.ss.at[q], self.rs.at[q, k], p.over_c)

    def core(self, k):
        self.core_copy(k).start()

    def add(self, k):
        r = self.rows
        self.core_copy(k).wait_recv()
        slab = self.slab(self.which(k))
        cp = pltpu.make_async_copy(self.b_core.at[k], self.temp, self.load)
        cp.start()
        cp.wait()

        def one(i, _):
            s = pl.ds(pl.multiple_of(i * r, 16), r)
            slab[s, :] = (slab[s, :].astype(f32) + self.temp[s, :].astype(f32)).astype(bf16)
            return 0

        lax.fori_loop(0, 2 * self.p.depth, one, 0)

    def corner_copy(self, z):
        p, q = self.p, self.part
        src = self.slab(1 - p.y).at[self.span(z, 1 - p.x), :]
        return remote(src, self.b_corner.at[z], self.sc.at[q], self.rc.at[q, z], p.over_x if (z + q) % 2 else p.over_y)

    def corner(self):
        for z in range(self.p.depth):
            self.corner_copy(z).start()

    def cross_copy(self, z, way):
        p, q = self.p, self.part
        src = self.slab(1 - p.y).at[self.span(z, p.x), :] if way else self.slab(p.y).at[self.span(z, 1 - p.x), :]
        to = p.over_y if way else p.over_x
        return remote(src, self.b_cross.at[way, z], self.sx.at[q], self.rx.at[q, way, z], to)

    def cross(self):
        p = self.p
        for z in range(p.depth):
            self.corner_copy(z).wait_recv()
            slab, s = (self.slab(1 - p.y), self.span(z, p.x)) if (z + self.part) % 2 else (self.slab(p.y), self.span(z, 1 - p.x))
            slab[s, :] = (slab[s, :].astype(f32) + self.b_corner[z].astype(f32)).astype(bf16)
            for way in range(2):
                self.cross_copy(z, way).start()

    def line_copy(self, k):
        p, q = self.p, self.part
        z = (p.z + k) % p.depth
        return remote(self.slab(p.y).at[self.span(z, p.x), :], self.b_line.at[k], self.sl.at[q], self.rl.at[q, k], p.along_z(k))

    def column(self, z):
        p = self.p
        for way in range(2):
            self.cross_copy(z, way).wait_recv()
        return self.slab(p.y)[self.span(z, p.x), :].astype(f32) + self.b_cross[0, z].astype(f32) + self.b_cross[1, z].astype(f32)

    def line(self):
        p = self.p
        for k in range(1, p.depth):
            z = (p.z + k) % p.depth
            self.slab(p.y)[self.span(z, p.x), :] = self.column(z).astype(bf16)
            self.line_copy(k).start()

    def last(self):
        p = self.p
        total = self.column(p.z)
        for k in range(1, p.depth):
            self.line_copy(k).wait_recv()
            total = total + self.b_line[k].astype(f32)
        self.out[...] = total

    def finish(self):
        q = self.part
        for ref, sem in ((self.b_core, self.ss), (self.b_corner, self.sc), (self.b_cross, self.sx), (self.b_line.at[1 : self.p.depth], self.sl)):
            pltpu.make_async_copy(ref, ref, sem.at[q]).wait()


def scatter_bufs(n, rows, width):
    return [pltpu.VMEM((n, rows, width), bf16), pltpu.VMEM((2, n, rows, width), bf16), pltpu.VMEM((n, rows, width), bf16)]


def scatter_sems(parts, n):
    dma = pltpu.SemaphoreType.DMA
    return [dma((parts,)), dma((parts, 2)), dma((parts,)), dma((parts, n)), dma((parts,)), dma((parts, 2, n)), dma((parts,)), dma((parts, n))]


def split3(row):
    hi = row.astype(bf16).astype(f32)
    mid = (row - hi).astype(bf16).astype(f32)
    return hi, mid, row - hi - mid


def aug_rows(*rows):
    width = rows[0].shape[1]
    at = lax.broadcasted_iota(jnp.int32, (16, width), 0)
    out = jnp.zeros((16, width), f32)
    for i, row in enumerate(rows):
        out = jnp.where(at == i, row, out)
    return out.astype(bf16)


def norm(r):
    cent = r - jnp.mean(r, axis=1, keepdims=True)
    rstd = lax.rsqrt(jnp.mean(cent * cent, axis=1, keepdims=True) + eps_norm)
    return cent * rstd, rstd


def any_spec(n):
    return [pl.BlockSpec(memory_space=pl.ANY)] * n


def vmem_spec(n):
    return [pl.BlockSpec(memory_space=pltpu.VMEM)] * n


def run(steps):
    for step in steps:
        step()


def at_step(index, hooks):
    for k, steps in hooks.items():
        pl.when(index == k)(functools.partial(run, steps))


NJ = HC // HD
ROWS = 256
CHUNKS = LEN // ROWS
PARTS = 7

PRE = ((0, 0), (3, 0), (1, 0), (0, 1), (0, 2), (3, 1), (3, 2), (1, 1), (1, 2), (0, 3), (0, 4), (3, 3), (3, 4), (1, 3), (1, 4), (0, 5), (2, 0), (0, 6), (3, 5), (3, 6), (0, 7), (4, 0), (0, 8), (0, 9), (0, 10), (1, 5), (1, 6), (2, 1), (0, 11), (3, 7), (3, 8), (0, 12), (3, 9), (2, 2), (4, 1), (4, 2), (5, 0), (1, 7), (3, 10), (3, 11), (1, 8), (1, 9), (3, 12), (1, 10), (2, 3), (2, 4))
HEAD = {2: ((4, 3), (1, 11), (4, 4), (1, 12)), 3: ((2, 5), (2, 6), (5, 1), (5, 2)), 4: ((2, 7), (2, 8), (2, 9), (2, 10)), 6: ((4, 5), (4, 6), (2, 11), (2, 12)), 9: ((4, 7), (4, 8), (4, 9), (4, 10), (5, 3), (5, 4)), 11: ((4, 11),)}
MID = ((4, 12), (5, 5), (5, 6))
LATE = {11: ((5, 7), (5, 8), (5, 9), (5, 10)), 15: ((5, 11), (5, 12))}


def pack(refs, wa, table, w1, w2, p, r, cb):
    qkv, out, up, down, col, row = refs
    dp, t = p.z * 2 + p.x, p.y * 2 + p.c
    at = pl.ds(pl.multiple_of(dp * r, 16), r)
    high = -(-r // 128) * 128
    out_t = jnp.concatenate([out[...], jnp.zeros((HC, high - r), f32)], axis=1)
    out_t = jnp.concatenate([out_t, jnp.zeros((256 - HC, high), f32)], axis=0).T[0:r]
    for j in range(NJ):
        s = slice(j * HD, j * HD + HD)
        wa[j, t, at, :] = jnp.concatenate([qkv[0, :, s], qkv[1, :, s], qkv[2, :, s], out_t[:, s]], axis=1).astype(bf16)
    tile = jnp.concatenate([row[...], jnp.zeros((10, r), f32)], axis=0)
    line = lax.broadcasted_iota(jnp.int32, (16, r), 0)
    for k in range(-(-cb // r)):
        wide = min(r, cb - k * r)
        piece = col[:, k * r : k * r + wide]
        if wide < r:
            piece = jnp.concatenate([piece, jnp.zeros((1, r - wide), f32)], axis=1)
        tile = jnp.where(line == 6 + k, piece, tile)
    tile = jnp.concatenate([tile, jnp.zeros((16, 128 - r), f32)], axis=1)
    own = pl.multiple_of(dp * 32, 32)
    table[t, pl.ds(own, 16), :] = tile.astype(bf16)
    table[t, pl.ds(pl.multiple_of(own + 16, 16), 16), :] = jnp.zeros((16, 128), bf16)
    w1[t, at, :] = up[...].astype(bf16)
    w2[t, at, :] = down[...].astype(bf16)


def loss_pull(pooled, groups, index):
    count = pooled.shape[0]
    inv = lax.rsqrt(jnp.sum(pooled * pooled, axis=1, keepdims=True) + eps_norm)
    unit = pooled * inv
    similar = temper * lax.dot_general(unit, unit, (((1,), (1,)), ((), ())), precision=highest, preferred_element_type=f32)
    rows = lax.broadcasted_iota(jnp.int32, (count, count), 0)
    cols = lax.broadcasted_iota(jnp.int32, (count, count), 1)
    others = jnp.where(rows == cols, masked, similar)
    members = groups.astype(f32)
    eye = jnp.where(rows == cols, 1.0, 0.0).astype(bf16)
    turned = nt(eye, members.astype(bf16))

    def pull(table, axis):
        top = jnp.max(others, axis=axis, keepdims=True)
        e = jnp.exp(others - top)
        return e / jnp.sum(e, axis=axis, keepdims=True) - table / jnp.sum(table, axis=axis, keepdims=True)

    both = temper * (pull(members, 1) + pull(turned, 0))
    grad = lax.dot_general(both, unit, (((1,), (0,)), ((), ())), precision=highest, preferred_element_type=f32)
    own = lax.broadcasted_iota(jnp.int32, (count, 1), 0) == index

    def pick(v):
        return jnp.sum(jnp.where(own, v, 0.0), axis=0, keepdims=True)

    unit, grad = pick(unit), pick(grad)
    return pick(inv) * (grad - unit * jnp.sum(unit * grad, axis=1, keepdims=True))


def forward_kernel(n, cb, comm, *refs):
    dp = 2 * n
    r = D // dp
    given, refs = (6, refs[:2] + refs[2:]) if comm else (4, refs)
    len_ref, groups_ref, x_ref = refs[:3]
    weights_in, refs = refs[3 : 3 + given], refs[3 + given :]
    (rstd1_ref, rstd2_ref, gain_ref, row_ref, hb_ref, u_ref,
     out_out, h1_out, xhat1_out, g_out, xhat2_out, ct_out, xt_out, gp_out, q_out, k_out, v_out, wa_out, w1_out, w2_out,
     out_ref, h1_ref, xhat1_ref, g_ref, xhat2_ref, ct_ref, xt,
     wa, w1, w2, table, bcol, col, qt, kt, vt, kn, sb, wo, pool, stage, every, pooled,
     local, q_sem, stage_sem, o_sem, *sems) = refs
    length = len_ref[0]
    hooks, middle, late = {}, [], {}
    if comm:
        p = Place(n)
        pack(weights_in, wa, table, w1, w2, p, r, cb)
        enter(p)
        wholes = [wa.at[j] for j in range(NJ)] + [table, w1, w2, every]
        straight = (False,) * NJ + (True, False, False, True)
        a0, a1, a2, bias, up, down, pools = [Gather(p, i, full, sems, way) for i, (full, way) in enumerate(zip(wholes, straight))]
        parts = (a0, a1, a2, bias, up, down)
        flows = [[g.start] + g.flow() for g in parts]

        def steps(pairs):
            return [flows[g][k] for g, k in pairs]

        if n == 4:
            run(steps(PRE[:5]))
            xt[...] = x_ref[...].T
            run(steps(PRE[5:]))
            hooks = {h: steps(pairs) for h, pairs in HEAD.items()}
            middle = steps(MID)
            late = {h: steps(pairs) for h, pairs in LATE.items()}
        else:
            xt[...] = x_ref[...].T
            for group in zip(*flows):
                run(group)
    else:
        loads = [pltpu.make_async_copy(src, dst, local.at[i]) for i, (src, dst) in enumerate(zip(weights_in, (wa, table, w1, w2)))]
        for cp in loads:
            cp.start()
        xt[...] = x_ref[...].T
        for cp in loads:
            cp.wait()
    saved = ((out_ref, out_out), (h1_ref, h1_out), (xhat1_ref, xhat1_out), (g_ref, g_out), (xhat2_ref, xhat2_out), (ct_ref, ct_out),
             (xt, xt_out), (wa, wa_out), (w1, w1_out), (w2, w2_out))

    def save(i):
        return pltpu.make_async_copy(*saved[i], o_sem.at[i])

    save(6).start()

    col_rows = -(-cb // r)
    for i in range(dp):
        rows = slice(i * 32, i * 32 + 16)
        row_ref[:, i * r : i * r + r] = table[0, rows, 0:r].astype(f32)
        for t in range(NT):
            tile = table[t, rows, :].astype(f32)
            for k in range(col_rows):
                wide = min(r, cb - k * r)
                col[t, :, i * cb + k * r : i * cb + k * r + wide] = jnp.broadcast_to(tile[6 + k : 7 + k, 0:wide], (8, wide))
    for t in range(NT):
        bcol[t] = jnp.transpose(col[t, :, 0 : 2 * HC])[:, 0:1]
        hb_ref[t] = col[t, 0:1, 2 * HC : 2 * HC + D]

    ones = jnp.ones((1, LEN), f32)
    where = lax.broadcasted_iota(jnp.int32, (1, LEN), 1)
    key_bias = jnp.where(where < length, 0.0, masked).astype(f32)
    kept = ((qt, q_out), (kt, k_out), (vt, v_out))
    key_rows = aug_rows(key_bias, ones, ones, ones)
    one_row = aug_rows(ones)
    half = LEN // 2

    def project(h):
        j, t = h // NT, h % NT
        qkv = tn(wa[j, t, :, 0 : 3 * HD], xt[...])
        qt[h, 0:HD, :] = ((qkv[0:HD] + bcol[t, pl.ds(pl.multiple_of(j * HD, HD), HD), :]) * HD**-0.5).astype(bf16)
        kt[h, 0:HD, :] = qkv[HD : 2 * HD].astype(bf16)
        vt[h] = (qkv[2 * HD : 3 * HD] + bcol[t, pl.ds(pl.multiple_of(HC + j * HD, HD), HD), :]).astype(bf16)
        qt[h, HD:AUG, :] = one_row
        kt[h, HD:AUG, :] = key_rows
        kn[h % 2] = kt[h].T

    def attend(h, i, s):
        where = slice(i * half, i * half + half)
        top = jnp.max(s, axis=0, keepdims=True)
        e = jnp.exp(s - top)
        total = jnp.sum(e, axis=0, keepdims=True)
        ct_ref[pl.ds(pl.multiple_of(h * HD, HD), HD), where] = (nn(vt[h], e.astype(bf16)) * (1.0 / total)).astype(bf16)
        hi, mid, lo = split3(-(top + jnp.log(total)))
        qt[h, HD:AUG, where] = aug_rows(ones[:, where], hi, mid, lo)

    project(0)
    sb[0] = nn(kn[0], qt[0, :, 0:half])

    def head(h, _):
        after = nn(kn[h % 2], qt[h, :, half:LEN])
        attend(h, 0, sb[0])
        sb[1] = after
        nxt = jnp.minimum(h + 1, H - 1)

        @pl.when(h + 1 < H)
        def _():
            project(nxt)

        after = nn(kn[nxt % 2], qt[nxt, :, 0:half])
        attend(h, 1, sb[1])
        sb[0] = after
        for i, (src, dst) in enumerate(kept):
            pltpu.make_async_copy(src.at[h], dst.at[h], q_sem.at[i, h]).start()
        at_step(h, hooks)
        return 0

    lax.fori_loop(0, H, head, 0)
    save(5).start()

    c_nat = out_ref
    c_nat[...] = ct_ref[...].T
    for j in range(NJ):
        for t in range(NT):
            h = j * NT + t
            wo[:, h * HD : h * HD + HD] = wa[j, t, :, 3 * HD : 4 * HD]
    save(7).start()

    def first(i, _):
        s = pl.ds(pl.multiple_of(i * ROWS, ROWS), ROWS)
        r1 = x_ref[s, :].astype(f32) + (nt(c_nat[s, :], wo[...]) + row_ref[0:1])
        xhat, rstd = norm(r1)
        xhat1_ref[s, :] = xhat
        rstd1_ref[s, :] = rstd
        h1_ref[s, :] = (xhat * row_ref[1:2] + row_ref[2:3]).astype(bf16)
        return 0

    lax.fori_loop(0, CHUNKS, first, 0)
    save(1).start()
    save(2).start()
    run(middle)

    def staged(step):
        t, i = step // CHUNKS, step % CHUNKS
        s = pl.ds(pl.multiple_of(i * ROWS, ROWS), ROWS)
        return pltpu.make_async_copy(stage.at[step % 2], gp_out.at[t, s, :], stage_sem.at[step % 2])

    def hidden(step, _):
        t, i = step // CHUNKS, step % CHUNKS
        s = pl.ds(pl.multiple_of(i * ROWS, ROWS), ROWS)
        z = nn(h1_ref[s, :], w1[t]) + hb_ref[t]
        cdf = 0.5 + 0.5 * lax.erf(z * 0.5**0.5)
        g_ref[t, s, :] = (z * cdf).astype(bf16)

        @pl.when(step >= 2)
        def _():
            staged(step - 2).wait()

        stage[step % 2] = cdf + z * (jnp.exp(-0.5 * z * z) * 0.3989422804014327)
        staged(step).start()
        at_step(step, late)
        return 0

    lax.fori_loop(0, NT * CHUNKS, hidden, 0)
    staged(NT * CHUNKS - 2).wait()
    staged(NT * CHUNKS - 1).wait()
    for i in (3, 8, 9):
        save(i).start()
    gain_ref[...] = jnp.zeros_like(gain_ref)
    pool[...] = jnp.zeros_like(pool)

    def second(i, _):
        s = pl.ds(pl.multiple_of(i * ROWS, ROWS), ROWS)
        res = xhat1_ref[s, :] * row_ref[1:2] + row_ref[2:3] + row_ref[3:4]
        for t in range(NT):
            res = res + nt(g_ref[t, s, :], w2[t])
        xhat, rstd = norm(res)
        xhat2_ref[s, :] = xhat
        rstd2_ref[s, :] = rstd
        y = xhat * row_ref[4:5] + row_ref[5:6]
        out_ref[s, :] = y.astype(bf16)
        here = i * ROWS + lax.broadcasted_iota(jnp.int32, (ROWS, 1), 0) < length
        pool[0:1] += jnp.sum(jnp.where(here, y, 0.0), axis=0, keepdims=True)
        gain_ref[...] += jnp.sum(jnp.where(here, xhat, 0.0), axis=0, keepdims=True)
        return 0

    lax.fori_loop(0, CHUNKS, second, 0)
    size = jnp.full((1, 1), length).astype(f32)
    mean = pool[0:1] / size
    if comm:
        block = [mean[:, i * 128 : i * 128 + 128] for i in range(D // 128)] + [jnp.zeros((16 - D // 128, 128), f32)]
        every[p.y * 2 + p.c, pl.ds(pl.multiple_of((p.z * 2 + p.x) * 16, 16), 16), :] = jnp.concatenate(block, axis=0)
        pools.start()
    save(0).start()
    save(4).start()
    if comm:
        run(pools.flow())
        for i in range(dp):
            for t in range(NT):
                for k in range(D // 128):
                    pooled[i * NT + t : i * NT + t + 1, k * 128 : k * 128 + 128] = every[t, i * 16 + k : i * 16 + k + 1, :]
        u_ref[...] = loss_pull(pooled[...], groups_ref[...], lax.axis_index("dp") * NT + lax.axis_index("tensor")) / size
        for g in parts + (pools,):
            g.finish()
    else:
        u_ref[...] = mean
    for h in range(H):
        for i, (src, dst) in enumerate(kept):
            pltpu.make_async_copy(src.at[h], dst.at[h], q_sem.at[i, h]).wait()
    for i in range(len(saved)):
        save(i).wait()


def forward(length, groups, x, weights, n, cb, comm):
    s = jax.ShapeDtypeStruct
    dp = 2 * n
    r = D // dp
    dma = pltpu.SemaphoreType.DMA
    shapes = [s((LEN, 1), f32), s((LEN, 1), f32), s((1, D), f32), s((16, D), f32), s((NT, 1, D), f32), s((1, D), f32)]
    big = [s((LEN, D), bf16), s((LEN, D), bf16), s((LEN, D), f32), s((NT, LEN, D), bf16), s((LEN, D), f32), s((D, LEN), bf16), s((D, LEN), bf16)]
    kept = [
        s((NT, LEN, D), f32), s((H, AUG, LEN), bf16), s((H, AUG, LEN), bf16), s((H, HD, LEN), bf16),
        s((NJ, NT, D, 4 * HD), bf16), s((NT, D, D), bf16), s((NT, D, D), bf16),
    ]
    scratch = [pltpu.VMEM(v.shape, v.dtype) for v in big] + [
        pltpu.VMEM((NJ, NT, D, 4 * HD), bf16), pltpu.VMEM((NT, D, D), bf16), pltpu.VMEM((NT, D, D), bf16),
        pltpu.VMEM((NT, dp * 32, 128), bf16), pltpu.VMEM((NT, 2 * HC, 1), f32), pltpu.VMEM((NT, 8, dp * cb), f32),
        pltpu.VMEM((H, AUG, LEN), bf16), pltpu.VMEM((H, AUG, LEN), bf16), pltpu.VMEM((H, HD, LEN), bf16),
        pltpu.VMEM((2, LEN, AUG), bf16), pltpu.VMEM((2, LEN, LEN // 2), f32),
        pltpu.VMEM((D, D), bf16), pltpu.VMEM((8, D), f32), pltpu.VMEM((2, ROWS, D), f32),
        pltpu.VMEM((NT, dp * 16, 128), f32), pltpu.VMEM((dp * NT, D), f32),
        dma((PARTS,)), dma((3, H)), dma((2,)), dma((len(big) + 3,)),
    ]
    if comm:
        scratch += gather_sems(PARTS, n)
        params = pltpu.CompilerParams(collective_id=0, has_side_effects=True, vmem_limit_bytes=VMEM_CAP)
    else:
        params = pltpu.CompilerParams(vmem_limit_bytes=VMEM_CAP)
    return pl.pallas_call(
        functools.partial(forward_kernel, n, cb, comm),
        out_shape=shapes + big + kept,
        in_specs=[pl.BlockSpec(memory_space=pltpu.SMEM)] + vmem_spec(2) + (vmem_spec(6) if comm else any_spec(4)),
        out_specs=vmem_spec(len(shapes)) + any_spec(len(big) + len(kept)),
        scratch_shapes=scratch,
        compiler_params=params,
    )(length, groups, x, *weights)


def backward_kernel(n, cb, comm, *refs):
    dp = 2 * n
    r = D // dp
    (len_ref, u_ref, gain_ref, rstd1_ref, rstd2_ref, row_ref,
     xhat2_in, xhat1_in, w1_in, w2_in, wa_in, g_in, gp_in, h1_in, ct_in, xt_in, q_in, k_in, v_in, *refs) = refs
    dx_out, *refs = refs
    outs, refs = refs[: NJ + 3], refs[NJ + 3 :]
    landing, refs = (refs[: NJ + 3], refs[NJ + 3 :]) if comm else ([], refs)
    (wa, w1, w2, t1, t2, dqkv, xt, ct, df, dz, dh, sd, pp, turned, qkv, wcat, grow, ghb, gcol, gbias,
     load, s_load, q_sem, x_sem, *refs) = refs
    length = len_ref[0]
    hooks, after, ends = {}, {}, {}
    grads = [wa.at[j] for j in range(NJ)]
    h1t, dft, dat, dct = t1, t2, t1, t2

    loads = [
        pltpu.make_async_copy(src, dst, load.at[i])
        for i, (src, dst) in enumerate(
            ((xhat2_in, sd.at[1, :, 0:D]), (w2_in, w2), (h1_in, dz), (w1_in, w1), (wa_in, wa), (ct_in, ct), (xt_in, xt))
        )
    ]

    def fetch(step):
        t = part_of(step)
        return [
            pltpu.make_async_copy(src.at[t], dst.at[step % 2, :, 0:D], s_load.at[step % 2, i])
            for i, (src, dst) in enumerate(((g_in, pp), (gp_in, sd)))
        ]

    if comm:
        p = Place(n)

        def part_of(step):
            first = jnp.where(step < 2, 1 - p.y, p.y)
            return first * 2 + step % 2
    else:

        def part_of(step):
            return step

    for cp in loads[:2]:
        cp.start()
    for cp in fetch(0):
        cp.start()
    for cp in loads[2:]:
        cp.start()
    if comm:
        temp = wcat
        bufs, sems = refs[:-8], refs[-8:]
        enter(p)
        where = [(lambda t: w1.at[t]), (lambda t: w2.at[t])] + [(lambda t, g=g: g.at[t]) for g in grads] + [lambda t: gbias.at[t]]
        parts = []
        for i, source in enumerate(where):
            rows, width = outs[i].shape
            parts.append(
                Scatter(p, i, rows, source, outs[i], [landing[i]] + list(bufs[3 * i : 3 * i + 3]),
                        temp.at[0 : 2 * n * rows, 0:width], x_sem.at[0], sems)
            )
        up, down, a0, a1, a2, bias = parts

        def call(*pairs):
            return [functools.partial(f, *args) for f, *args in pairs]

        after = {
            1: call((up.core, 0), (down.core, 0)),
            2: call((up.add, 0), (up.corner,), (down.add, 0), (down.corner,)),
            3: call((up.core, 1), (down.core, 1)),
        }
        hooks = {
            0: call((down.cross,)), 3: call((a0.core, 0), (a0.core, 1)), 4: call((up.line,)),
            5: call((a0.add, 0), (a0.corner,), (a0.add, 1)), 6: call((down.line,)), 7: call((a1.core, 0), (a1.core, 1), (a0.cross,)),
            8: call((up.last,)), 9: call((a1.add, 0), (a1.corner,), (a1.add, 1), (a0.line,)), 10: call((down.last,)),
            11: call((a1.cross,), (a2.core, 0), (a2.core, 1)),
        }

    u = u_ref[...]
    du = u * row_ref[4:5]
    mean_du = jnp.mean(du, axis=1, keepdims=True)
    grow[...] = jnp.zeros_like(grow)
    loads[0].wait()

    def outer(i, _):
        s = pl.ds(pl.multiple_of(i * ROWS, ROWS), ROWS)
        here = i * ROWS + lax.broadcasted_iota(jnp.int32, (ROWS, 1), 0) < length
        hat = sd[1, s, 0:D]
        dot = jnp.mean(hat * du, axis=1, keepdims=True)
        dr = jnp.where(here, rstd2_ref[s, :] * (du - mean_du - hat * dot), 0.0)
        dh[s, :] = dr
        low = dr.astype(bf16)
        df[s, :] = low
        grow[3:4] += jnp.sum(low.astype(f32), axis=0, keepdims=True)
        return 0

    lax.fori_loop(0, CHUNKS, outer, 0)
    grow[4:5] = u * gain_ref[...]
    grow[5:6] = u * jnp.full((1, 1), length).astype(f32)
    dft[...] = df[...].T
    loads[2].wait()
    h1t[...] = dz[...].T
    last_hat = pltpu.make_async_copy(xhat1_in, sd.at[0, :, 0:D], load.at[0])
    loads[1].wait()
    loads[3].wait()

    def hidden(step, _):
        t = part_of(step)
        slot = step % 2
        for cp in fetch(step):
            cp.wait()

        @pl.when(step + 1 < NT)
        def _():
            for cp in fetch(step + 1):
                cp.start()

        hb = jnp.zeros((1, D), f32)
        for i in range(CHUNKS):
            s = pl.ds(i * ROWS, ROWS)
            low = (nn(df[s, :], w2[t]) * sd[slot, s, 0:D]).astype(bf16)
            dz[s, :] = low
            hb = hb + jnp.sum(low.astype(f32), axis=0, keepdims=True)
            dh[s, :] += nt(low, w1[t])
        ghb[t] = hb
        for i in range(D // ROWS):
            s = slice(i * ROWS, (i + 1) * ROWS)
            w1[t, s, :] = nn(h1t[s, :], dz[...]).astype(bf16)
            w2[t, s, :] = nn(dft[s, :], pp[slot, :, 0:D]).astype(bf16)
        pl.when(step == NT - 2)(last_hat.start)
        at_step(step, after)
        return 0

    lax.fori_loop(0, NT, hidden, 0)

    def fetch_head(h, slot):
        return [
            pltpu.make_async_copy(src.at[h], qkv.at[slot, i, 0 : src.shape[1], :], q_sem.at[slot, i])
            for i, src in enumerate((q_in, k_in, v_in))
        ]

    for cp in fetch_head(0, 0):
        cp.start()
    last_hat.wait()

    def inner_norm(i, _):
        s = pl.ds(pl.multiple_of(i * ROWS, ROWS), ROWS)
        d = dh[s, :]
        hat = sd[0, s, 0:D]
        grow[1:2] += jnp.sum(d * hat, axis=0, keepdims=True)
        grow[2:3] += jnp.sum(d, axis=0, keepdims=True)
        dn = d * row_ref[1:2]
        dr = rstd1_ref[s, :] * (dn - jnp.mean(dn, axis=1, keepdims=True) - hat * jnp.mean(dn * hat, axis=1, keepdims=True))
        dh[s, :] = dr
        low = dr.astype(bf16)
        grow[0:1] += jnp.sum(low.astype(f32), axis=0, keepdims=True)
        df[s, :] = low
        return 0

    lax.fori_loop(0, CHUNKS, inner_norm, 0)
    dat[...] = df[...].T
    if comm:
        run(call((up.add, 1), (down.add, 1), (up.cross,)))
    loads[4].wait()
    loads[5].wait()
    for j in range(NJ):
        for t in range(NT):
            h = j * NT + t
            wcat[:, h * HD : h * HD + HD] = wa[j, t, :, 3 * HD : 4 * HD]
    for i in range(D // ROWS):
        s = slice(i * ROWS, (i + 1) * ROWS)
        dct[s, :] = tn(wcat[:, s], dat[...]).astype(bf16)
        gwo = nt(dat[s, :], ct[...]).astype(bf16)
        for j in range(NJ):
            for t in range(NT):
                h = j * NT + t
                wa[j, t, s, 3 * HD : 4 * HD] = gwo[:, h * HD : h * HD + HD]
    loads[6].wait()

    def head(h, _):
        j, t = h // NT, h % NT
        slot = h % 2
        for cp in fetch_head(h, slot):
            cp.wait()

        @pl.when(h + 1 < H)
        def _():
            for cp in fetch_head(h + 1, 1 - slot):
                cp.start()

        own = pl.ds(pl.multiple_of(h * HD, HD), HD)
        prob = jnp.exp(tn(qkv[slot, 0], qkv[slot, 1]))
        sd[0] = prob
        sd[1] = tn(dct[own, :], qkv[slot, 2, 0:HD, :])
        pp[0] = prob.astype(bf16)
        inner = jnp.sum(sd[0] * sd[1], axis=1, keepdims=True)
        pp[1] = (sd[0] * (sd[1] - inner)).astype(bf16)
        turned[...] = pp[1].T
        at = pl.multiple_of(t * 3 * HD, HD)
        dqkv[pl.ds(at + HD, HD), :] = nn(qkv[slot, 0, 0:HD, :], pp[1]).astype(bf16)
        dqkv[pl.ds(at + 2 * HD, HD), :] = nn(dct[own, :], pp[0]).astype(bf16)
        dqkv[pl.ds(at, HD), :] = (nn(qkv[slot, 1, 0:HD, :], turned[...]) * HD**-0.5).astype(bf16)

        @pl.when(t == NT - 1)
        def _():
            for k in range(NT):
                wcat[:, k * 3 * HD : (k + 1) * 3 * HD] = wa[j, k, :, 0 : 3 * HD]
            sums = nt(jnp.ones((16, LEN), bf16), dqkv[...])
            for k in range(NT):
                gcol[j, k] = sums[0:8, k * 3 * HD : (k + 1) * 3 * HD]
            for i in range(D // ROWS):
                s = slice(i * ROWS, (i + 1) * ROWS)
                g = nt(xt[s, :], dqkv[...]).astype(bf16)
                for k in range(NT):
                    wa[j, k, s, 0 : 3 * HD] = g[:, k * 3 * HD : (k + 1) * 3 * HD]
            for i in range(CHUNKS):
                s = slice(i * ROWS, (i + 1) * ROWS)
                dh[s, :] += lax.dot_general(dqkv[:, s], wcat[...], (((0,), (1,)), ((), ())), preferred_element_type=f32)

        at_step(h, hooks)
        return 0

    lax.fori_loop(0, H, head, 0)
    dx = pltpu.make_async_copy(dh, dx_out, load.at[0])
    dx.start()

    col_rows = -(-cb // r)
    cols = []
    for t in range(NT):
        pieces = [gcol[j, t, 0:1, 0:HD] for j in range(NJ)] + [gcol[j, t, 0:1, 2 * HD : 3 * HD] for j in range(NJ)]
        cols.append(jnp.concatenate(pieces + [ghb[t]], axis=1))
    at = lax.broadcasted_iota(jnp.int32, (32, 128), 0)
    for i in range(dp):
        rows = jnp.pad(grow[0:8, i * r : i * r + r], ((0, 24), (0, 128 - r)))
        for t in range(NT):
            block = jnp.where(at < 6, rows, 0.0)
            for k in range(col_rows):
                wide = min(r, cb - k * r)
                piece = cols[t][:, i * cb + k * r : i * cb + k * r + wide]
                block = jnp.where(at == 6 + k, jnp.pad(piece, ((0, 0), (0, 128 - wide))), block)
            gbias[t, i * 32 : i * 32 + 32, :] = block.astype(bf16)
    if comm:
        run(call(
            (bias.core, 0), (bias.core, 1), (a2.add, 0), (a2.corner,), (bias.add, 0), (bias.corner,), (a2.add, 1), (bias.add, 1),
            (a0.last,), (a1.line,), (a2.cross,), (bias.cross,), (a1.last,), (a2.line,), (bias.line,), (a2.last,), (bias.last,),
        ))
        for part in parts:
            part.finish()
    else:
        copies = [pltpu.make_async_copy(src, dst, load.at[1 + i]) for i, (src, dst) in enumerate(zip([w1, w2] + grads + [gbias], outs))]
        for cp in copies:
            cp.start()
        for cp in copies:
            cp.wait()
    dx.wait()


def backward(length, u, gain, rstd1, rstd2, row, big, n, cb, comm):
    s = jax.ShapeDtypeStruct
    dp = 2 * n
    r = D // dp
    dma = pltpu.SemaphoreType.DMA
    widths = [(r, D), (r, D)] + [(r, 4 * HD)] * NJ + [(32, 128)]
    if comm:
        sums = [s(shape, f32) for shape in widths]
        landing = [s((2, dp * rows, wide), bf16) for rows, wide in widths]
        specs = vmem_spec(len(sums)) + any_spec(len(landing))
    else:
        sums = [s((NT, dp * rows, wide), bf16) for rows, wide in widths]
        landing = []
        specs = any_spec(len(sums))
    turned = pltpu.VMEM((D, LEN), bf16)
    rows_low = pltpu.VMEM((LEN, D), bf16)
    rows_full = pltpu.VMEM((LEN, D), f32)
    scratch = [
        pltpu.VMEM((NJ, NT, D, 4 * HD), bf16), pltpu.VMEM((NT, D, D), bf16), pltpu.VMEM((NT, D, D), bf16),
        turned, turned, turned, turned, turned, rows_low, rows_low, rows_full,
        pltpu.VMEM((2, LEN, LEN), f32), pltpu.VMEM((2, LEN, LEN), bf16), pltpu.VMEM((LEN, LEN), bf16), pltpu.VMEM((2, 3, AUG, LEN), bf16), pltpu.VMEM((D, D), bf16),
        pltpu.VMEM((16, D), f32), pltpu.VMEM((NT, 1, D), f32), pltpu.VMEM((NJ, NT, 8, 3 * HD), f32), pltpu.VMEM((NT, dp * 32, 128), bf16),
        dma((8,)), dma((2, 2)), dma((2, 3)), dma((1,)),
    ]
    if comm:
        for rows, wide in widths:
            scratch += scatter_bufs(n, rows, wide)
        scratch += scatter_sems(len(widths), n)
        params = pltpu.CompilerParams(collective_id=1, has_side_effects=True, vmem_limit_bytes=VMEM_CAP)
    else:
        params = pltpu.CompilerParams(vmem_limit_bytes=VMEM_CAP)
    return pl.pallas_call(
        functools.partial(backward_kernel, n, cb, comm),
        out_shape=[s((LEN, D), f32)] + sums + landing,
        in_specs=[pl.BlockSpec(memory_space=pltpu.SMEM)] + vmem_spec(5) + any_spec(len(big)),
        out_specs=any_spec(1) + specs,
        scratch_shapes=scratch,
        compiler_params=params,
    )(length, u, gain, rstd1, rstd2, row, *big)


def adam_kernel(cb, *refs):
    moved, sums, old, refs = refs[:2], refs[2:8], refs[8:32], refs[32:]
    landed, new, held, sem = refs[:2], refs[2:26], refs[26:28], refs[28]
    inward = [pltpu.make_async_copy(src, dst, sem.at[i]) for i, (src, dst) in enumerate(zip(moved, held))]
    outward = [pltpu.make_async_copy(src, dst, sem.at[i]) for i, (src, dst) in enumerate(zip(held, landed))]
    for cp in inward:
        cp.start()
    gw1, gw2, ga, gbias = sums[0], sums[1], sums[2:5], sums[5]
    r = gw1.shape[0]

    def wide(k):
        return jnp.concatenate([ga[j][:, k * HD : k * HD + HD] for j in range(NJ)], axis=1)

    def update(i, grad, rate, at=()):
        where = at + (Ellipsis,)
        out = adam_update(*[old[4 * i + k][where] for k in range(4)], grad, rate)
        for k, v in enumerate(out):
            new[4 * i + k][where] = v

    for k in range(3):
        update(0, wide(k), D ** (-0.5), (k,))
    high = -(-r // 128) * 128
    turned = jnp.concatenate([wide(3), jnp.zeros((r, 256 - HC), f32)], axis=1)
    if high > r:
        turned = jnp.concatenate([turned, jnp.zeros((high - r, 256), f32)], axis=0)
    update(1, turned.T[0:HC, 0:r], D ** (-0.5))
    for one, two in zip(inward, outward):
        one.wait()
        two.start()
    update(2, gw1[...], D ** (-0.5))
    update(3, gw2[...], FF ** (-0.5))
    rows = gbias[...]
    pieces = [rows[6 + k : 7 + k, 0 : min(r, cb - k * r)] for k in range(-(-cb // r))]
    update(4, jnp.concatenate(pieces, axis=1), 0.1)
    update(5, rows[0:6, 0:r], 0.15)
    for cp in outward:
        cp.wait()


def adam(moved, sums, olds, cb):
    flat = [v for group in olds for v in group]
    s = jax.ShapeDtypeStruct
    shapes = [s(group[0].shape, f32) for group in olds for _ in range(4)]
    return pl.pallas_call(
        functools.partial(adam_kernel, cb),
        out_shape=[s(v.shape, v.dtype) for v in moved] + shapes,
        in_specs=any_spec(2) + vmem_spec(6 + 24),
        out_specs=any_spec(2) + vmem_spec(24),
        scratch_shapes=[pltpu.VMEM(v.shape, v.dtype) for v in moved] + [pltpu.SemaphoreType.DMA((2,))],
        compiler_params=pltpu.CompilerParams(vmem_limit_bytes=VMEM_CAP),
    )(*moved, *sums, *flat)


def gather_plain(own):
    return lax.all_gather(lax.all_gather(own, "dp", axis=0, tiled=True), "tensor", axis=0)


def scatter_plain(full):
    own = lax.psum_scatter(full.astype(f32), "tensor", scatter_dimension=0, tiled=False)
    return lax.psum_scatter(own, "dp", scatter_dimension=0, tiled=True)


def by_head(wide):
    return jnp.moveaxis(wide.reshape(*wide.shape[:-1], NJ, HD), -2, 0)


def packed(qkv_weight, out_weight, up_weight, down_weight, col_bias, row_params, r, cb):
    own_a = jnp.concatenate([by_head(qkv_weight[i]) for i in range(3)] + [by_head(out_weight.T)], axis=-1).astype(bf16)
    col_rows = -(-cb // r)
    col_pad = jnp.pad(col_bias[0], (0, col_rows * r - cb)).reshape(col_rows, r)
    own_b = jnp.pad(jnp.concatenate([row_params, col_pad], axis=0), ((0, 26 - col_rows), (0, 128 - r))).astype(bf16)
    return own_a, own_b, up_weight.astype(bf16), down_weight.T.astype(bf16)


def on_device(
    inputs, lengths, groups, qkv_weight, out_weight, up_weight, down_weight, col_bias, row_params,
    qkv_first, out_first, up_first, down_first, col_first, row_first,
    qkv_second, out_second, up_second, down_second, col_second, row_second,
    qkv_ema, out_ema, up_ema, down_ema, col_ema, row_ema,
):
    dp = lax.axis_size("dp")
    n = dp // 2
    r = D // dp
    cb = col_bias.shape[1]
    length = lax.dynamic_slice_in_dim(lengths, lax.axis_index("tensor"), 1)
    comm = r % 32 == 0
    if comm:
        weights = (qkv_weight, out_weight, up_weight, down_weight.T, col_bias, row_params)
    else:
        own_a, *others = packed(qkv_weight, out_weight, up_weight, down_weight, col_bias, row_params, r, cb)
        own_b, own_1, own_2 = [gather_plain(v) for v in others]
        weights = (jnp.stack([gather_plain(own_a[j]) for j in range(NJ)]), own_b, own_1, own_2)
    (rstd1, rstd2, gain, row, hb, u, outputs, h1, xhat1, g, xhat2, ct, xt, gp, qt, kt, vt, wa, w1, w2) = forward(
        length, groups, inputs, weights, n, cb, comm
    )
    if not comm:
        every = lax.all_gather(u, ("dp", "tensor"), axis=0, tiled=True)
        u = loss_pull(every, groups, lax.axis_index(("dp", "tensor"))) / length[0].astype(f32)

    big = (xhat2, xhat1, w1, w2, wa, g, gp, h1, ct, xt, qt, kt, vt)
    input_grad, *sums = backward(length, u, gain, rstd1, rstd2, row, big, n, cb, comm)
    sums = sums[: NJ + 3] if comm else [scatter_plain(v) for v in sums]
    olds = (
        (qkv_weight, qkv_first, qkv_second, qkv_ema),
        (out_weight, out_first, out_second, out_ema),
        (up_weight, up_first, up_second, up_ema),
        (down_weight.T, down_first.T, down_second.T, down_ema.T),
        (col_bias, col_first, col_second, col_ema),
        (row_params, row_first, row_second, row_ema),
    )
    outputs, input_grad, *new = adam((outputs, input_grad), sums, olds, cb)
    new[12:16] = [v.T for v in new[12:16]]
    return (outputs, input_grad, *new)


def solution(mesh):
    tokens = P(("dp", "tensor"), None)
    placed = (P(None, "dp", "tensor"), P("tensor", "dp"), P("dp", "tensor"), P("tensor", "dp"), P("tensor", "dp"), P(None, "dp"))
    new = tuple(spec for spec in placed for _ in range(4))
    return jax.shard_map(
        on_device,
        mesh=mesh,
        in_specs=(tokens, P("dp"), P()) + placed * 4,
        out_specs=(tokens, tokens) + new,
        check_vma=False,
    )
```

time: 255 us -> 244 us (0.957)
  Pallas kernels: 248 us -> 241 us
  local copies, waits for them, and re-layouts: 5.56 us -> 1.24 us
    pallas_call x2 -> x1, Pallas kernels: 35.8 us -> 8.54 us  [adam(): pl.pallas_call(functools.partial(adam_kernel, cb), out_shape=[s(v.shape,...]
    pallas_call x1, Pallas kernels: 95.1 us -> 119 us  [backward(): pl.pallas_call(functools.partial(backward_kernel, n, cb, comm), out_shape...]
    unnamed x4 -> x0, local copies, waits for them, and re-layouts: 4.32 us -> none
    pallas_call x1, Pallas kernels: 118 us -> 114 us  [forward(): pl.pallas_call(functools.partial(forward_kernel, n, cb, comm), out_shape=...]
where the time goes in v3:
time: 244 us; the launch traced here: 243 us
  Pallas kernels  241 us (99%)
    pallas_call x1, Pallas kernels, backward(): pl.pallas_call(functools.partial(backward_kernel, n, cb, comm), out_shape...  119 us
    pallas_call x1, Pallas kernels, forward(): pl.pallas_call(functools.partial(forward_kernel, n, cb, comm), out_shape=...  114 us
    pallas_call x1, Pallas kernels, adam(): pl.pallas_call(functools.partial(adam_kernel, cb), out_shape=[s(v.shape,...  8.54 us

profile of v3, /device:TPU:0, one launch (start us, length us, event | category | flops | bytes accessed | tf_op | source)
XLA Modules:
  0.0 243.4 jit_solution(15328768380358250639)
XLA Ops:
  0.7 1.2 dynamic_slice.3.refs_0_
  1.9 114.1 %shard_map.458 = (f32[1024,1]{1,0:T(8,128)}, f32[1024,1]{1,0:T(8,128)}, f32[1,768]{1,0:T(1,128)}, f32[16,768]{1,0:T(8,128)}, f32[4,1,768]{2,1,0:T(1,128)}, /*ind...) custom-call(s32[1]{0:T(128)} %dynamic_slice.3.refs_0_, ...), custom_call_target="tpu_custom_call" | custom-call | tf_op jit(solution)/shard_map/pallas_call | solution.py:676
  116.0 118.7 %shard_map.459 = (f32[1024,768]{1,0:T(8,128)}, f32[96,768]{1,0:T(8,128)}, f32[96,768]{1,0:T(8,128)}, f32[96,256]{1,0:T(8,128)}, f32[96,256]{1,0:T(8,128)}, /*ind...) custom-call(s32[1]{0:T(128)} %dynamic_slice.3.refs_0_, ...), custom_call_target="tpu_custom_call" | custom-call | tf_op jit(solution)/shard_map/pallas_call | solution.py:971
  234.7 8.5 %shard_map.460 = (bf16[1024,768]{1,0:T(8,128)(2,1)}, f32[1024,768]{1,0:T(8,128)}, f32[3,96,192]{2,1,0:T(8,128)}, f32[3,96,192]{2,1,0:T(8,128)}, f32[3,96,192]{2,...) custom-call(bf16[1024,768]{1,0:T(8,128)(2,1)} %get-tuple-element.78., ...), custom_call_target="tpu_custom_call" | custom-call | tf_op jit(solution)/shard_map/pallas_call | solution.py:1024

commit v4 on v3

--- a/solution.py
+++ b/solution.py
@@ -72,17 +72,31 @@
         return ((self.z + k) % self.depth, self.x, self.y, self.c)
 
 
+    def others(self):
+        return [(z, x, y) for z in range(self.depth) for x in range(2) for y in range(2) if z + x + y > 0]
+
+    def chip(self, z, x, y):
+        return ((self.z + z) % self.depth, (self.x + x) % 2, (self.y + y) % 2, self.c)
+
+
 def device(place):
     z, x, y, c = place
     return (z * 2 + x, y * 2 + c)
 
 
-def enter(p):
+def greet(p, everyone=False):
     bar = pltpu.get_barrier_semaphore()
-    to = [p.over_x, p.over_y, p.over_c] + [p.along_z(k) for k in range(1, p.depth)]
+    if everyone:
+        to = [p.over_c] + [p.chip(*far) for far in p.others()]
+    else:
+        to = [p.over_c, p.over_x, p.over_y] + [p.along_z(k) for k in range(1, p.depth)]
     for place in to:
         pl.semaphore_signal(bar, inc=1, device_id=device(place), device_id_type=MESH)
-    pl.semaphore_wait(bar, len(to))
+    return len(to)
+
+
+def enter(count):
+    pl.semaphore_wait(pltpu.get_barrier_semaphore(), count)
 
 
 def remote(src, dst, send, recv, to):
@@ -228,6 +242,42 @@
                     pl.when(self.p.z == z)(functools.partial(left, self.full.at[0, 0 : count * r, :], self.sz))
 
 
+class Exchange:
+    def __init__(self, p, full, sems):
+        self.p, self.full = p, full
+        self.sent, self.recv, self.core_sent, self.core_recv = sems
+
+    def spot(self, place):
+        z, x, y, c = place
+        return self.full.at[c, pl.ds(pl.multiple_of(((z * 2 + x) * 2 + y) * 8, 8), 8), :]
+
+    def copy(self, i, far):
+        ref = self.spot(self.p.me)
+        return remote(ref, ref, self.sent.at[0], self.recv.at[i], self.p.chip(*far))
+
+    def core_copy(self):
+        ref = self.full.at[self.p.c]
+        return remote(ref, ref, self.core_sent.at[0], self.core_recv.at[0], self.p.over_c)
+
+    def start(self):
+        for i, far in enumerate(self.p.others()):
+            self.copy(i, far).start()
+
+    def finish(self):
+        others = self.p.others()
+        for i, far in enumerate(others):
+            self.copy(i, far).wait_recv()
+        self.core_copy().start()
+        self.core_copy().wait()
+        left = self.full.at[0, 0 : 8 * len(others), :]
+        pltpu.make_async_copy(left, left, self.sent.at[0]).wait()
+
+
+def exchange_sems(n):
+    dma = pltpu.SemaphoreType.DMA
+    return [dma((1,)), dma((4 * n,)), dma((1,)), dma((1,))]
+
+
 def gather_sems(parts, n):
     dma = pltpu.SemaphoreType.DMA
     return [dma((parts, 8 * n)), dma((parts, 2 * n))] + [dma((parts,))] * 5
@@ -255,13 +305,17 @@
     def core(self, k):
         self.core_copy(k).start()
 
+    def pulled(self, k):
+        return pltpu.make_async_copy(self.b_core.at[k], self.temp, self.load)
+
+    def pull(self, k):
+        self.core_copy(k).wait_recv()
+        self.pulled(k).start()
+
     def add(self, k):
         r = self.rows
-        self.core_copy(k).wait_recv()
         slab = self.slab(self.which(k))
-        cp = pltpu.make_async_copy(self.b_core.at[k], self.temp, self.load)
-        cp.start()
-        cp.wait()
+        self.pulled(k).wait()
 
         def one(i, _):
             s = pl.ds(pl.multiple_of(i * r, 16), r)
@@ -285,14 +339,13 @@
         to = p.over_y if way else p.over_x
         return remote(src, self.b_cross.at[way, z], self.sx.at[q], self.rx.at[q, way, z], to)
 
-    def cross(self):
+    def cross(self, z):
+        self.corner_copy(z).wait_recv()
         p = self.p
-        for z in range(p.depth):
-            self.corner_copy(z).wait_recv()
-            slab, s = (self.slab(1 - p.y), self.span(z, p.x)) if (z + self.part) % 2 else (self.slab(p.y), self.span(z, 1 - p.x))
-            slab[s, :] = (slab[s, :].astype(f32) + self.b_corner[z].astype(f32)).astype(bf16)
-            for way in range(2):
-                self.cross_copy(z, way).start()
+        slab, s = (self.slab(1 - p.y), self.span(z, p.x)) if (z + self.part) % 2 else (self.slab(p.y), self.span(z, 1 - p.x))
+        slab[s, :] = (slab[s, :].astype(f32) + self.b_corner[z].astype(f32)).astype(bf16)
+        for way in range(2):
+            self.cross_copy(z, way).start()
 
     def line_copy(self, k):
         p, q = self.p, self.part
@@ -305,12 +358,11 @@
             self.cross_copy(z, way).wait_recv()
         return self.slab(p.y)[self.span(z, p.x), :].astype(f32) + self.b_cross[0, z].astype(f32) + self.b_cross[1, z].astype(f32)
 
-    def line(self):
+    def line(self, k):
         p = self.p
-        for k in range(1, p.depth):
-            z = (p.z + k) % p.depth
-            self.slab(p.y)[self.span(z, p.x), :] = self.column(z).astype(bf16)
-            self.line_copy(k).start()
+        z = (p.z + k) % p.depth
+        self.slab(p.y)[self.span(z, p.x), :] = self.column(z).astype(bf16)
+        self.line_copy(k).start()
 
     def last(self):
         p = self.p
@@ -320,6 +372,15 @@
             total = total + self.b_line[k].astype(f32)
         self.out[...] = total
 
+    def flow(self, early):
+        call, n = functools.partial, self.p.depth
+        core = [call(self.core, 0), call(self.core, 1)]
+        first = [call(self.pull, 0), call(self.add, 0), self.corner]
+        steps = core[:1] + first + core[1:] if early else core + first
+        steps += [call(self.pull, 1), call(self.add, 1)]
+        steps += [call(self.cross, z) for z in range(n)] + [call(self.line, k) for k in range(1, n)]
+        return steps + [self.last]
+
     def finish(self):
         q = self.part
         for ref, sem in ((self.b_core, self.ss), (self.b_corner, self.sc), (self.b_cross, self.sx), (self.b_line.at[1 : self.p.depth], self.sl)):
@@ -371,18 +432,20 @@
 
 def at_step(index, hooks):
     for k, steps in hooks.items():
-        pl.when(index == k)(functools.partial(run, steps))
+        if steps:
+            pl.when(index == k)(functools.partial(run, steps))
 
 
 NJ = HC // HD
 ROWS = 256
 CHUNKS = LEN // ROWS
-PARTS = 7
-
-PRE = ((0, 0), (3, 0), (1, 0), (0, 1), (0, 2), (3, 1), (3, 2), (1, 1), (1, 2), (0, 3), (0, 4), (3, 3), (3, 4), (1, 3), (1, 4), (0, 5), (2, 0), (0, 6), (3, 5), (3, 6), (0, 7), (4, 0), (0, 8), (0, 9), (0, 10), (1, 5), (1, 6), (2, 1), (0, 11), (3, 7), (3, 8), (0, 12), (3, 9), (2, 2), (4, 1), (4, 2), (5, 0), (1, 7), (3, 10), (3, 11), (1, 8), (1, 9), (3, 12), (1, 10), (2, 3), (2, 4))
-HEAD = {2: ((4, 3), (1, 11), (4, 4), (1, 12)), 3: ((2, 5), (2, 6), (5, 1), (5, 2)), 4: ((2, 7), (2, 8), (2, 9), (2, 10)), 6: ((4, 5), (4, 6), (2, 11), (2, 12)), 9: ((4, 7), (4, 8), (4, 9), (4, 10), (5, 3), (5, 4)), 11: ((4, 11),)}
-MID = ((4, 12), (5, 5), (5, 6))
-LATE = {11: ((5, 7), (5, 8), (5, 9), (5, 10)), 15: ((5, 11), (5, 12))}
+PARTS = 6
+
+PRE = ((0, 0), (3, 0), (1, 0), (2, 0), (0, 1), (0, 2), (3, 1), (3, 2), (1, 1), (1, 2), (2, 1), (2, 2), (3, 3), (3, 4), (0, 3), (1, 3), (1, 4), (0, 4), (3, 5), (3, 6), (4, 0), (2, 3), (3, 7), (0, 5), (0, 6), (2, 4), (3, 8), (5, 0), (3, 9), (0, 7), (0, 8), (1, 5), (3, 10), (0, 9), (1, 6), (2, 5), (2, 6), (0, 10), (0, 11), (4, 1), (0, 12), (3, 11), (1, 7), (4, 2), (5, 1), (1, 8), (3, 12), (1, 9), (2, 7), (2, 8))
+HEAD = {0: ((1, 10),), 1: ((1, 11),), 2: ((5, 2), (2, 9), (1, 12), (2, 10)), 3: ((4, 3),), 4: ((4, 4), (2, 11), (5, 3)), 5: ((5, 4),), 6: ((2, 12),), 8: ((4, 5), (4, 6)), 10: ((5, 5),), 11: ((4, 7), (4, 8), (4, 9), (5, 6), (4, 10))}
+MID = ((4, 11), (4, 12))
+LATE = {0: ((5, 7), (5, 8)), 2: ((5, 9), (5, 10)), 8: ((5, 11),), 11: ((5, 12),)}
+BACK = {0: ((0, 0), (1, 0)), 1: ((0, 1),), 2: ((0, 2), (0, 3), (1, 1)), 3: ((1, 2), (1, 3)), 5: ((0, 4),), 6: ((0, 5), (1, 4)), 7: ((0, 6),), 8: ((0, 7), (1, 5)), 9: ((1, 6), (0, 8), (0, 9), (0, 10)), 10: ((2, 0), (2, 1)), 11: ((1, 7),), 12: ((0, 11), (1, 8), (1, 9), (0, 12), (2, 2)), 13: ((1, 10),), 14: ((2, 3), (2, 4), (2, 5), (3, 0), (3, 1)), 15: ((2, 6), (2, 7), (2, 8), (3, 2), (1, 11)), 16: ((1, 12), (3, 3)), 17: ((3, 4), (3, 5)), 18: ((4, 0), (3, 6), (3, 7), (1, 13), (2, 9), (4, 1), (0, 13), (3, 8), (2, 10), (4, 2), (3, 9), (4, 3), (4, 4)), 19: ((2, 11), (3, 10), (4, 5), (5, 0), (2, 12), (2, 13), (5, 1), (4, 6), (5, 2), (4, 7), (5, 3), (5, 4), (4, 8), (3, 11), (5, 5), (4, 9), (1, 14), (4, 10), (3, 12), (5, 6), (5, 7), (3, 13), (5, 8), (4, 11), (5, 9), (5, 10), (4, 12), (4, 13), (0, 14), (2, 14), (5, 11), (3, 14), (5, 12), (5, 13), (4, 14), (5, 14))}
 
 
 def pack(refs, wa, table, w1, w2, p, r, cb):
@@ -450,16 +513,17 @@
      out_ref, h1_ref, xhat1_ref, g_ref, xhat2_ref, ct_ref, xt,
      wa, w1, w2, table, bcol, col, qt, kt, vt, kn, sb, wo, pool, stage, every, pooled,
      local, q_sem, stage_sem, o_sem, *sems) = refs
-    length = len_ref[0]
+    length = len_ref[lax.axis_index("tensor")]
     hooks, middle, late = {}, [], {}
     if comm:
         p = Place(n)
+        count = greet(p, True)
         pack(weights_in, wa, table, w1, w2, p, r, cb)
-        enter(p)
-        wholes = [wa.at[j] for j in range(NJ)] + [table, w1, w2, every]
-        straight = (False,) * NJ + (True, False, False, True)
-        a0, a1, a2, bias, up, down, pools = [Gather(p, i, full, sems, way) for i, (full, way) in enumerate(zip(wholes, straight))]
-        parts = (a0, a1, a2, bias, up, down)
+        enter(count)
+        wholes = [wa.at[j] for j in range(NJ)] + [table, w1, w2]
+        straight = (False,) * NJ + (True, False, False)
+        parts = [Gather(p, i, full, sems[:7], way) for i, (full, way) in enumerate(zip(wholes, straight))]
+        pools = Exchange(p, every, sems[7:])
         flows = [[g.start] + g.flow() for g in parts]
 
         def steps(pairs):
@@ -625,19 +689,20 @@
     size = jnp.full((1, 1), length).astype(f32)
     mean = pool[0:1] / size
     if comm:
-        block = [mean[:, i * 128 : i * 128 + 128] for i in range(D // 128)] + [jnp.zeros((16 - D // 128, 128), f32)]
-        every[p.y * 2 + p.c, pl.ds(pl.multiple_of((p.z * 2 + p.x) * 16, 16), 16), :] = jnp.concatenate(block, axis=0)
+        block = [mean[:, i * 128 : i * 128 + 128] for i in range(D // 128)] + [jnp.zeros((8 - D // 128, 128), f32)]
+        every[p.c, pl.ds(pl.multiple_of(((p.z * 2 + p.x) * 2 + p.y) * 8, 8), 8), :] = jnp.concatenate(block, axis=0)
         pools.start()
     save(0).start()
     save(4).start()
     if comm:
-        run(pools.flow())
+        pools.finish()
         for i in range(dp):
             for t in range(NT):
+                at = (i * 2 + t // 2) * 8
                 for k in range(D // 128):
-                    pooled[i * NT + t : i * NT + t + 1, k * 128 : k * 128 + 128] = every[t, i * 16 + k : i * 16 + k + 1, :]
+                    pooled[i * NT + t : i * NT + t + 1, k * 128 : k * 128 + 128] = every[t % 2, at + k : at + k + 1, :]
         u_ref[...] = loss_pull(pooled[...], groups_ref[...], lax.axis_index("dp") * NT + lax.axis_index("tensor")) / size
-        for g in parts + (pools,):
+        for g in parts:
             g.finish()
     else:
         u_ref[...] = mean
@@ -665,11 +730,11 @@
         pltpu.VMEM((H, AUG, LEN), bf16), pltpu.VMEM((H, AUG, LEN), bf16), pltpu.VMEM((H, HD, LEN), bf16),
         pltpu.VMEM((2, LEN, AUG), bf16), pltpu.VMEM((2, LEN, LEN // 2), f32),
         pltpu.VMEM((D, D), bf16), pltpu.VMEM((8, D), f32), pltpu.VMEM((2, ROWS, D), f32),
-        pltpu.VMEM((NT, dp * 16, 128), f32), pltpu.VMEM((dp * NT, D), f32),
+        pltpu.VMEM((2, dp * 16, 128), f32), pltpu.VMEM((dp * NT, D), f32),
         dma((PARTS,)), dma((3, H)), dma((2,)), dma((len(big) + 3,)),
     ]
     if comm:
-        scratch += gather_sems(PARTS, n)
+        scratch += gather_sems(PARTS, n) + exchange_sems(n)
         params = pltpu.CompilerParams(collective_id=0, has_side_effects=True, vmem_limit_bytes=VMEM_CAP)
     else:
         params = pltpu.CompilerParams(vmem_limit_bytes=VMEM_CAP)
@@ -693,8 +758,8 @@
     landing, refs = (refs[: NJ + 3], refs[NJ + 3 :]) if comm else ([], refs)
     (wa, w1, w2, t1, t2, dqkv, xt, ct, df, dz, dh, sd, pp, turned, qkv, wcat, grow, ghb, gcol, gbias,
      load, s_load, q_sem, x_sem, *refs) = refs
-    length = len_ref[0]
-    hooks, after, ends = {}, {}, {}
+    length = len_ref[lax.axis_index("tensor")]
+    hooks, after, ends = {}, {}, [[], [], []]
     grads = [wa.at[j] for j in range(NJ)]
     h1t, dft, dat, dct = t1, t2, t1, t2
 
@@ -716,8 +781,8 @@
         p = Place(n)
 
         def part_of(step):
-            first = jnp.where(step < 2, 1 - p.y, p.y)
-            return first * 2 + step % 2
+            y = jnp.where(step < 2, 1 - p.y, p.y)
+            return y * 2 + jnp.where(step % 2 == 0, 1 - p.c, p.c)
     else:
 
         def part_of(step):
@@ -730,9 +795,9 @@
     for cp in loads[2:]:
         cp.start()
     if comm:
-        temp = wcat
+        temp, *refs = refs
         bufs, sems = refs[:-8], refs[-8:]
-        enter(p)
+        count = greet(p)
         where = [(lambda t: w1.at[t]), (lambda t: w2.at[t])] + [(lambda t, g=g: g.at[t]) for g in grads] + [lambda t: gbias.at[t]]
         parts = []
         for i, source in enumerate(where):
@@ -741,22 +806,22 @@
                 Scatter(p, i, rows, source, outs[i], [landing[i]] + list(bufs[3 * i : 3 * i + 3]),
                         temp.at[0 : 2 * n * rows, 0:width], x_sem.at[0], sems)
             )
-        up, down, a0, a1, a2, bias = parts
-
-        def call(*pairs):
-            return [functools.partial(f, *args) for f, *args in pairs]
-
-        after = {
-            1: call((up.core, 0), (down.core, 0)),
-            2: call((up.add, 0), (up.corner,), (down.add, 0), (down.corner,)),
-            3: call((up.core, 1), (down.core, 1)),
-        }
-        hooks = {
-            0: call((down.cross,)), 3: call((a0.core, 0), (a0.core, 1)), 4: call((up.line,)),
-            5: call((a0.add, 0), (a0.corner,), (a0.add, 1)), 6: call((down.line,)), 7: call((a1.core, 0), (a1.core, 1), (a0.cross,)),
-            8: call((up.last,)), 9: call((a1.add, 0), (a1.corner,), (a1.add, 1), (a0.line,)), 10: call((down.last,)),
-            11: call((a1.cross,), (a2.core, 0), (a2.core, 1)),
-        }
+        flows = [part.flow(i < 2) for i, part in enumerate(parts)]
+
+        def steps(pairs):
+            return [flows[g][k] for g, k in pairs]
+
+        if n == 4:
+            plan = {slot: steps(pairs) for slot, pairs in BACK.items()}
+        else:
+            plan = {1: steps([(g, k) for g in range(2) for k in range(4)]), 3: steps([(g, k) for g in range(2) for k in range(4, 7)])}
+            plan[6] = [step for flow in flows[:2] for step in flow[7:]]
+            for j in range(NJ):
+                plan[7 + j * NT + NT - 1] = flows[2 + j]
+            plan[7 + H] = flows[-1]
+        after = {k: plan.get(k, []) for k in range(NT)}
+        hooks = {h: plan.get(7 + h, []) for h in range(H)}
+        ends = [plan.get(5, []), plan.get(6, []), plan.get(7 + H, [])]
 
     u = u_ref[...]
     du = u * row_ref[4:5]
@@ -777,6 +842,8 @@
         return 0
 
     lax.fori_loop(0, CHUNKS, outer, 0)
+    if comm:
+        enter(count)
     grow[4:5] = u * gain_ref[...]
     grow[5:6] = u * jnp.full((1, 1), length).astype(f32)
     dft[...] = df[...].T
@@ -841,8 +908,7 @@
 
     lax.fori_loop(0, CHUNKS, inner_norm, 0)
     dat[...] = df[...].T
-    if comm:
-        run(call((up.add, 1), (down.add, 1), (up.cross,)))
+    run(ends[0])
     loads[4].wait()
     loads[5].wait()
     for j in range(NJ):
@@ -858,6 +924,7 @@
                 h = j * NT + t
                 wa[j, t, s, 3 * HD : 4 * HD] = gwo[:, h * HD : h * HD + HD]
     loads[6].wait()
+    run(ends[1])
 
     def head(h, _):
         j, t = h // NT, h % NT
@@ -895,11 +962,14 @@
                 g = nt(xt[s, :], dqkv[...]).astype(bf16)
                 for k in range(NT):
                     wa[j, k, s, 0 : 3 * HD] = g[:, k * 3 * HD : (k + 1) * 3 * HD]
+        at_step(h, hooks)
+
+        @pl.when(t == NT - 1)
+        def _():
             for i in range(CHUNKS):
                 s = slice(i * ROWS, (i + 1) * ROWS)
                 dh[s, :] += lax.dot_general(dqkv[:, s], wcat[...], (((0,), (1,)), ((), ())), preferred_element_type=f32)
 
-        at_step(h, hooks)
         return 0
 
     lax.fori_loop(0, H, head, 0)
@@ -921,11 +991,8 @@
                 piece = cols[t][:, i * cb + k * r : i * cb + k * r + wide]
                 block = jnp.where(at == 6 + k, jnp.pad(piece, ((0, 0), (0, 128 - wide))), block)
             gbias[t, i * 32 : i * 32 + 32, :] = block.astype(bf16)
+    run(ends[2])
     if comm:
-        run(call(
-            (bias.core, 0), (bias.core, 1), (a2.add, 0), (a2.corner,), (bias.add, 0), (bias.corner,), (a2.add, 1), (bias.add, 1),
-            (a0.last,), (a1.line,), (a2.cross,), (bias.cross,), (a1.last,), (a2.line,), (bias.line,), (a2.last,), (bias.last,),
-        ))
         for part in parts:
             part.finish()
     else:
@@ -962,6 +1029,7 @@
         dma((8,)), dma((2, 2)), dma((2, 3)), dma((1,)),
     ]
     if comm:
+        scratch += [pltpu.VMEM((D, D), bf16)]
         for rows, wide in widths:
             scratch += scatter_bufs(n, rows, wide)
         scratch += scatter_sems(len(widths), n)
@@ -1062,7 +1130,6 @@
     n = dp // 2
     r = D // dp
     cb = col_bias.shape[1]
-    length = lax.dynamic_slice_in_dim(lengths, lax.axis_index("tensor"), 1)
     comm = r % 32 == 0
     if comm:
         weights = (qkv_weight, out_weight, up_weight, down_weight.T, col_bias, row_params)
@@ -1071,14 +1138,14 @@
         own_b, own_1, own_2 = [gather_plain(v) for v in others]
         weights = (jnp.stack([gather_plain(own_a[j]) for j in range(NJ)]), own_b, own_1, own_2)
     (rstd1, rstd2, gain, row, hb, u, outputs, h1, xhat1, g, xhat2, ct, xt, gp, qt, kt, vt, wa, w1, w2) = forward(
-        length, groups, inputs, weights, n, cb, comm
+        lengths, groups, inputs, weights, n, cb, comm
     )
     if not comm:
         every = lax.all_gather(u, ("dp", "tensor"), axis=0, tiled=True)
-        u = loss_pull(every, groups, lax.axis_index(("dp", "tensor"))) / length[0].astype(f32)
+        u = loss_pull(every, groups, lax.axis_index(("dp", "tensor"))) / lengths[lax.axis_index("tensor")].astype(f32)
 
     big = (xhat2, xhat1, w1, w2, wa, g, gp, h1, ct, xt, qt, kt, vt)
-    input_grad, *sums = backward(length, u, gain, rstd1, rstd2, row, big, n, cb, comm)
+    input_grad, *sums = backward(lengths, u, gain, rstd1, rstd2, row, big, n, cb, comm)
     sums = sums[: NJ + 3] if comm else [scatter_plain(v) for v in sums]
     olds = (
         (qkv_weight, qkv_first, qkv_second, qkv_ema),

time: 244 us -> 220 us (0.902)
  Pallas kernels: 241 us -> 219 us
    pallas_call x1, Pallas kernels: 114 us -> 102 us  [forward(): pl.pallas_call(functools.partial(forward_kernel, n, cb, comm), out_shape=...]
    pallas_call x1, Pallas kernels: 119 us -> 108 us  [backward(): pl.pallas_call(functools.partial(backward_kernel, n, cb, comm), out_shape...]
where the time goes in v4:
time: 220 us
  Pallas kernels  219 us (100%)
    pallas_call x1, Pallas kernels, backward(): pl.pallas_call(functools.partial(backward_kernel, n, cb, comm), out_shape...  108 us
    pallas_call x1, Pallas kernels, forward(): pl.pallas_call(functools.partial(forward_kernel, n, cb, comm), out_shape=...  102 us
    pallas_call x1, Pallas kernels, adam(): pl.pallas_call(functools.partial(adam_kernel, cb), out_shape=[s(v.shape,...  8.54 us

profile of v4, /device:TPU:0, one launch (start us, length us, event | category | flops | bytes accessed | tf_op | source)
XLA Modules:
  0.0 220.1 jit_solution(13110422356503336106)
XLA Ops:
  0.7 102.3 %shard_map.458 = (f32[1024,1]{1,0:T(8,128)}, f32[1024,1]{1,0:T(8,128)}, f32[1,768]{1,0:T(1,128)}, f32[16,768]{1,0:T(8,128)}, f32[4,1,768]{2,1,0:T(1,128)}, /*ind...) custom-call(s32[4]{0:T(128)} %refs_0_.3, ...), custom_call_target="tpu_custom_call" | custom-call | tf_op jit(solution)/shard_map/pallas_call | solution.py:741
  103.0 108.3 %shard_map.459 = (f32[1024,768]{1,0:T(8,128)}, f32[96,768]{1,0:T(8,128)}, f32[96,768]{1,0:T(8,128)}, f32[96,256]{1,0:T(8,128)}, f32[96,256]{1,0:T(8,128)}, /*ind...) custom-call(s32[4]{0:T(128)} %refs_0_.3, ...), custom_call_target="tpu_custom_call" | custom-call | tf_op jit(solution)/shard_map/pallas_call | solution.py:1039
  211.3 8.5 %shard_map.460 = (bf16[1024,768]{1,0:T(8,128)(2,1)}, f32[1024,768]{1,0:T(8,128)}, f32[3,96,192]{2,1,0:T(8,128)}, f32[3,96,192]{2,1,0:T(8,128)}, f32[3,96,192]{2,...) custom-call(bf16[1024,768]{1,0:T(8,128)(2,1)} %get-tuple-element.78., ...), custom_call_target="tpu_custom_call" | custom-call | tf_op jit(solution)/shard_map/pallas_call | solution.py:1092

commit v5 on v4

--- a/solution.py
+++ b/solution.py
@@ -106,8 +106,8 @@
 
 
 class Gather:
-    def __init__(self, p, part, full, sems, straight=False):
-        self.p, self.part, self.full, self.straight = p, part, full, straight
+    def __init__(self, p, part, full, sems, straight=False, upright=False):
+        self.p, self.part, self.full, self.straight, self.upright = p, part, full, straight, upright
         self.rows = full.shape[1] // (2 * p.depth)
         self.recv, self.pair_recv, self.sz, self.sx, self.sy, self.sk, self.sc = sems
 
@@ -192,6 +192,9 @@
             self.arrived(self.at(far, 1 - p.x, p.y))
             self.arrived(self.at(far, p.x, 1 - p.y))
             z = (p.z + far) % p.depth
+            if self.upright and k:
+                self.pair_copy(z, p.y, p.c).start()
+                return
             odd = (z + self.part) % 2
             x, y = jnp.where(odd == 1, p.x, 1 - p.x), jnp.where(odd == 1, 1 - p.y, p.y)
             to = (p.z, jnp.where(odd == 1, 1 - p.x, p.x), jnp.where(odd == 1, p.y, 1 - p.y), p.c)
@@ -201,10 +204,15 @@
         self.each(k, step)
 
     def corner(self, k):
-        p = self.p
+        p, n = self.p, self.p.depth
 
         def step(sign, far):
-            self.arrived(self.at(far, 1 - p.x, 1 - p.y))
+            place = functools.partial(self.at, far, 1 - p.x, 1 - p.y)
+            self.arrived(place())
+            if self.upright and sign <= 0:
+                self.send(place, p.along_z(1), self.sz, lambda: p.z + 1 < n)
+            if self.upright and sign >= 0:
+                self.send(place, p.along_z(-1), self.sz, lambda: p.z > 0)
             self.pair_copy((p.z + far) % p.depth, 1 - p.y, p.c).start()
 
         self.each(k, step)
@@ -216,11 +224,16 @@
 
     def flow(self):
         n = self.p.depth
+        order = [1, n - 1] + list(range(2, n - 1)) if self.straight and n > 2 else list(range(1, n))
         steps = [functools.partial(self.cross, 0)]
-        order = [1, n - 1] + list(range(2, n - 1)) if self.straight and n > 2 else list(range(1, n))
+        if self.upright:
+            steps.append(functools.partial(self.corner, 0))
         for k in order:
             steps += [functools.partial(self.line, k), functools.partial(self.cross, k)]
-        steps += [functools.partial(self.corner, k) for k in range(n)]
+            if self.upright:
+                steps.append(functools.partial(self.corner, k))
+        if not self.upright:
+            steps += [functools.partial(self.corner, k) for k in range(n)]
         steps.append(self.other_core)
         return steps
 
@@ -230,8 +243,9 @@
         def left(ref, sem):
             pltpu.make_async_copy(ref, ref, sem.at[self.part]).wait()
 
-        for sem in (self.sx, self.sy, self.sk):
+        for sem in (self.sx, self.sy):
             left(self.full.at[0, 0 : n * r, :], sem)
+        left(self.full.at[0, 0 : r if self.upright else n * r, :], self.sk)
         left(self.full.at[0:2], self.sc)
         if self.straight:
             left(self.full.at[0, 0 : (n - 1) * r, :], self.sz)
@@ -239,7 +253,8 @@
             for z in range(n):
                 count = (z + 1 if z + 1 < n else 0) + (n - z if z > 0 else 0)
                 if count:
-                    pl.when(self.p.z == z)(functools.partial(left, self.full.at[0, 0 : count * r, :], self.sz))
+                    ref = self.full.at[0 : 2 if self.upright else 1, 0 : count * r, :]
+                    pl.when(self.p.z == z)(functools.partial(left, ref, self.sz))
 
 
 class Exchange:
@@ -441,10 +456,10 @@
 CHUNKS = LEN // ROWS
 PARTS = 6
 
-PRE = ((0, 0), (3, 0), (1, 0), (2, 0), (0, 1), (0, 2), (3, 1), (3, 2), (1, 1), (1, 2), (2, 1), (2, 2), (3, 3), (3, 4), (0, 3), (1, 3), (1, 4), (0, 4), (3, 5), (3, 6), (4, 0), (2, 3), (3, 7), (0, 5), (0, 6), (2, 4), (3, 8), (5, 0), (3, 9), (0, 7), (0, 8), (1, 5), (3, 10), (0, 9), (1, 6), (2, 5), (2, 6), (0, 10), (0, 11), (4, 1), (0, 12), (3, 11), (1, 7), (4, 2), (5, 1), (1, 8), (3, 12), (1, 9), (2, 7), (2, 8))
-HEAD = {0: ((1, 10),), 1: ((1, 11),), 2: ((5, 2), (2, 9), (1, 12), (2, 10)), 3: ((4, 3),), 4: ((4, 4), (2, 11), (5, 3)), 5: ((5, 4),), 6: ((2, 12),), 8: ((4, 5), (4, 6)), 10: ((5, 5),), 11: ((4, 7), (4, 8), (4, 9), (5, 6), (4, 10))}
-MID = ((4, 11), (4, 12))
-LATE = {0: ((5, 7), (5, 8)), 2: ((5, 9), (5, 10)), 8: ((5, 11),), 11: ((5, 12),)}
+PRE = ((0, 0), (3, 0), (2, 0), (1, 0), (0, 1), (3, 1), (0, 2), (3, 2), (1, 1), (1, 2), (2, 1), (3, 3), (3, 4), (4, 0), (1, 3), (0, 3), (0, 4), (2, 2), (1, 4), (4, 1), (2, 3), (3, 5), (3, 6), (1, 5), (0, 5), (1, 6), (0, 6), (2, 4), (1, 7), (1, 8), (4, 2), (0, 7), (3, 7), (4, 3), (1, 9), (3, 8), (1, 10), (0, 8), (0, 9), (3, 9), (0, 10), (5, 0), (3, 10), (0, 11), (3, 11), (2, 5), (3, 12), (2, 6), (0, 12))
+HEAD = {1: ((1, 11),), 2: ((2, 7), (4, 4), (2, 8), (2, 9), (4, 5), (1, 12), (5, 1)), 3: ((4, 6),), 5: ((2, 10), (2, 11), (5, 2), (5, 3)), 6: ((2, 12),), 7: ((4, 7), (4, 8), (4, 9)), 10: ((4, 10), (5, 4), (5, 5), (5, 6)), 11: ((4, 11),)}
+MID = ((5, 7), (4, 12), (5, 8))
+LATE = {2: ((5, 9),), 11: ((5, 10), (5, 11)), 15: ((5, 12),)}
 BACK = {0: ((0, 0), (1, 0)), 1: ((0, 1),), 2: ((0, 2), (0, 3), (1, 1)), 3: ((1, 2), (1, 3)), 5: ((0, 4),), 6: ((0, 5), (1, 4)), 7: ((0, 6),), 8: ((0, 7), (1, 5)), 9: ((1, 6), (0, 8), (0, 9), (0, 10)), 10: ((2, 0), (2, 1)), 11: ((1, 7),), 12: ((0, 11), (1, 8), (1, 9), (0, 12), (2, 2)), 13: ((1, 10),), 14: ((2, 3), (2, 4), (2, 5), (3, 0), (3, 1)), 15: ((2, 6), (2, 7), (2, 8), (3, 2), (1, 11)), 16: ((1, 12), (3, 3)), 17: ((3, 4), (3, 5)), 18: ((4, 0), (3, 6), (3, 7), (1, 13), (2, 9), (4, 1), (0, 13), (3, 8), (2, 10), (4, 2), (3, 9), (4, 3), (4, 4)), 19: ((2, 11), (3, 10), (4, 5), (5, 0), (2, 12), (2, 13), (5, 1), (4, 6), (5, 2), (4, 7), (5, 3), (5, 4), (4, 8), (3, 11), (5, 5), (4, 9), (1, 14), (4, 10), (3, 12), (5, 6), (5, 7), (3, 13), (5, 8), (4, 11), (5, 9), (5, 10), (4, 12), (4, 13), (0, 14), (2, 14), (5, 11), (3, 14), (5, 12), (5, 13), (4, 14), (5, 14))}
 
 
@@ -521,8 +536,7 @@
         pack(weights_in, wa, table, w1, w2, p, r, cb)
         enter(count)
         wholes = [wa.at[j] for j in range(NJ)] + [table, w1, w2]
-        straight = (False,) * NJ + (True, False, False)
-        parts = [Gather(p, i, full, sems[:7], way) for i, (full, way) in enumerate(zip(wholes, straight))]
+        parts = [Gather(p, i, full, sems[:7], i == NJ, i > NJ) for i, full in enumerate(wholes)]
         pools = Exchange(p, every, sems[7:])
         flows = [[g.start] + g.flow() for g in parts]
 
@@ -1047,17 +1061,22 @@
 
 
 def adam_kernel(cb, *refs):
-    moved, sums, old, refs = refs[:2], refs[2:8], refs[8:32], refs[32:]
-    landed, new, held, sem = refs[:2], refs[2:26], refs[26:28], refs[28]
-    inward = [pltpu.make_async_copy(src, dst, sem.at[i]) for i, (src, dst) in enumerate(zip(moved, held))]
-    outward = [pltpu.make_async_copy(src, dst, sem.at[i]) for i, (src, dst) in enumerate(zip(held, landed))]
+    ins, outs, refs = refs[:32], refs[32:58], refs[58:]
+    held, new, sem_in, sem_out = refs[:32], refs[32:56], refs[56], refs[57]
+    inward = [pltpu.make_async_copy(src, dst, sem_in.at[i]) for i, (src, dst) in enumerate(zip(ins, held))]
+    outward = [pltpu.make_async_copy(src, dst, sem_out.at[i]) for i, (src, dst) in enumerate(zip((*held[:2], *new), outs))]
     for cp in inward:
         cp.start()
+    moved, sums, old = held[:2], held[2:8], held[8:]
     gw1, gw2, ga, gbias = sums[0], sums[1], sums[2:5], sums[5]
     r = gw1.shape[0]
 
     def wide(k):
         return jnp.concatenate([ga[j][:, k * HD : k * HD + HD] for j in range(NJ)], axis=1)
+
+    def group(i):
+        for k in range(4):
+            inward[8 + 4 * i + k].wait()
 
     def update(i, grad, rate, at=()):
         where = at + (Ellipsis,)
@@ -1065,22 +1084,39 @@
         for k, v in enumerate(out):
             new[4 * i + k][where] = v
 
+    def leave(*at):
+        for i in at:
+            outward[i].start()
+
+    for i in range(2):
+        inward[i].wait()
+    leave(0, 1)
+    for i in range(2, 8):
+        inward[i].wait()
+    group(0)
     for k in range(3):
         update(0, wide(k), D ** (-0.5), (k,))
+    leave(2, 3, 4, 5)
+    group(2)
+    update(2, gw1[...], D ** (-0.5))
+    leave(10, 11, 12, 13)
+    group(3)
+    update(3, gw2[...], FF ** (-0.5))
+    leave(14, 15, 16, 17)
     high = -(-r // 128) * 128
     turned = jnp.concatenate([wide(3), jnp.zeros((r, 256 - HC), f32)], axis=1)
     if high > r:
         turned = jnp.concatenate([turned, jnp.zeros((high - r, 256), f32)], axis=0)
+    group(1)
     update(1, turned.T[0:HC, 0:r], D ** (-0.5))
-    for one, two in zip(inward, outward):
-        one.wait()
-        two.start()
-    update(2, gw1[...], D ** (-0.5))
-    update(3, gw2[...], FF ** (-0.5))
+    leave(6, 7, 8, 9)
+    group(4)
     rows = gbias[...]
     pieces = [rows[6 + k : 7 + k, 0 : min(r, cb - k * r)] for k in range(-(-cb // r))]
     update(4, jnp.concatenate(pieces, axis=1), 0.1)
+    group(5)
     update(5, rows[0:6, 0:r], 0.15)
+    leave(*range(18, 26))
     for cp in outward:
         cp.wait()
 
@@ -1089,14 +1125,15 @@
     flat = [v for group in olds for v in group]
     s = jax.ShapeDtypeStruct
     shapes = [s(group[0].shape, f32) for group in olds for _ in range(4)]
+    ins = [*moved, *sums, *flat]
     return pl.pallas_call(
         functools.partial(adam_kernel, cb),
         out_shape=[s(v.shape, v.dtype) for v in moved] + shapes,
-        in_specs=any_spec(2) + vmem_spec(6 + 24),
-        out_specs=any_spec(2) + vmem_spec(24),
-        scratch_shapes=[pltpu.VMEM(v.shape, v.dtype) for v in moved] + [pltpu.SemaphoreType.DMA((2,))],
+        in_specs=any_spec(32),
+        out_specs=any_spec(26),
+        scratch_shapes=[pltpu.VMEM(v.shape, v.dtype) for v in ins + shapes] + [pltpu.SemaphoreType.DMA((32,)), pltpu.SemaphoreType.DMA((26,))],
         compiler_params=pltpu.CompilerParams(vmem_limit_bytes=VMEM_CAP),
-    )(*moved, *sums, *flat)
+    )(*ins)
 
 
 def gather_plain(own):

time: 220 us -> 214 us (0.973)
  Pallas kernels: 219 us -> 213 us
    pallas_call x1, Pallas kernels: 102 us -> 97.9 us  [forward(): pl.pallas_call(functools.partial(forward_kernel, n, cb, comm), out_shape=...]
where the time goes in v5:
time: 214 us
  Pallas kernels  213 us (100%)
    pallas_call x1, Pallas kernels, backward(): pl.pallas_call(functools.partial(backward_kernel, n, cb, comm), out_shape...  108 us
    pallas_call x1, Pallas kernels, forward(): pl.pallas_call(functools.partial(forward_kernel, n, cb, comm), out_shape=...  97.9 us
    pallas_call x1, Pallas kernels, adam(): pl.pallas_call(functools.partial(adam_kernel, cb), out_shape=[s(v.shape,...  6.8 us

profile of v5, /device:TPU:0, one launch (start us, length us, event | category | flops | bytes accessed | tf_op | source)
XLA Modules:
  0.0 213.7 jit_solution(12835935436798022523)
XLA Ops:
  0.7 97.9 %shard_map.458 = (f32[1024,1]{1,0:T(8,128)}, f32[1024,1]{1,0:T(8,128)}, f32[1,768]{1,0:T(1,128)}, f32[16,768]{1,0:T(8,128)}, f32[4,1,768]{2,1,0:T(1,128)}, /*ind...) custom-call(s32[4]{0:T(128)} %refs_0_.3, ...), custom_call_target="tpu_custom_call" | custom-call | tf_op jit(solution)/shard_map/pallas_call | solution.py:755
  98.6 108.1 %shard_map.459 = (f32[1024,768]{1,0:T(8,128)}, f32[96,768]{1,0:T(8,128)}, f32[96,768]{1,0:T(8,128)}, f32[96,256]{1,0:T(8,128)}, f32[96,256]{1,0:T(8,128)}, /*ind...) custom-call(s32[4]{0:T(128)} %refs_0_.3, ...), custom_call_target="tpu_custom_call" | custom-call | tf_op jit(solution)/shard_map/pallas_call | solution.py:1053
  206.7 6.8 %shard_map.460 = (bf16[1024,768]{1,0:T(8,128)(2,1)}, f32[1024,768]{1,0:T(8,128)}, f32[3,96,192]{2,1,0:T(8,128)}, f32[3,96,192]{2,1,0:T(8,128)}, f32[3,96,192]{2,...) custom-call(bf16[1024,768]{1,0:T(8,128)(2,1)} %get-tuple-element.78., ...), custom_call_target="tpu_custom_call" | custom-call | tf_op jit(solution)/shard_map/pallas_call | solution.py:1129

commit v6 on v5

--- a/solution.py
+++ b/solution.py
@@ -456,11 +456,11 @@
 CHUNKS = LEN // ROWS
 PARTS = 6
 
-PRE = ((0, 0), (3, 0), (2, 0), (1, 0), (0, 1), (3, 1), (0, 2), (3, 2), (1, 1), (1, 2), (2, 1), (3, 3), (3, 4), (4, 0), (1, 3), (0, 3), (0, 4), (2, 2), (1, 4), (4, 1), (2, 3), (3, 5), (3, 6), (1, 5), (0, 5), (1, 6), (0, 6), (2, 4), (1, 7), (1, 8), (4, 2), (0, 7), (3, 7), (4, 3), (1, 9), (3, 8), (1, 10), (0, 8), (0, 9), (3, 9), (0, 10), (5, 0), (3, 10), (0, 11), (3, 11), (2, 5), (3, 12), (2, 6), (0, 12))
-HEAD = {1: ((1, 11),), 2: ((2, 7), (4, 4), (2, 8), (2, 9), (4, 5), (1, 12), (5, 1)), 3: ((4, 6),), 5: ((2, 10), (2, 11), (5, 2), (5, 3)), 6: ((2, 12),), 7: ((4, 7), (4, 8), (4, 9)), 10: ((4, 10), (5, 4), (5, 5), (5, 6)), 11: ((4, 11),)}
-MID = ((5, 7), (4, 12), (5, 8))
-LATE = {2: ((5, 9),), 11: ((5, 10), (5, 11)), 15: ((5, 12),)}
-BACK = {0: ((0, 0), (1, 0)), 1: ((0, 1),), 2: ((0, 2), (0, 3), (1, 1)), 3: ((1, 2), (1, 3)), 5: ((0, 4),), 6: ((0, 5), (1, 4)), 7: ((0, 6),), 8: ((0, 7), (1, 5)), 9: ((1, 6), (0, 8), (0, 9), (0, 10)), 10: ((2, 0), (2, 1)), 11: ((1, 7),), 12: ((0, 11), (1, 8), (1, 9), (0, 12), (2, 2)), 13: ((1, 10),), 14: ((2, 3), (2, 4), (2, 5), (3, 0), (3, 1)), 15: ((2, 6), (2, 7), (2, 8), (3, 2), (1, 11)), 16: ((1, 12), (3, 3)), 17: ((3, 4), (3, 5)), 18: ((4, 0), (3, 6), (3, 7), (1, 13), (2, 9), (4, 1), (0, 13), (3, 8), (2, 10), (4, 2), (3, 9), (4, 3), (4, 4)), 19: ((2, 11), (3, 10), (4, 5), (5, 0), (2, 12), (2, 13), (5, 1), (4, 6), (5, 2), (4, 7), (5, 3), (5, 4), (4, 8), (3, 11), (5, 5), (4, 9), (1, 14), (4, 10), (3, 12), (5, 6), (5, 7), (3, 13), (5, 8), (4, 11), (5, 9), (5, 10), (4, 12), (4, 13), (0, 14), (2, 14), (5, 11), (3, 14), (5, 12), (5, 13), (4, 14), (5, 14))}
+PRE = ((0, 0), (3, 0), (2, 0), (1, 0), (0, 1), (3, 1), (2, 1), (3, 2), (1, 1), (4, 0), (3, 3), (3, 4), (1, 2), (1, 3), (0, 2), (0, 3), (3, 5), (2, 2), (3, 6), (4, 1), (2, 3), (1, 4), (1, 5), (1, 6), (3, 7), (0, 4), (0, 5), (3, 8), (3, 9), (0, 6), (5, 0), (1, 7), (1, 8), (1, 9), (2, 4), (0, 7), (0, 8), (0, 9), (2, 5), (4, 2), (2, 6), (3, 10), (1, 10), (4, 3), (3, 11), (1, 11), (0, 10), (0, 11), (3, 12), (1, 12), (5, 1), (0, 12))
+HEAD = {2: ((2, 7), (2, 8), (2, 9), (4, 4), (4, 5)), 3: ((4, 6),), 4: ((5, 2), (5, 3), (2, 10), (2, 11)), 6: ((2, 12), (4, 7)), 7: ((4, 8), (4, 9)), 10: ((5, 4), (4, 10), (5, 5), (5, 6)), 11: ((4, 11),)}
+MID = ((4, 12), (5, 7))
+LATE = {0: ((5, 8),), 2: ((5, 9),), 11: ((5, 10), (5, 11)), 15: ((5, 12),)}
+BACK = {0: ((0, 0),), 1: ((0, 1), (1, 0)), 2: ((0, 2), (0, 3), (1, 1)), 3: ((0, 4), (1, 2), (1, 3)), 5: ((0, 5), (1, 4)), 6: ((0, 6), (1, 5), (0, 7)), 7: ((0, 8),), 8: ((0, 9), (0, 10), (1, 6)), 9: ((1, 7),), 10: ((2, 0),), 11: ((2, 1), (2, 2), (1, 8), (1, 9), (0, 11), (1, 10), (2, 3), (2, 4), (0, 12)), 13: ((2, 5),), 14: ((2, 6), (1, 11), (1, 12), (2, 7), (3, 0), (2, 8), (3, 1), (2, 9), (2, 10)), 15: ((1, 13), (3, 2)), 16: ((3, 3), (3, 4), (3, 5)), 17: ((3, 6),), 18: ((4, 0), (3, 7), (2, 11), (3, 8), (4, 1)), 19: ((4, 2), (3, 9), (2, 12), (0, 13), (4, 3), (5, 0), (5, 1), (4, 4), (3, 10), (4, 5), (2, 13)), 20: ((4, 6), (5, 2), (5, 3), (5, 4), (5, 5), (4, 7), (4, 8), (4, 9), (3, 11), (5, 6), (4, 10), (3, 12), (5, 7), (5, 8), (5, 9)), 21: ((5, 10), (2, 14), (3, 13), (4, 11), (0, 14), (4, 12), (4, 13), (1, 14), (5, 11)), 22: ((5, 12), (3, 14), (5, 13), (4, 14), (5, 14))}
 
 
 def pack(refs, wa, table, w1, w2, p, r, cb):
@@ -521,12 +521,12 @@
     dp = 2 * n
     r = D // dp
     given, refs = (6, refs[:2] + refs[2:]) if comm else (4, refs)
-    len_ref, groups_ref, x_ref = refs[:3]
-    weights_in, refs = refs[3 : 3 + given], refs[3 + given :]
-    (rstd1_ref, rstd2_ref, gain_ref, row_ref, hb_ref, u_ref,
+    len_ref, x_ref = refs[:2]
+    weights_in, refs = refs[2 : 2 + given], refs[2 + given :]
+    (rstd_ref, gain_ref, row_ref, hb_ref, pooled,
      out_out, h1_out, xhat1_out, g_out, xhat2_out, ct_out, xt_out, gp_out, q_out, k_out, v_out, wa_out, w1_out, w2_out,
      out_ref, h1_ref, xhat1_ref, g_ref, xhat2_ref, ct_ref, xt,
-     wa, w1, w2, table, bcol, col, qt, kt, vt, kn, sb, wo, pool, stage, every, pooled,
+     wa, w1, w2, table, bcol, col, qt, kt, vt, kn, sb, wo, pool, stage, every,
      local, q_sem, stage_sem, o_sem, *sems) = refs
     length = len_ref[lax.axis_index("tensor")]
     hooks, middle, late = {}, [], {}
@@ -536,7 +536,7 @@
         pack(weights_in, wa, table, w1, w2, p, r, cb)
         enter(count)
         wholes = [wa.at[j] for j in range(NJ)] + [table, w1, w2]
-        parts = [Gather(p, i, full, sems[:7], i == NJ, i > NJ) for i, full in enumerate(wholes)]
+        parts = [Gather(p, i, full, sems[:7], i == NJ, i != NJ) for i, full in enumerate(wholes)]
         pools = Exchange(p, every, sems[7:])
         flows = [[g.start] + g.flow() for g in parts]
 
@@ -646,7 +646,7 @@
         r1 = x_ref[s, :].astype(f32) + (nt(c_nat[s, :], wo[...]) + row_ref[0:1])
         xhat, rstd = norm(r1)
         xhat1_ref[s, :] = xhat
-        rstd1_ref[s, :] = rstd
+        rstd_ref[s, 0:1] = rstd
         h1_ref[s, :] = (xhat * row_ref[1:2] + row_ref[2:3]).astype(bf16)
         return 0
 
@@ -691,7 +691,7 @@
             res = res + nt(g_ref[t, s, :], w2[t])
         xhat, rstd = norm(res)
         xhat2_ref[s, :] = xhat
-        rstd2_ref[s, :] = rstd
+        rstd_ref[s, 1:2] = rstd
         y = xhat * row_ref[4:5] + row_ref[5:6]
         out_ref[s, :] = y.astype(bf16)
         here = i * ROWS + lax.broadcasted_iota(jnp.int32, (ROWS, 1), 0) < length
@@ -715,11 +715,10 @@
                 at = (i * 2 + t // 2) * 8
                 for k in range(D // 128):
                     pooled[i * NT + t : i * NT + t + 1, k * 128 : k * 128 + 128] = every[t % 2, at + k : at + k + 1, :]
-        u_ref[...] = loss_pull(pooled[...], groups_ref[...], lax.axis_index("dp") * NT + lax.axis_index("tensor")) / size
         for g in parts:
             g.finish()
     else:
-        u_ref[...] = mean
+        pooled[...] = mean
     for h in range(H):
         for i, (src, dst) in enumerate(kept):
             pltpu.make_async_copy(src.at[h], dst.at[h], q_sem.at[i, h]).wait()
@@ -727,12 +726,12 @@
         save(i).wait()
 
 
-def forward(length, groups, x, weights, n, cb, comm):
+def forward(length, x, weights, n, cb, comm):
     s = jax.ShapeDtypeStruct
     dp = 2 * n
     r = D // dp
     dma = pltpu.SemaphoreType.DMA
-    shapes = [s((LEN, 1), f32), s((LEN, 1), f32), s((1, D), f32), s((16, D), f32), s((NT, 1, D), f32), s((1, D), f32)]
+    shapes = [s((LEN, 2), f32), s((1, D), f32), s((16, D), f32), s((NT, 1, D), f32), s((dp * NT if comm else 1, D), f32)]
     big = [s((LEN, D), bf16), s((LEN, D), bf16), s((LEN, D), f32), s((NT, LEN, D), bf16), s((LEN, D), f32), s((D, LEN), bf16), s((D, LEN), bf16)]
     kept = [
         s((NT, LEN, D), f32), s((H, AUG, LEN), bf16), s((H, AUG, LEN), bf16), s((H, HD, LEN), bf16),
@@ -744,7 +743,7 @@
         pltpu.VMEM((H, AUG, LEN), bf16), pltpu.VMEM((H, AUG, LEN), bf16), pltpu.VMEM((H, HD, LEN), bf16),
         pltpu.VMEM((2, LEN, AUG), bf16), pltpu.VMEM((2, LEN, LEN // 2), f32),
         pltpu.VMEM((D, D), bf16), pltpu.VMEM((8, D), f32), pltpu.VMEM((2, ROWS, D), f32),
-        pltpu.VMEM((2, dp * 16, 128), f32), pltpu.VMEM((dp * NT, D), f32),
+        pltpu.VMEM((2, dp * 16, 128), f32),
         dma((PARTS,)), dma((3, H)), dma((2,)), dma((len(big) + 3,)),
     ]
     if comm:
@@ -755,27 +754,30 @@
     return pl.pallas_call(
         functools.partial(forward_kernel, n, cb, comm),
         out_shape=shapes + big + kept,
-        in_specs=[pl.BlockSpec(memory_space=pltpu.SMEM)] + vmem_spec(2) + (vmem_spec(6) if comm else any_spec(4)),
+        in_specs=[pl.BlockSpec(memory_space=pltpu.SMEM)] + vmem_spec(1) + (vmem_spec(6) if comm else any_spec(4)),
         out_specs=vmem_spec(len(shapes)) + any_spec(len(big) + len(kept)),
         scratch_shapes=scratch,
         compiler_params=params,
-    )(length, groups, x, *weights)
+    )(length, x, *weights)
 
 
 def backward_kernel(n, cb, comm, *refs):
     dp = 2 * n
     r = D // dp
-    (len_ref, u_ref, gain_ref, rstd1_ref, rstd2_ref, row_ref,
+    (len_ref, pooled_ref, groups_ref, gain_ref, rstd_ref, row_ref,
      xhat2_in, xhat1_in, w1_in, w2_in, wa_in, g_in, gp_in, h1_in, ct_in, xt_in, q_in, k_in, v_in, *refs) = refs
     dx_out, *refs = refs
     outs, refs = refs[: NJ + 3], refs[NJ + 3 :]
     landing, refs = (refs[: NJ + 3], refs[NJ + 3 :]) if comm else ([], refs)
-    (wa, w1, w2, t1, t2, dqkv, xt, ct, df, dz, dh, sd, pp, turned, qkv, wcat, grow, ghb, gcol, gbias,
+    (wa, w1, w2, t2, dqkv, xt, df, dz, dh, sd, pp, turned, qkv, wcat, grow, ghb, gcol, gbias,
      load, s_load, q_sem, x_sem, *refs) = refs
     length = len_ref[lax.axis_index("tensor")]
-    hooks, after, ends = {}, {}, [[], [], []]
+    hooks, after, ends = {}, {}, [[]] * 6
     grads = [wa.at[j] for j in range(NJ)]
-    h1t, dft, dat, dct = t1, t2, t1, t2
+    h1t = dat = dqkv.at[1]
+    ct = dqkv.at[2]
+    dft = dct = t2
+    folded = [df.at[0:D, :], dz.at[0:D, :], wcat]
 
     loads = [
         pltpu.make_async_copy(src, dst, load.at[i])
@@ -835,9 +837,10 @@
             plan[7 + H] = flows[-1]
         after = {k: plan.get(k, []) for k in range(NT)}
         hooks = {h: plan.get(7 + h, []) for h in range(H)}
-        ends = [plan.get(5, []), plan.get(6, []), plan.get(7 + H, [])]
-
-    u = u_ref[...]
+        ends = [plan.get(k, []) for k in (5, 6, 7 + H, 8 + H, 9 + H, 10 + H)]
+
+    size = jnp.full((1, 1), length).astype(f32)
+    u = loss_pull(pooled_ref[...], groups_ref[...], lax.axis_index("dp") * NT + lax.axis_index("tensor")) / size
     du = u * row_ref[4:5]
     mean_du = jnp.mean(du, axis=1, keepdims=True)
     grow[...] = jnp.zeros_like(grow)
@@ -848,7 +851,7 @@
         here = i * ROWS + lax.broadcasted_iota(jnp.int32, (ROWS, 1), 0) < length
         hat = sd[1, s, 0:D]
         dot = jnp.mean(hat * du, axis=1, keepdims=True)
-        dr = jnp.where(here, rstd2_ref[s, :] * (du - mean_du - hat * dot), 0.0)
+        dr = jnp.where(here, rstd_ref[s, 1:2] * (du - mean_du - hat * dot), 0.0)
         dh[s, :] = dr
         low = dr.astype(bf16)
         df[s, :] = low
@@ -859,7 +862,7 @@
     if comm:
         enter(count)
     grow[4:5] = u * gain_ref[...]
-    grow[5:6] = u * jnp.full((1, 1), length).astype(f32)
+    grow[5:6] = u * size
     dft[...] = df[...].T
     loads[2].wait()
     h1t[...] = dz[...].T
@@ -913,7 +916,7 @@
         grow[1:2] += jnp.sum(d * hat, axis=0, keepdims=True)
         grow[2:3] += jnp.sum(d, axis=0, keepdims=True)
         dn = d * row_ref[1:2]
-        dr = rstd1_ref[s, :] * (dn - jnp.mean(dn, axis=1, keepdims=True) - hat * jnp.mean(dn * hat, axis=1, keepdims=True))
+        dr = rstd_ref[s, 0:1] * (dn - jnp.mean(dn, axis=1, keepdims=True) - hat * jnp.mean(dn * hat, axis=1, keepdims=True))
         dh[s, :] = dr
         low = dr.astype(bf16)
         grow[0:1] += jnp.sum(low.astype(f32), axis=0, keepdims=True)
@@ -960,35 +963,32 @@
         pp[1] = (sd[0] * (sd[1] - inner)).astype(bf16)
         turned[...] = pp[1].T
         at = pl.multiple_of(t * 3 * HD, HD)
-        dqkv[pl.ds(at + HD, HD), :] = nn(qkv[slot, 0, 0:HD, :], pp[1]).astype(bf16)
-        dqkv[pl.ds(at + 2 * HD, HD), :] = nn(dct[own, :], pp[0]).astype(bf16)
-        dqkv[pl.ds(at, HD), :] = (nn(qkv[slot, 1, 0:HD, :], turned[...]) * HD**-0.5).astype(bf16)
+        dqkv[j, pl.ds(at + HD, HD), :] = nn(qkv[slot, 0, 0:HD, :], pp[1]).astype(bf16)
+        dqkv[j, pl.ds(at + 2 * HD, HD), :] = nn(dct[own, :], pp[0]).astype(bf16)
+        dqkv[j, pl.ds(at, HD), :] = (nn(qkv[slot, 1, 0:HD, :], turned[...]) * HD**-0.5).astype(bf16)
 
         @pl.when(t == NT - 1)
         def _():
-            for k in range(NT):
-                wcat[:, k * 3 * HD : (k + 1) * 3 * HD] = wa[j, k, :, 0 : 3 * HD]
-            sums = nt(jnp.ones((16, LEN), bf16), dqkv[...])
+            for i in range(NJ):
+
+                @pl.when(j == i)
+                def _(i=i):
+                    for k in range(NT):
+                        folded[i][:, k * 3 * HD : (k + 1) * 3 * HD] = wa[i, k, :, 0 : 3 * HD]
+
+            sums = nt(jnp.ones((16, LEN), bf16), dqkv[j])
             for k in range(NT):
                 gcol[j, k] = sums[0:8, k * 3 * HD : (k + 1) * 3 * HD]
             for i in range(D // ROWS):
                 s = slice(i * ROWS, (i + 1) * ROWS)
-                g = nt(xt[s, :], dqkv[...]).astype(bf16)
+                g = nt(xt[s, :], dqkv[j]).astype(bf16)
                 for k in range(NT):
                     wa[j, k, s, 0 : 3 * HD] = g[:, k * 3 * HD : (k + 1) * 3 * HD]
+
         at_step(h, hooks)
-
-        @pl.when(t == NT - 1)
-        def _():
-            for i in range(CHUNKS):
-                s = slice(i * ROWS, (i + 1) * ROWS)
-                dh[s, :] += lax.dot_general(dqkv[:, s], wcat[...], (((0,), (1,)), ((), ())), preferred_element_type=f32)
-
         return 0
 
     lax.fori_loop(0, H, head, 0)
-    dx = pltpu.make_async_copy(dh, dx_out, load.at[0])
-    dx.start()
 
     col_rows = -(-cb // r)
     cols = []
@@ -1006,6 +1006,14 @@
                 block = jnp.where(at == 6 + k, jnp.pad(piece, ((0, 0), (0, 128 - wide))), block)
             gbias[t, i * 32 : i * 32 + 32, :] = block.astype(bf16)
     run(ends[2])
+    for j in range(NJ):
+        for i in range(CHUNKS):
+            s = slice(i * ROWS, (i + 1) * ROWS)
+            dh[s, :] += lax.dot_general(dqkv[j, :, s], folded[j][...], (((0,), (1,)), ((), ())), preferred_element_type=f32)
+        if j == NJ - 1:
+            dx = pltpu.make_async_copy(dh, dx_out, load.at[0])
+            dx.start()
+        run(ends[3 + j])
     if comm:
         for part in parts:
             part.finish()
@@ -1018,7 +1026,7 @@
     dx.wait()
 
 
-def backward(length, u, gain, rstd1, rstd2, row, big, n, cb, comm):
+def backward(length, pooled, groups, gain, rstd, row, big, n, cb, comm):
     s = jax.ShapeDtypeStruct
     dp = 2 * n
     r = D // dp
@@ -1037,7 +1045,7 @@
     rows_full = pltpu.VMEM((LEN, D), f32)
     scratch = [
         pltpu.VMEM((NJ, NT, D, 4 * HD), bf16), pltpu.VMEM((NT, D, D), bf16), pltpu.VMEM((NT, D, D), bf16),
-        turned, turned, turned, turned, turned, rows_low, rows_low, rows_full,
+        turned, pltpu.VMEM((NJ, D, LEN), bf16), turned, rows_low, rows_low, rows_full,
         pltpu.VMEM((2, LEN, LEN), f32), pltpu.VMEM((2, LEN, LEN), bf16), pltpu.VMEM((LEN, LEN), bf16), pltpu.VMEM((2, 3, AUG, LEN), bf16), pltpu.VMEM((D, D), bf16),
         pltpu.VMEM((16, D), f32), pltpu.VMEM((NT, 1, D), f32), pltpu.VMEM((NJ, NT, 8, 3 * HD), f32), pltpu.VMEM((NT, dp * 32, 128), bf16),
         dma((8,)), dma((2, 2)), dma((2, 3)), dma((1,)),
@@ -1057,7 +1065,7 @@
         out_specs=any_spec(1) + specs,
         scratch_shapes=scratch,
         compiler_params=params,
-    )(length, u, gain, rstd1, rstd2, row, *big)
+    )(length, pooled, groups, gain, rstd, row, *big)
 
 
 def adam_kernel(cb, *refs):
@@ -1174,15 +1182,13 @@
         own_a, *others = packed(qkv_weight, out_weight, up_weight, down_weight, col_bias, row_params, r, cb)
         own_b, own_1, own_2 = [gather_plain(v) for v in others]
         weights = (jnp.stack([gather_plain(own_a[j]) for j in range(NJ)]), own_b, own_1, own_2)
-    (rstd1, rstd2, gain, row, hb, u, outputs, h1, xhat1, g, xhat2, ct, xt, gp, qt, kt, vt, wa, w1, w2) = forward(
-        lengths, groups, inputs, weights, n, cb, comm
+    (rstd, gain, row, hb, pooled, outputs, h1, xhat1, g, xhat2, ct, xt, gp, qt, kt, vt, wa, w1, w2) = forward(
+        lengths, inputs, weights, n, cb, comm
     )
     if not comm:
-        every = lax.all_gather(u, ("dp", "tensor"), axis=0, tiled=True)
-        u = loss_pull(every, groups, lax.axis_index(("dp", "tensor"))) / lengths[lax.axis_index("tensor")].astype(f32)
-
+        pooled = lax.all_gather(pooled, ("dp", "tensor"), axis=0, tiled=True)
     big = (xhat2, xhat1, w1, w2, wa, g, gp, h1, ct, xt, qt, kt, vt)
-    input_grad, *sums = backward(lengths, u, gain, rstd1, rstd2, row, big, n, cb, comm)
+    input_grad, *sums = backward(lengths, pooled, groups, gain, rstd, row, big, n, cb, comm)
     sums = sums[: NJ + 3] if comm else [scatter_plain(v) for v in sums]
     olds = (
         (qkv_weight, qkv_first, qkv_second, qkv_ema),

time: 214 us -> 208 us (0.972)
  Pallas kernels: 213 us -> 207 us
    pallas_call x1, Pallas kernels: 97.9 us -> 95 us  [forward(): pl.pallas_call(functools.partial(forward_kernel, n, cb, comm), out_shape=...]
    pallas_call x1, Pallas kernels: 108 us -> 105 us  [backward(): pl.pallas_call(functools.partial(backward_kernel, n, cb, comm), out_shape...]
where the time goes in v6:
time: 208 us
  Pallas kernels  207 us (100%)
    pallas_call x1, Pallas kernels, backward(): pl.pallas_call(functools.partial(backward_kernel, n, cb, comm), out_shape...  105 us
    pallas_call x1, Pallas kernels, forward(): pl.pallas_call(functools.partial(forward_kernel, n, cb, comm), out_shape=...  95 us
    pallas_call x1, Pallas kernels, adam(): pl.pallas_call(functools.partial(adam_kernel, cb), out_shape=[s(v.shape,...  6.8 us

profile of v6, /device:TPU:0, one launch (start us, length us, event | category | flops | bytes accessed | tf_op | source)
XLA Modules:
  0.0 208.1 jit_solution(18058346779739895938)
XLA Ops:
  0.7 95.0 %shard_map.458 = (f32[1024,2]{1,0:T(8,128)}, f32[1,768]{1,0:T(1,128)}, f32[16,768]{1,0:T(8,128)}, f32[4,1,768]{2,1,0:T(1,128)}, f32[32,768]{1,0:T(8,128)}, /*ind...) custom-call(s32[4]{0:T(128)} %refs_0_.3, ...), custom_call_target="tpu_custom_call" | custom-call | tf_op jit(solution)/shard_map/pallas_call | solution.py:754
  95.7 105.4 %shard_map.459 = (f32[1024,768]{1,0:T(8,128)}, f32[96,768]{1,0:T(8,128)}, f32[96,768]{1,0:T(8,128)}, f32[96,256]{1,0:T(8,128)}, f32[96,256]{1,0:T(8,128)}, /*ind...) custom-call(s32[4]{0:T(128)} %refs_0_.3, ...), custom_call_target="tpu_custom_call" | custom-call | tf_op jit(solution)/shard_map/pallas_call | solution.py:1061
  201.1 6.8 %shard_map.460 = (bf16[1024,768]{1,0:T(8,128)(2,1)}, f32[1024,768]{1,0:T(8,128)}, f32[3,96,192]{2,1,0:T(8,128)}, f32[3,96,192]{2,1,0:T(8,128)}, f32[3,96,192]{2,...) custom-call(bf16[1024,768]{1,0:T(8,128)(2,1)} %get-tuple-element.77., ...), custom_call_target="tpu_custom_call" | custom-call | tf_op jit(solution)/shard_map/pallas_call | solution.py:1137

commit v7 on v6

--- a/solution.py
+++ b/solution.py
@@ -456,10 +456,10 @@
 CHUNKS = LEN // ROWS
 PARTS = 6
 
-PRE = ((0, 0), (3, 0), (2, 0), (1, 0), (0, 1), (3, 1), (2, 1), (3, 2), (1, 1), (4, 0), (3, 3), (3, 4), (1, 2), (1, 3), (0, 2), (0, 3), (3, 5), (2, 2), (3, 6), (4, 1), (2, 3), (1, 4), (1, 5), (1, 6), (3, 7), (0, 4), (0, 5), (3, 8), (3, 9), (0, 6), (5, 0), (1, 7), (1, 8), (1, 9), (2, 4), (0, 7), (0, 8), (0, 9), (2, 5), (4, 2), (2, 6), (3, 10), (1, 10), (4, 3), (3, 11), (1, 11), (0, 10), (0, 11), (3, 12), (1, 12), (5, 1), (0, 12))
-HEAD = {2: ((2, 7), (2, 8), (2, 9), (4, 4), (4, 5)), 3: ((4, 6),), 4: ((5, 2), (5, 3), (2, 10), (2, 11)), 6: ((2, 12), (4, 7)), 7: ((4, 8), (4, 9)), 10: ((5, 4), (4, 10), (5, 5), (5, 6)), 11: ((4, 11),)}
-MID = ((4, 12), (5, 7))
-LATE = {0: ((5, 8),), 2: ((5, 9),), 11: ((5, 10), (5, 11)), 15: ((5, 12),)}
+PRE = ((0, 0), (2, 0), (3, 0), (1, 0), (0, 1), (4, 0), (1, 1), (3, 1), (3, 2), (2, 1), (0, 2), (0, 3), (3, 3), (3, 4), (1, 2), (1, 3), (2, 2), (2, 3), (0, 4), (0, 5), (3, 5), (0, 6), (3, 6), (1, 4), (1, 5), (1, 6), (4, 1), (0, 7), (3, 7), (3, 8), (0, 8), (2, 4), (1, 7), (2, 5), (3, 9), (2, 6), (3, 10), (1, 8), (0, 9), (1, 9), (5, 0), (3, 11), (0, 10), (0, 11), (1, 10), (2, 7), (4, 2), (2, 8), (2, 9), (0, 12), (4, 3), (1, 11), (3, 12))
+HEAD = {0: ((1, 12),), 1: ((2, 10), (5, 1)), 3: ((2, 11), (4, 4), (4, 5)), 4: ((2, 12), (4, 6)), 6: ((5, 2), (5, 3)), 7: ((4, 7), (4, 8)), 8: ((4, 9),), 10: ((5, 4), (5, 5)), 11: ((5, 6), (4, 10))}
+MID = ((4, 11), (5, 7), (5, 8), (4, 12))
+LATE = {2: ((5, 9),), 11: ((5, 10), (5, 11)), 15: ((5, 12),)}
 BACK = {0: ((0, 0),), 1: ((0, 1), (1, 0)), 2: ((0, 2), (0, 3), (1, 1)), 3: ((0, 4), (1, 2), (1, 3)), 5: ((0, 5), (1, 4)), 6: ((0, 6), (1, 5), (0, 7)), 7: ((0, 8),), 8: ((0, 9), (0, 10), (1, 6)), 9: ((1, 7),), 10: ((2, 0),), 11: ((2, 1), (2, 2), (1, 8), (1, 9), (0, 11), (1, 10), (2, 3), (2, 4), (0, 12)), 13: ((2, 5),), 14: ((2, 6), (1, 11), (1, 12), (2, 7), (3, 0), (2, 8), (3, 1), (2, 9), (2, 10)), 15: ((1, 13), (3, 2)), 16: ((3, 3), (3, 4), (3, 5)), 17: ((3, 6),), 18: ((4, 0), (3, 7), (2, 11), (3, 8), (4, 1)), 19: ((4, 2), (3, 9), (2, 12), (0, 13), (4, 3), (5, 0), (5, 1), (4, 4), (3, 10), (4, 5), (2, 13)), 20: ((4, 6), (5, 2), (5, 3), (5, 4), (5, 5), (4, 7), (4, 8), (4, 9), (3, 11), (5, 6), (4, 10), (3, 12), (5, 7), (5, 8), (5, 9)), 21: ((5, 10), (2, 14), (3, 13), (4, 11), (0, 14), (4, 12), (4, 13), (1, 14), (5, 11)), 22: ((5, 12), (3, 14), (5, 13), (4, 14), (5, 14))}
 
 

time: 208 us -> 207 us (level)
  no operation moved by 1% of the time
where the time goes in v7:
time: 207 us
  Pallas kernels  206 us (100%)
    pallas_call x1, Pallas kernels, backward(): pl.pallas_call(functools.partial(backward_kernel, n, cb, comm), out_shape...  105 us
    pallas_call x1, Pallas kernels, forward(): pl.pallas_call(functools.partial(forward_kernel, n, cb, comm), out_shape=...  94 us
    pallas_call x1, Pallas kernels, adam(): pl.pallas_call(functools.partial(adam_kernel, cb), out_shape=[s(v.shape,...  6.8 us

profile of v7, /device:TPU:0, one launch (start us, length us, event | category | flops | bytes accessed | tf_op | source)
XLA Modules:
  0.0 207.0 jit_solution(9379158682412558310)
XLA Ops:
  0.7 94.0 %shard_map.458 = (f32[1024,2]{1,0:T(8,128)}, f32[1,768]{1,0:T(1,128)}, f32[16,768]{1,0:T(8,128)}, f32[4,1,768]{2,1,0:T(1,128)}, f32[32,768]{1,0:T(8,128)}, /*ind...) custom-call(s32[4]{0:T(128)} %refs_0_.3, ...), custom_call_target="tpu_custom_call" | custom-call | tf_op jit(solution)/shard_map/pallas_call | solution.py:754
  94.6 105.4 %shard_map.459 = (f32[1024,768]{1,0:T(8,128)}, f32[96,768]{1,0:T(8,128)}, f32[96,768]{1,0:T(8,128)}, f32[96,256]{1,0:T(8,128)}, f32[96,256]{1,0:T(8,128)}, /*ind...) custom-call(s32[4]{0:T(128)} %refs_0_.3, ...), custom_call_target="tpu_custom_call" | custom-call | tf_op jit(solution)/shard_map/pallas_call | solution.py:1061
  200.0 6.8 %shard_map.460 = (bf16[1024,768]{1,0:T(8,128)(2,1)}, f32[1024,768]{1,0:T(8,128)}, f32[3,96,192]{2,1,0:T(8,128)}, f32[3,96,192]{2,1,0:T(8,128)}, f32[3,96,192]{2,...) custom-call(bf16[1024,768]{1,0:T(8,128)(2,1)} %get-tuple-element.77., ...), custom_call_target="tpu_custom_call" | custom-call | tf_op jit(solution)/shard_map/pallas_call | solution.py:1137
